TPU v7x, 32 devices: a whole 2x2x4 slice. The times are simulated.
32 devices in a mesh: energy: 8 (over y, x, core), space: 4 (over z).
Axes of the slice: x: 2, y: 2, z: 4, core: 2. Of those that a mesh axis runs over, the one named last changes fastest.
Arguments:
- onsite: float32 [4, 2, 128, 128], P('space'), may hold values from -0.25 to 0.25
- hopping: float32 [4, 2, 128, 128], P('space'), may hold values from -0.25 to 0.25
- sigma_old: float32 [8, 4, 2, 128, 128], P('energy', 'space'), may hold values from -0.0390625 to 0.0390625
- screened: float32 [8, 4, 2, 3, 2, 128, 128], P('energy', 'space'), may hold values from -2 to 2
Outputs:
- green_retarded: float32 [8, 4, 3, 2, 128, 128], P('energy', 'space')
- self_energy: float32 [8, 4, 2, 3, 2, 128, 128], P('energy', 'space')
All inputs are finite; a program needn't handle non-finite values.
Results may differ from a plain program's by a relative error of at most 0.0003.
Values sent between devices are 32-bit elements; how exact they have to be, the bound alone decides.
No kernel may reach another device: no remote copies, remote signals or barrier semaphores. Data moves between devices by JAX's collectives and lax.ppermute only.
A program may use at most 128 MiB of HBM per device.

v0:
```python
import functools
import math

import jax
import jax.numpy as jnp
from jax import lax
from jax.experimental import pallas as pl
from jax.experimental.pallas import tpu as pltpu
from jax.sharding import PartitionSpec as P

BROADEN = 0.45
THERMAL = 0.1
F32 = jnp.float32
BF16 = jnp.bfloat16

LOWEST = 1.0 / 128.0
SQUARINGS = 6
DONE = 1e-4
STEPS_MAX = 60
WORK = 1
WORK2 = 2
WORK3 = 0.1
WORK4 = 0.1
WORK5 = 0.01
WORK6 = 0.1


def schedule():
    rho = (1.0 - LOWEST) / (1.0 + LOWEST)
    scales = []
    for _ in range(SQUARINGS):
        scales.append(2.0 / (2.0 - rho * rho))
        rho = rho * rho / (2.0 - rho * rho)
    return 2.0 / (1.0 + LOWEST), scales


def real_of(x):
    return x[:, : x.shape[1] // 2]


def imag_of(x):
    return x[:, x.shape[1] // 2 :]


def wide(x):
    return jnp.concatenate([x, jnp.concatenate([-imag_of(x), real_of(x)], axis=1)], axis=0)


def dagger(x):
    return jnp.concatenate([real_of(x).T, -imag_of(x).T], axis=1)


def dot(a, b):
    return jnp.dot(a, b, preferred_element_type=F32)


def split(x):
    high = x.astype(BF16)
    return high, (x - high.astype(F32)).astype(BF16)


def product(a, b):
    rows = a.shape[0]
    a_high, a_low = split(a)
    b_high, b_low = split(b)
    both = dot(jnp.concatenate([a_high, a_low], axis=0), wide(b_high))
    return both[:rows] + both[rows:] + dot(a_high, wide(b_low))


def times_complex(x, re, im):
    return jnp.concatenate(
        [re * real_of(x) - im * imag_of(x), re * imag_of(x) + im * real_of(x)], axis=1
    )


def identity_like(x):
    size = x.shape[0]
    row = lax.broadcasted_iota(jnp.int32, x.shape, 0)
    column = lax.broadcasted_iota(jnp.int32, x.shape, 1)
    return jnp.where(row == column, 1.0, 0.0).astype(F32)


def largest(x, axis):
    return jnp.max(x, axis=axis, keepdims=True)


def invert(s, out_ref):
    size = s.shape[0]
    one = identity_like(s)
    first, scales = schedule()
    s_dagger = dagger(s)
    s_dagger_b = s_dagger.astype(BF16)
    normal = dot(s.astype(BF16), wide(s_dagger_b))
    normal_b = normal.astype(BF16)
    both = dot(jnp.concatenate([s_dagger_b, normal_b], axis=0), wide(normal_b))
    square = both[size:]
    sums = jnp.sum(jnp.sqrt(real_of(square) ** 2 + imag_of(square) ** 2), axis=0, keepdims=True)
    a = first * lax.rsqrt(largest(sums, 1))
    c = scales[0]
    x = (2.0 * c * a) * s_dagger - (c * a * a) * both[:size]
    r = one - (2.0 * c * a) * normal + (c * a * a) * square
    for c in scales[1:]:
        r_b = r.astype(BF16)
        both = dot(jnp.concatenate([x.astype(BF16), r_b], axis=0), wide(r_b))
        x = c * (x + both[:size])
        r = (1.0 - c) * one + c * both[size:]
    s_high, s_low = split(s)
    s_both = jnp.concatenate([s_high, s_low], axis=0)
    x_b = x.astype(BF16)
    both = dot(s_both, wide(x_b))
    e_b = (one - both[:size] - both[size:]).astype(BF16)
    x = x_b.astype(F32) + dot(x_b, wide(e_b))

    def step(x):
        x_high, x_low = split(x)
        both = dot(s_both, wide(x_high))
        e = one - both[:size] - both[size:] - dot(s_high, wide(x_low))
        return x + dot(x_high, wide(e.astype(BF16))), jnp.sum(e * e)

    x, left = step(x)
    out_ref[...] = x

    @pl.when(jnp.logical_not(left < DONE))
    def _():
        bound = jnp.sqrt(largest(jnp.sum(jnp.abs(s), axis=1, keepdims=True), 0))
        other = jnp.sqrt(largest(jnp.sum(jnp.abs(real_of(s)) + jnp.abs(imag_of(s)), axis=0, keepdims=True), 1))
        safe = s_dagger / (bound * bound) / (other * other)
        good = left < 0.5
        start = jnp.where(good, x, safe)

        def unfinished(state):
            count, value, _ = state
            return jnp.logical_and(count < STEPS_MAX, jnp.logical_not(value < DONE))

        def body(state):
            count, _, x = state
            new = product(x, one - product(s, x))
            e = one - product(s, x)
            return count + 1, jnp.sum(e * e), x + new

        _, _, result = lax.while_loop(unfinished, body, (0, left, start))
        out_ref[...] = result


def energy_at(index, energies_all):
    return -1.5 + 3.0 * (index + 0.5) / energies_all


def energy_point(axes):
    chips, cores, _ = axes
    index = lax.axis_index("chip") * cores + lax.axis_index("core")
    return energy_at(index.astype(F32), chips * cores)


def place(axes):
    position, cells_all = lax.axis_index("space"), axes[2]
    return position, jnp.minimum(position, cells_all - 1 - position), position < cells_all // 2


def outer_kernel(
    axes, onsite_far, hopping_far, sigma_far, system_ref, green_ref, message_ref, h_ref, hd_ref, token_ref, onsite, hopping, sigma, arrivals
):
    copies = [
        pltpu.make_async_copy(far, near, arrivals.at[i])
        for i, (far, near) in enumerate(((onsite_far, onsite), (hopping_far, hopping), (sigma_far, sigma)))
    ]
    for copy in copies:
        copy.start()
    for copy in copies:
        copy.wait()
    position, depth, left = place(axes)
    energy = energy_point(axes)
    on = jnp.concatenate([onsite[0, 0], onsite[0, 1]], axis=1)
    sg = jnp.concatenate([sigma[0, 0, 0], sigma[0, 0, 1]], axis=1)
    h = jnp.concatenate([hopping[0, 0], hopping[0, 1]], axis=1)
    hd = dagger(h)
    h_ref[...] = h
    token_ref[...] = jnp.zeros_like(token_ref)
    hd_ref[...] = hd
    shape = on.shape
    row = lax.broadcasted_iota(jnp.int32, shape, 0)
    column = lax.broadcasted_iota(jnp.int32, shape, 1)
    point = jnp.where(row == column, energy, 0.0) + jnp.where(row + shape[0] == column, BROADEN, 0.0)
    system_ref[...] = point - 0.5 * (on + dagger(on)) - sg

    @pl.when(position == 0)
    def _():
        magnitude = energy * energy + BROADEN * BROADEN
        system_ref[...] = system_ref[...] - times_complex(product(hd, h), energy / magnitude, -BROADEN / magnitude)

    @pl.when(depth == 0)
    def _():
        invert(system_ref[...], green_ref)
        send(left, green_ref, h, hd, message_ref)

    @pl.when(depth != 0)
    def _():
        green_ref[...] = jnp.zeros(shape, F32)
        message_ref[...] = jnp.zeros(shape, F32)


def send(plain, green_ref, h, hd, message_ref):
    @pl.when(plain)
    def _():
        message_ref[...] = green_ref[...]

    @pl.when(jnp.logical_not(plain))
    def _():
        message_ref[...] = product(h, product(green_ref[...], hd))


def inward_kernel(axes, level, _, received, system, green, message, u, outside, h, hd, system_ref, green_ref, message_ref, u_ref, outside_ref, token_ref):
    token_ref[...] = jnp.zeros_like(token_ref)
    _, depth, left = place(axes)

    @pl.when(depth == level)
    def _():
        got = received[...]

        @pl.when(left)
        def _():
            gh = product(got, h[...])
            u_ref[...] = gh
            outside_ref[...] = got
            system_ref[...] = system[...] - product(hd[...], gh)

        @pl.when(jnp.logical_not(left))
        def _():
            system_ref[...] = system[...] - got
            u_ref[...] = u[...]
            outside_ref[...] = outside[...]

        invert(system_ref[...], green_ref)
        send(left, green_ref, h[...], hd[...], message_ref)

    @pl.when(depth != level)
    def _():
        system_ref[...] = system[...]
        green_ref[...] = green[...]
        message_ref[...] = message[...]
        u_ref[...] = u[...]
        outside_ref[...] = outside[...]


def middle_kernel(axes, received, system, green, h, hd, diagonal_ref, message_ref, u_ref):
    _, depth, left = place(axes)

    @pl.when(depth == axes[2] // 2 - 1)
    def _():
        got = received[...]

        @pl.when(left)
        def _():
            u_ref[...] = system[...] - got

        @pl.when(jnp.logical_not(left))
        def _():
            message_ref[...] = product(got, h[...])
            u_ref[...] = system[...] - product(hd[...], message_ref[...])

        s = u_ref[...]
        u_ref[...] = message_ref[...]
        invert(s, diagonal_ref)
        send(jnp.logical_not(left), diagonal_ref, h[...], hd[...], message_ref)

    @pl.when(depth != axes[2] // 2 - 1)
    def _():
        diagonal_ref[...] = green[...]
        u_ref[...] = jnp.zeros_like(u_ref)
        message_ref[...] = jnp.zeros_like(message_ref)


def waiting_kernel(axes, received, diagonal, u_in, u_out, outside, h, hd, upper_ref, lower_ref, ready_ref):
    position, depth, left = place(axes)
    energy = energy_point(axes)
    magnitude = energy * energy + BROADEN * BROADEN
    contact_re, contact_im = energy / magnitude, -BROADEN / magnitude

    @pl.when(depth == axes[2] // 2 - 1)
    def _():
        u = jnp.where(left, u_out[...], u_in[...])
        v = product(hd[...], jnp.where(left, outside[...], received[...]))
        upper_ref[...] = product(u, diagonal[...])
        lower_ref[...] = product(diagonal[...], v)
        ready_ref[...] = jnp.zeros_like(ready_ref)

    @pl.when(depth != axes[2] // 2 - 1)
    def _():
        g = diagonal[...]

        @pl.when(left)
        def _():
            at_contact = position == 0
            u = jnp.where(at_contact, times_complex(h[...], contact_re, contact_im), u_out[...])
            v = jnp.where(at_contact, times_complex(hd[...], contact_re, contact_im), product(hd[...], outside[...]))
            ready_ref[0] = g
            ready_ref[1] = g
            ready_ref[2] = product(u, g)
            ready_ref[3] = product(g, v)

        @pl.when(jnp.logical_not(left))
        def _():
            ready_ref[0] = product(g, hd[...])
            ready_ref[1] = product(h[...], g)
            ready_ref[2] = jnp.zeros_like(g)
            ready_ref[3] = jnp.zeros_like(g)

        upper_ref[...] = jnp.zeros_like(upper_ref)
        lower_ref[...] = jnp.zeros_like(lower_ref)


def outward_kernel(axes, level, final, waited, *refs):
    outward(axes, level, final, *refs[waited:])


def outward(axes, level, final, received, ready, diagonal, upper, lower, h, hd, *outputs):
    _, depth, left = place(axes)
    if final:
        green_out, packed_ref, green_ref, upper_ref, lower_ref = outputs
    else:
        message_ref, _, green_ref, upper_ref, lower_ref = outputs
        message_ref[...] = jnp.zeros_like(message_ref)

    @pl.when(depth != level)
    def _():
        green_ref[...] = diagonal[...]
        upper_ref[...] = upper[...]
        lower_ref[...] = lower[...]

    @pl.when(depth == level)
    def _():
        g_in = received[...]
        p = ready[0]
        w = product(g_in, ready[1])
        green_ref[...] = diagonal[...] + product(p, w)

        @pl.when(left)
        def _():
            upper_ref[...] = ready[2] + product(ready[2], w)
            lower_ref[...] = ready[3] + product(p, product(g_in, ready[3]))

        @pl.when(jnp.logical_not(left))
        def _():
            upper_ref[...] = w
            lower_ref[...] = product(p, g_in)

        if not final:
            send(jnp.logical_not(left), green_ref, h[...], hd[...], message_ref)

    if final:
        size = diagonal.shape[0]
        blocks = (green_ref[...], upper_ref[...], lower_ref[...])
        for b, block in enumerate(blocks):
            green_out[b, 0] = real_of(block)
            green_out[b, 1] = imag_of(block)
        d0 = blocks[0] - dagger(blocks[0])
        d1 = blocks[1] - dagger(blocks[2])
        row = lax.broadcasted_iota(jnp.int32, (size, size), 0)
        column = lax.broadcasted_iota(jnp.int32, (size, size), 1)
        packed_ref[0] = jnp.where(row > column, real_of(d0), imag_of(d0))
        packed_ref[1] = real_of(d1)
        packed_ref[2] = imag_of(d1)


def unpack(pack, out):
    size = pack.shape[-1]
    row = lax.broadcasted_iota(jnp.int32, (size, size), 0)
    column = lax.broadcasted_iota(jnp.int32, (size, size), 1)
    mixed = pack[0]
    turned = mixed.T
    out[0, 0] = jnp.where(row > column, mixed, jnp.where(row < column, -turned, 0.0))
    out[0, 1] = jnp.where(row > column, turned, mixed)
    out[1] = pack[1:]
    out[2, 0] = -pack[1].T
    out[2, 1] = pack[2].T


def add_term(out, spectral, blocks, scale):
    for b in range(3):
        w_re, w_im = blocks[b, 0], blocks[b, 1]
        g_re, g_im = scale * spectral[b, 0], scale * spectral[b, 1]
        out[b, 0] -= g_re * w_im + g_im * w_re
        out[b, 1] += g_re * w_re - g_im * w_im


def add_terms(axes, same, only, pieces, outs, spectral):
    chips, cores, _ = axes
    chip, core = lax.axis_index("chip"), lax.axis_index("core")
    for offset in range(chips):
        kappa = jnp.bitwise_xor(chip, offset) if len(pieces) > 1 else jnp.int32(offset)
        for c in range(cores):
            p = c if same else 1 - c
            for k in range(cores):
                r = kappa + (p + k) // 2
                to = 0 if (p + k) % 2 == c else 1
                if to not in only:
                    continue

                @pl.when(jnp.logical_and(core == c, r <= chip))
                def _():
                    index = (chip - r) * cores + p
                    energy = energy_at(index.astype(F32), chips * cores)
                    occupation = 1.0 / (1.0 + jnp.exp(jnp.full((1, 1), energy / THERMAL, F32)))
                    scale = -occupation if c == 0 else 1.0 - occupation
                    add_term(outs[to], spectral.at[r], screened_at(pieces, offset, kappa, k), scale)


def unpack_all(chips, packs, spectral):
    chip = lax.axis_index("chip")
    for r in range(chips):
        @pl.when(chip >= r)
        def _():
            unpack(packs[r], spectral.at[r])


def same_core_kernel(axes, *refs):
    chips = axes[0]
    packs, pieces, outs, spectral = refs[:chips], refs[chips:-3], refs[-3:-1], refs[-1]
    for out in outs:
        out[...] = jnp.zeros_like(out)
    unpack_all(chips, packs, spectral)
    add_terms(axes, True, (0, 1), pieces, outs, spectral)


def theirs_kernel(axes, *refs):
    chips = axes[0]
    packs, before, pieces, out, spectral = refs[:chips], refs[chips], refs[chips + 1 : -2], refs[-2], refs[-1]
    out[...] = before[...]
    unpack_all(chips, packs, spectral)
    add_terms(axes, False, (1,), pieces, (None, out), spectral)


def mine_kernel(axes, spectral, before, *refs):
    pieces, out, held, arrival = refs[:-3], refs[-3], refs[-2], refs[-1]
    held[...] = before[...]
    add_terms(axes, False, (0,), pieces, (held, None), spectral)
    copy = pltpu.make_async_copy(held, out.at[lax.axis_index("core")], arrival)
    copy.start()
    copy.wait()


def screened_at(pieces, offset, kappa, k):
    if len(pieces) == 1:
        return pieces[0].at[kappa, k]
    return pieces[2 * offset + k]


def join_kernel(axes, received, _, out, arrival):
    copy = pltpu.make_async_copy(received, out.at[1 - lax.axis_index("core")], arrival)
    copy.start()
    copy.wait()


class Exchange:
    def __init__(self, chips, screened, swap):
        self.paired = chips == 4
        self.own = screened[0, 0]
        self.got = lax.ppermute(self.own, "core", swap)
        self.later = []

    def moved(self, piece, offset):
        return lax.ppermute(piece, "chip", [(i, i ^ offset) for i in range(4)])

    def begin(self, after):
        core = lax.axis_index("core")
        own, got, _ = lax.optimization_barrier((self.own, self.got, after))
        one, two = jnp.where(core == 0, own[0], got[1]), jnp.where(core == 0, got[0], own[1])
        if self.paired:
            self.along = [self.moved(one, 1), self.moved(two, 2)]
            self.later = [self.moved(two, 1), self.moved(one, 2)]
            self.pieces = [one, two, self.along[0], self.later[0], self.later[1], self.along[1]]
        else:
            self.pieces = [lax.all_gather(jnp.stack([one, two]), "chip", axis=0)]

    def go_on(self, after):
        if self.paired:
            first, second, _ = lax.optimization_barrier((*self.along, after))
            self.pieces += [self.moved(first, 2), self.moved(second, 1)]


def local(axes, onsite, hopping, sigma_old, screened):
    chips, cores, cells_all = axes
    size = sigma_old.shape[-1]
    half = cells_all // 2
    matrix = jax.ShapeDtypeStruct((size, 2 * size), F32)
    def call(body, out_shape, *operands, space=pltpu.VMEM, grant=16, work=WORK, out_space=None, **options):
        spec = pl.BlockSpec(memory_space=pltpu.VMEM)
        spaces = space if isinstance(space, list) else [space] * len(operands)
        return pl.pallas_call(
            functools.partial(body, axes),
            out_shape=out_shape,
            in_specs=[pl.BlockSpec(memory_space=space) for space in spaces],
            out_specs=jax.tree.map(lambda _: spec, out_shape)
            if out_space is None
            else jax.tree.map(lambda space: pl.BlockSpec(memory_space=space), out_space),
            compiler_params=pltpu.CompilerParams(vmem_limit_bytes=grant * 1024 * 1024),
            cost_estimate=pl.CostEstimate(
                flops=int(work * 80 * (2 * size) ** 3), bytes_accessed=2 * 1024 * 1024, transcendentals=0
            ),
            **options,
        )(*operands)

    swap = [(i, i ^ 1) for i in range(cores)]
    exchange = Exchange(chips, screened, swap)
    token = jax.ShapeDtypeStruct((8, size), F32)
    system, green, message, h, hd, mark = call(
        outer_kernel,
        (matrix,) * 5 + (token,),
        *(pltpu.with_memory_space_constraint(a, pltpu.HBM) for a in (onsite, hopping, sigma_old)),
        space=pltpu.HBM,
        scratch_shapes=[pltpu.VMEM(a.shape, F32) for a in (onsite, hopping, sigma_old)]
        + [pltpu.SemaphoreType.DMA((3,))],
    )
    mark = lax.ppermute(mark, "core", swap)
    exchange.begin(mark)
    u_out = outside = jnp.zeros((size, 2 * size), F32)
    for level in range(1, half):
        route = [(level - 1, level), (cells_all - level, cells_all - 1 - level)]
        received = lax.ppermute(message, "space", route)
        system, green, message, u_out, outside, next_mark = call(
            functools.partial(swapped, inward_kernel, level),
            (matrix,) * 5 + (token,),
            mark, received, system, green, message, u_out, outside, h, hd,
            work=WORK2,
        )
        if level == half - 1:
            exchange.go_on(next_mark)
    received = lax.ppermute(message, "space", [(half - 1, half), (half, half - 1)])
    diagonal, message, u_in = call(
        middle_kernel, (matrix,) * 3, received, system, green, h, hd,
        work=WORK3,
    )
    upper = None
    for level in reversed(range(half - 1)):
        route = [(level + 1, level), (cells_all - 2 - level, cells_all - 1 - level)]
        arrived = lax.ppermute(message, "space", route)
        if upper is None:
            upper, lower, ready = call(
                waiting_kernel,
                (matrix, matrix, jax.ShapeDtypeStruct((4, size, 2 * size), F32)),
                received, diagonal, u_in, u_out, outside, h, hd,
                work=WORK4,
            )
        final = level == 0
        shapes = (matrix,) * 3
        if final:
            shapes = (
                jax.ShapeDtypeStruct((3, 2, size, size), F32),
                jax.ShapeDtypeStruct((3, size, size), F32),
            ) + shapes
        else:
            shapes = (matrix, token) + shapes
        results = call(
            functools.partial(swapped, outward_kernel, level, final, len(exchange.later)),
            shapes,
            *exchange.later, arrived, ready, diagonal, upper, lower, h, hd,
            space=[pl.ANY] * len(exchange.later) + [pltpu.VMEM] * 7,
            work=WORK6,
        )
        message, _, diagonal, upper, lower = results
    green_out, packed = results[:2]
    own = [packed] + [
        lax.ppermute(packed, "chip", [(i, i + r) for i in range(chips - r)]) for r in range(1, chips)
    ]
    other = [lax.ppermute(pack, "core", swap) for pack in own]
    kind = jax.ShapeDtypeStruct(screened.shape[3:], F32)
    unpacked = (chips, 3, 2, size, size)
    mine, theirs = call(
        same_core_kernel, (kind,) * 2, *own, *exchange.pieces,
        scratch_shapes=[pltpu.VMEM(unpacked, F32)],
        work=WORK5,
    )
    theirs, spectral = call(
        theirs_kernel, (kind, jax.ShapeDtypeStruct(unpacked, F32)), *other, theirs, *exchange.pieces
    )
    received = lax.ppermute(theirs, "core", swap)
    half_out = call(
        mine_kernel,
        jax.ShapeDtypeStruct(screened.shape[2:], F32),
        spectral, mine, *exchange.pieces,
        out_space=pl.ANY,
        scratch_shapes=[pltpu.VMEM(kind.shape, F32), pltpu.SemaphoreType.DMA],
    )
    sigma_out = call(
        join_kernel,
        jax.ShapeDtypeStruct(screened.shape[2:], F32),
        received, half_out,
        space=pl.ANY,
        out_space=pl.ANY,
        input_output_aliases={1: 0},
        scratch_shapes=[pltpu.SemaphoreType.DMA],
    )
    return green_out[None, None], sigma_out[None, None]


def swapped(body, *arguments):
    fixed = [a for a in arguments if isinstance(a, (int, bool))]
    axes, *refs = arguments[len(fixed) :]
    return body(axes, *fixed, *refs)


def solution(mesh):
    cores = 2
    axes = (mesh.shape["energy"] // cores, cores, mesh.shape["space"])
    split_mesh = jax.sharding.Mesh(mesh.devices.reshape(axes), ("chip", "core", "space"))
    energy = ("chip", "core")
    placed = (
        P("space", None, None, None),
        P("space", None, None, None),
        P(energy, "space", None, None, None),
        P(energy, "space", None, None, None, None, None),
    )
    return jax.shard_map(
        functools.partial(local, axes),
        mesh=split_mesh,
        in_specs=placed,
        out_specs=(
            P(energy, "space", None, None, None, None),
            P(energy, "space", None, None, None, None, None),
        ),
        check_vma=False,
    )
```

profile of v0, /device:TPU:0, one launch (start us, length us, event | category | flops | bytes accessed | tf_op | source)
XLA Modules:
  0.0 51.6 jit_solution(4492241205578844551)
XLA Ops:
  0.6 0.5 %collective-permute-start = (f32[2,3,2,128,128]{4,3,2,1,0:T(8,128)}, f32[2,3,2,128,128]{4,3,2,1,0:T(8,128)S(1)}, u32[]{:S(2)}, u32[]{:S(2)}) collective-permute-start(f32[2,3,2,128,128]{4,3,2,1,0:T(8,128)} %bitcast.7), channel_id=1, source_target_pairs={{0,4},{4,0},{1,5},{5,1},{2,6},{6,2},{3,7},{7,3},{8,12},{12,8},{9,1... | collective-permute-start | bytes 2359304 | tf_op jit(solution)/shard_map/ppermute | solution.py:458
  1.2 3.8 %shard_map.59 = (f32[128,256]{1,0:T(8,128)S(1)}, f32[128,256]{1,0:T(8,128)S(1)}, f32[128,256]{1,0:T(8,128)S(1)}, f32[128,256]{1,0:T(8,128)S(1)}, f32[128,256]{1,0:T(8,128)S(1)}, /*index=5*/f32[8,128]{1,0:T(8,128)S(1)}) custom-call(f32[1,2,128,128]{3,2,1,0:T(8,128)} %onsite_far.1, f32[1,2,128,128]{3,2,1,0:T(8,128)} %hopping_far.1, ...), custom_call_target="tpu_custom_call" | custom-call | flops 1342177280 | bytes 2097152 | tf_op jit(solution)/shard_map/pallas_call | solution.py:489
  5.1 2.3 %collective-permute-start.4 = (f32[128,256]{1,0:T(8,128)S(1)}, f32[128,256]{1,0:T(8,128)S(1)}, u32[]{:S(2)}, u32[]{:S(2)}) collective-permute-start(f32[128,256]{1,0:T(8,128)S(1)} %get-tuple-element.32.arguments_4_), channel_id=1, source_target_pairs={{0,1},{3,2},{4,5},{7,6},{8,9},{11,10},{12,13},{15,14},{16,17},{19,... | collective-permute-start | bytes 393224 | tf_op jit(solution)/shard_map/ppermute | solution.py:519
  7.6 1.9 %collective-permute-start.14 = (f32[3,2,128,128]{3,2,1,0:T(8,128)S(1)}, f32[3,2,128,128]{3,2,1,0:T(8,128)S(1)}, u32[]{:S(2)}, u32[]{:S(2)}) collective-permute-start(f32[3,2,128,128]{3,2,1,0:T(8,128)S(1)} %get-tuple-element.56.refs_4_.refs_5_.refs_0_), channel_id=1, source_target_pairs={{0,8},{8,0},{16,24},{24,16},{1,9},{9,1},{17,25},{25,17},{2,10},{10... | collective-permute-start | bytes 1179656 | tf_op jit(solution)/shard_map/ppermute | solution.py:462
  9.5 1.5 %collective-permute-start.15 = (f32[3,2,128,128]{3,2,1,0:T(8,128)S(1)}, f32[3,2,128,128]{3,2,1,0:T(8,128)S(1)}, u32[]{:S(2)}, u32[]{:S(2)}) collective-permute-start(f32[3,2,128,128]{3,2,1,0:T(8,128)S(1)} %get-tuple-element.57.refs_5_.refs_6_.refs_1_), channel_id=1, source_target_pairs={{0,16},{8,24},{16,0},{24,8},{1,17},{9,25},{17,1},{25,9},{2,18},{10... | collective-permute-start | bytes 1179656 | tf_op jit(solution)/shard_map/ppermute | solution.py:462
  11.7 0.7 %shard_map.60 = (f32[128,256]{1,0:T(8,128)S(1)}, f32[128,256]{1,0:T(8,128)S(1)}, f32[128,256]{1,0:T(8,128)S(1)}, f32[128,256]{1,0:T(8,128)S(1)}, f32[128,256]{1,0:T(8,128)S(1)}, /*index=5*/f32[8,128]{1,0:T(8,128)}) custom-call(f32[8,128]{1,0:T(8,128)S(1)} %collective-permute-done.1.arguments_0_, f32[128,256]{1,0:T(8,128)S(1)} %collective-permute-done.4.arguments_1_, ...), custom_call_target="tpu_custom_call" | custom-call | flops 2684354560 | bytes 2097152 | tf_op jit(solution)/shard_map/pallas_call | solution.py:489
  12.4 0.7 %collective-permute-start.5 = (f32[128,256]{1,0:T(8,128)S(1)}, f32[128,256]{1,0:T(8,128)S(1)}, u32[]{:S(2)}, u32[]{:S(2)}) collective-permute-start(f32[128,256]{1,0:T(8,128)S(1)} %get-tuple-element.37), channel_id=1, source_target_pairs={{1,2},{2,1},{5,6},{6,5},{9,10},{10,9},{13,14},{14,13},{17,18},{18,... | collective-permute-start | bytes 393224 | tf_op jit(solution)/shard_map/ppermute | solution.py:528
  13.0 6.6 %collective-permute-done.14.refs_6_.refs_7_.refs_2_ = f32[3,2,128,128]{3,2,1,0:T(8,128)S(1)} collective-permute-done((f32[3,2,128,128]{3,2,1,0:T(8,128)S(1)}, f32[3,2,128,128]{3,2,1,0:T(8,128)S(1)}, u32[]{:S(2)}, u32[]{:S(2)}) %collective-permute-start.14) | collective-permute-done | bytes 393248 | tf_op jit(solution)/shard_map/ppermute | solution.py:462
  19.6 1.9 %collective-permute-done.15.refs_9_.refs_10_.refs_5_ = f32[3,2,128,128]{3,2,1,0:T(8,128)S(1)} collective-permute-done((f32[3,2,128,128]{3,2,1,0:T(8,128)S(1)}, f32[3,2,128,128]{3,2,1,0:T(8,128)S(1)}, u32[]{:S(2)}, u32[]{:S(2)}) %collective-permute-start.15) | collective-permute-done | bytes 393248 | tf_op jit(solution)/shard_map/ppermute | solution.py:462
  21.5 1.5 %collective-permute-start.16 = (f32[3,2,128,128]{3,2,1,0:T(8,128)S(1)}, f32[3,2,128,128]{3,2,1,0:T(8,128)S(1)}, u32[]{:S(2)}, u32[]{:S(2)}) collective-permute-start(f32[3,2,128,128]{3,2,1,0:T(8,128)S(1)} %collective-permute-done.14.refs_6_.refs_7_.refs_2_), channel_id=1, source_target_pairs={{0,16},{8,24},{16,0},{24,8},{1,17},{9,25},{17,1},{25,9},{2,18},{10... | collective-permute-start | bytes 1179656 | tf_op jit(solution)/shard_map/ppermute | solution.py:462
  23.1 1.3 %collective-permute-start.6 = (f32[128,256]{1,0:T(8,128)S(1)}, f32[128,256]{1,0:T(8,128)S(1)}, u32[]{:S(2)}, u32[]{:S(2)}) collective-permute-start(f32[128,256]{1,0:T(8,128)S(1)} %get-tuple-element.40), channel_id=1, source_target_pairs={{1,0},{2,3},{5,4},{6,7},{9,8},{10,11},{13,12},{14,15},{17,16},{18,... | collective-permute-start | bytes 393224 | tf_op jit(solution)/shard_map/ppermute | solution.py:536
  24.4 0.6 %shard_map.62 = (f32[128,256]{1,0:T(8,128)S(1)}, f32[128,256]{1,0:T(8,128)S(1)}, f32[4,128,256]{2,1,0:T(8,128)S(1)}) custom-call(f32[128,256]{1,0:T(8,128)S(1)} %collective-permute-done.5.received, f32[128,256]{1,0:T(8,128)S(1)} %get-tuple-element.41.diagonal.arguments_4_, f32[128,256]{1,0:T(8,128)S(1)} %get-tuple-element.42.u_in, ...), custom_call_target="tpu_custom_call" | custom-call | flops 134217728 | bytes 2097152 | tf_op jit(solution)/shard_map/pallas_call | solution.py:489
  24.9 0.6 %collective-permute-start.17 = (f32[3,2,128,128]{3,2,1,0:T(8,128)S(1)}, f32[3,2,128,128]{3,2,1,0:T(8,128)S(1)}, u32[]{:S(2)}, u32[]{:S(2)}) collective-permute-start(f32[3,2,128,128]{3,2,1,0:T(8,128)S(1)} %collective-permute-done.15.refs_9_.refs_10_.refs_5_), channel_id=1, source_target_pairs={{0,8},{8,0},{16,24},{24,16},{1,9},{9,1},{17,25},{25,17},{2,10},{10... | collective-permute-start | bytes 1179656 | tf_op jit(solution)/shard_map/ppermute | solution.py:462
  25.5 6.7 %collective-permute-done.6.arguments_2_ = f32[128,256]{1,0:T(8,128)S(1)} collective-permute-done((f32[128,256]{1,0:T(8,128)S(1)}, f32[128,256]{1,0:T(8,128)S(1)}, u32[]{:S(2)}, u32[]{:S(2)}) %collective-permute-start.6) | collective-permute-done | bytes 131104 | tf_op jit(solution)/shard_map/ppermute | solution.py:536
  32.2 1.9 %shard_map.63 = (f32[3,2,128,128]{3,2,1,0:T(8,128)}, f32[3,128,128]{2,1,0:T(8,128)S(1)}, f32[128,256]{1,0:T(8,128)}, f32[128,256]{1,0:T(8,128)}, f32[128,256]{1,0:T(8,128)}) custom-call(f32[3,2,128,128]{3,2,1,0:T(8,128)S(1)} %collective-permute-done.2.arguments_0_.refs_7_.refs_8_.refs_3_, ...), custom_call_target="tpu_custom_call" | custom-call | flops 134217728 | bytes 2097152 | tf_op jit(solution)/shard_map/pallas_call | solution.py:489
  34.2 4.3 %collective-permute-start.12 = (f32[3,128,128]{2,1,0:T(8,128)S(1)}, f32[3,128,128]{2,1,0:T(8,128)S(1)}, u32[]{:S(2)}, u32[]{:S(2)}) collective-permute-start(f32[3,128,128]{2,1,0:T(8,128)S(1)} %get-tuple-element.49.refs_0_), channel_id=1, source_target_pairs={{0,24},{1,25},{2,26},{3,27},{4,28},{5,29},{6,30},{7,31}} | collective-permute-start | bytes 589832 | tf_op jit(solution)/shard_map/ppermute | solution.py:563
  38.5 1.3 %collective-permute-start.10 = (f32[3,128,128]{2,1,0:T(8,128)S(1)}, f32[3,128,128]{2,1,0:T(8,128)S(1)}, u32[]{:S(2)}, u32[]{:S(2)}) collective-permute-start(f32[3,128,128]{2,1,0:T(8,128)S(1)} %get-tuple-element.49.refs_0_), channel_id=1, source_target_pairs={{0,16},{8,24},{1,17},{9,25},{2,18},{10,26},{3,19},{11,27},{4,20},{... | collective-permute-start | bytes 589832 | tf_op jit(solution)/shard_map/ppermute | solution.py:563
  39.8 2.5 %collective-permute-start.8 = (f32[3,128,128]{2,1,0:T(8,128)S(1)}, f32[3,128,128]{2,1,0:T(8,128)S(1)}, u32[]{:S(2)}, u32[]{:S(2)}) collective-permute-start(f32[3,128,128]{2,1,0:T(8,128)S(1)} %get-tuple-element.49.refs_0_), channel_id=1, source_target_pairs={{0,8},{8,16},{16,24},{1,9},{9,17},{17,25},{2,10},{10,18},{18,26},{... | collective-permute-start | bytes 589832 | tf_op jit(solution)/shard_map/ppermute | solution.py:563
  42.3 0.6 %collective-permute-done.12.refs_3_ = f32[3,128,128]{2,1,0:T(8,128)S(1)} collective-permute-done((f32[3,128,128]{2,1,0:T(8,128)S(1)}, f32[3,128,128]{2,1,0:T(8,128)S(1)}, u32[]{:S(2)}, u32[]{:S(2)}) %collective-permute-start.12) | collective-permute-done | bytes 196640 | tf_op jit(solution)/shard_map/ppermute | solution.py:563
  42.9 3.8 %collective-permute-done.10.refs_2_ = f32[3,128,128]{2,1,0:T(8,128)S(1)} collective-permute-done((f32[3,128,128]{2,1,0:T(8,128)S(1)}, f32[3,128,128]{2,1,0:T(8,128)S(1)}, u32[]{:S(2)}, u32[]{:S(2)}) %collective-permute-start.10) | collective-permute-done | bytes 196640 | tf_op jit(solution)/shard_map/ppermute | solution.py:563
  46.7 0.5 collective-permute-start.11
  49.3 0.8 %shard_map.66._ = f32[2,3,2,128,128]{4,3,2,1,0:T(8,128)} custom-call(f32[4,3,2,128,128]{4,3,2,1,0:T(8,128)S(1)} %get-tuple-element.54.spectral, f32[3,2,128,128]{3,2,1,0:T(8,128)S(1)} %get-tuple-element.55.before, f32[3,2,128,128]{3,2,1,0:T(8,128)S(1)} %get-tuple-element.56.refs_4_.refs_5_.refs_0_, ...), custom_call_target="tpu_custom_call" | custom-call | flops 1342177280 | bytes 2097152 | tf_op jit(solution)/shard_map/pallas_call | solution.py:489
  50.1 0.7 %collective-permute-done.18.received = f32[3,2,128,128]{3,2,1,0:T(8,128)S(1)} collective-permute-done((f32[3,2,128,128]{3,2,1,0:T(8,128)S(1)}, f32[3,2,128,128]{3,2,1,0:T(8,128)S(1)}, u32[]{:S(2)}, u32[]{:S(2)}) %collective-permute-start.18) | collective-permute-done | bytes 393248 | tf_op jit(solution)/shard_map/ppermute | solution.py:576
  50.8 0.8 %shard_map.67 = f32[2,3,2,128,128]{4,3,2,1,0:T(8,128)} custom-call(f32[3,2,128,128]{3,2,1,0:T(8,128)S(1)} %collective-permute-done.18.received, f32[2,3,2,128,128]{4,3,2,1,0:T(8,128)} %shard_map.66._), custom_call_target="tpu_custom_call", output_to_operand_aliasing={{}: (1, {})} | custom-call | flops 1342177280 | bytes 2097152 | tf_op jit(solution)/shard_map/pallas_call | solution.py:489
  (27 shorter events, 3.1 us)
Async XLA Ops:
  0.6 6.8 %copy-start = (f32[1,1,2,3,2,128,128]{6,5,4,3,2,1,0:T(8,128)S(1)}, f32[1,1,2,3,2,128,128]{6,5,4,3,2,1,0:T(8,128)}, u32[]{:S(2)}) copy-start(f32[1,1,2,3,2,128,128]{6,5,4,3,2,1,0:T(8,128)} %param.7) | copy-start | bytes 2359300
  0.6 6.8 %collective-permute-start = (f32[2,3,2,128,128]{4,3,2,1,0:T(8,128)}, f32[2,3,2,128,128]{4,3,2,1,0:T(8,128)S(1)}, u32[]{:S(2)}, u32[]{:S(2)}) collective-permute-start(f32[2,3,2,128,128]{4,3,2,1,0:T(8,128)} %bitcast.7), channel_id=1, source_target_pairs={{0,4},{4,0},{1,5},{5,1},{2,6},{6,2},{3,7},{7,3},{8,12},{12,8},{9,1... | collective-permute-start | bytes 2359304 | tf_op jit(solution)/shard_map/ppermute | solution.py:458
  5.0 2.5 %collective-permute-start.1 = (f32[8,128]{1,0:T(8,128)S(1)}, f32[8,128]{1,0:T(8,128)S(1)}, u32[]{:S(2)}, u32[]{:S(2)}) collective-permute-start(f32[8,128]{1,0:T(8,128)S(1)} %get-tuple-element.29), channel_id=1, source_target_pairs={{0,4},{4,0},{1,5},{5,1},{2,6},{6,2},{3,7},{7,3},{8,12},{12,8},{9,1... | collective-permute-start | bytes 12296 | tf_op jit(solution)/shard_map/ppermute | solution.py:514
  5.1 6.5 %collective-permute-start.4 = (f32[128,256]{1,0:T(8,128)S(1)}, f32[128,256]{1,0:T(8,128)S(1)}, u32[]{:S(2)}, u32[]{:S(2)}) collective-permute-start(f32[128,256]{1,0:T(8,128)S(1)} %get-tuple-element.32.arguments_4_), channel_id=1, source_target_pairs={{0,1},{3,2},{4,5},{7,6},{8,9},{11,10},{12,13},{15,14},{16,17},{19,... | collective-permute-start | bytes 393224 | tf_op jit(solution)/shard_map/ppermute | solution.py:519
  7.6 12.0 %collective-permute-start.14 = (f32[3,2,128,128]{3,2,1,0:T(8,128)S(1)}, f32[3,2,128,128]{3,2,1,0:T(8,128)S(1)}, u32[]{:S(2)}, u32[]{:S(2)}) collective-permute-start(f32[3,2,128,128]{3,2,1,0:T(8,128)S(1)} %get-tuple-element.56.refs_4_.refs_5_.refs_0_), channel_id=1, source_target_pairs={{0,8},{8,0},{16,24},{24,16},{1,9},{9,1},{17,25},{25,17},{2,10},{10... | collective-permute-start | bytes 1179656 | tf_op jit(solution)/shard_map/ppermute | solution.py:462
  9.5 12.0 %collective-permute-start.15 = (f32[3,2,128,128]{3,2,1,0:T(8,128)S(1)}, f32[3,2,128,128]{3,2,1,0:T(8,128)S(1)}, u32[]{:S(2)}, u32[]{:S(2)}) collective-permute-start(f32[3,2,128,128]{3,2,1,0:T(8,128)S(1)} %get-tuple-element.57.refs_5_.refs_6_.refs_1_), channel_id=1, source_target_pairs={{0,16},{8,24},{16,0},{24,8},{1,17},{9,25},{17,1},{25,9},{2,18},{10... | collective-permute-start | bytes 1179656 | tf_op jit(solution)/shard_map/ppermute | solution.py:462
  11.0 21.2 %collective-permute-start.3 = (f32[3,2,128,128]{3,2,1,0:T(8,128)S(1)}, f32[3,2,128,128]{3,2,1,0:T(8,128)S(1)}, u32[]{:S(2)}, u32[]{:S(2)}) collective-permute-start(f32[3,2,128,128]{3,2,1,0:T(8,128)S(1)} %get-tuple-element.56.refs_4_.refs_5_.refs_0_), channel_id=1, source_target_pairs={{0,16},{8,24},{16,0},{24,8},{1,17},{9,25},{17,1},{25,9},{2,18},{10... | collective-permute-start | bytes 1179656 | tf_op jit(solution)/shard_map/ppermute | solution.py:462
  11.5 20.7 %collective-permute-start.2 = (f32[3,2,128,128]{3,2,1,0:T(8,128)S(1)}, f32[3,2,128,128]{3,2,1,0:T(8,128)S(1)}, u32[]{:S(2)}, u32[]{:S(2)}) collective-permute-start(f32[3,2,128,128]{3,2,1,0:T(8,128)S(1)} %get-tuple-element.57.refs_5_.refs_6_.refs_1_), channel_id=1, source_target_pairs={{0,8},{8,0},{16,24},{24,16},{1,9},{9,1},{17,25},{25,17},{2,10},{10... | collective-permute-start | bytes 1179656 | tf_op jit(solution)/shard_map/ppermute | solution.py:462
  12.4 10.7 %collective-permute-start.5 = (f32[128,256]{1,0:T(8,128)S(1)}, f32[128,256]{1,0:T(8,128)S(1)}, u32[]{:S(2)}, u32[]{:S(2)}) collective-permute-start(f32[128,256]{1,0:T(8,128)S(1)} %get-tuple-element.37), channel_id=1, source_target_pairs={{1,2},{2,1},{5,6},{6,5},{9,10},{10,9},{13,14},{14,13},{17,18},{18,... | collective-permute-start | bytes 393224 | tf_op jit(solution)/shard_map/ppermute | solution.py:528
  21.5 25.7 %collective-permute-start.16 = (f32[3,2,128,128]{3,2,1,0:T(8,128)S(1)}, f32[3,2,128,128]{3,2,1,0:T(8,128)S(1)}, u32[]{:S(2)}, u32[]{:S(2)}) collective-permute-start(f32[3,2,128,128]{3,2,1,0:T(8,128)S(1)} %collective-permute-done.14.refs_6_.refs_7_.refs_2_), channel_id=1, source_target_pairs={{0,16},{8,24},{16,0},{24,8},{1,17},{9,25},{17,1},{25,9},{2,18},{10... | collective-permute-start | bytes 1179656 | tf_op jit(solution)/shard_map/ppermute | solution.py:462
  23.1 9.2 %collective-permute-start.6 = (f32[128,256]{1,0:T(8,128)S(1)}, f32[128,256]{1,0:T(8,128)S(1)}, u32[]{:S(2)}, u32[]{:S(2)}) collective-permute-start(f32[128,256]{1,0:T(8,128)S(1)} %get-tuple-element.40), channel_id=1, source_target_pairs={{1,0},{2,3},{5,4},{6,7},{9,8},{10,11},{13,12},{14,15},{17,16},{18,... | collective-permute-start | bytes 393224 | tf_op jit(solution)/shard_map/ppermute | solution.py:536
  24.9 22.4 %collective-permute-start.17 = (f32[3,2,128,128]{3,2,1,0:T(8,128)S(1)}, f32[3,2,128,128]{3,2,1,0:T(8,128)S(1)}, u32[]{:S(2)}, u32[]{:S(2)}) collective-permute-start(f32[3,2,128,128]{3,2,1,0:T(8,128)S(1)} %collective-permute-done.15.refs_9_.refs_10_.refs_5_), channel_id=1, source_target_pairs={{0,8},{8,0},{16,24},{24,16},{1,9},{9,1},{17,25},{25,17},{2,10},{10... | collective-permute-start | bytes 1179656 | tf_op jit(solution)/shard_map/ppermute | solution.py:462
  34.2 8.7 %collective-permute-start.12 = (f32[3,128,128]{2,1,0:T(8,128)S(1)}, f32[3,128,128]{2,1,0:T(8,128)S(1)}, u32[]{:S(2)}, u32[]{:S(2)}) collective-permute-start(f32[3,128,128]{2,1,0:T(8,128)S(1)} %get-tuple-element.49.refs_0_), channel_id=1, source_target_pairs={{0,24},{1,25},{2,26},{3,27},{4,28},{5,29},{6,30},{7,31}} | collective-permute-start | bytes 589832 | tf_op jit(solution)/shard_map/ppermute | solution.py:563
  38.5 8.2 %collective-permute-start.10 = (f32[3,128,128]{2,1,0:T(8,128)S(1)}, f32[3,128,128]{2,1,0:T(8,128)S(1)}, u32[]{:S(2)}, u32[]{:S(2)}) collective-permute-start(f32[3,128,128]{2,1,0:T(8,128)S(1)} %get-tuple-element.49.refs_0_), channel_id=1, source_target_pairs={{0,16},{8,24},{1,17},{9,25},{2,18},{10,26},{3,19},{11,27},{4,20},{... | collective-permute-start | bytes 589832 | tf_op jit(solution)/shard_map/ppermute | solution.py:563
  39.8 6.9 %collective-permute-start.8 = (f32[3,128,128]{2,1,0:T(8,128)S(1)}, f32[3,128,128]{2,1,0:T(8,128)S(1)}, u32[]{:S(2)}, u32[]{:S(2)}) collective-permute-start(f32[3,128,128]{2,1,0:T(8,128)S(1)} %get-tuple-element.49.refs_0_), channel_id=1, source_target_pairs={{0,8},{8,16},{16,24},{1,9},{9,17},{17,25},{2,10},{10,18},{18,26},{... | collective-permute-start | bytes 589832 | tf_op jit(solution)/shard_map/ppermute | solution.py:563
  42.9 4.8 %collective-permute-start.7 = (f32[3,128,128]{2,1,0:T(8,128)S(1)}, f32[3,128,128]{2,1,0:T(8,128)S(1)}, u32[]{:S(2)}, u32[]{:S(2)}) collective-permute-start(f32[3,128,128]{2,1,0:T(8,128)S(1)} %get-tuple-element.49.refs_0_), channel_id=1, source_target_pairs={{0,4},{4,0},{1,5},{5,1},{2,6},{6,2},{3,7},{7,3},{8,12},{12,8},{9,1... | collective-permute-start | bytes 589832 | tf_op jit(solution)/shard_map/ppermute | solution.py:565
  46.7 1.4 %collective-permute-start.13 = (f32[3,128,128]{2,1,0:T(8,128)S(1)}, f32[3,128,128]{2,1,0:T(8,128)S(1)}, u32[]{:S(2)}, u32[]{:S(2)}) collective-permute-start(f32[3,128,128]{2,1,0:T(8,128)S(1)} %collective-permute-done.12.refs_3_), channel_id=1, source_target_pairs={{0,4},{4,0},{1,5},{5,1},{2,6},{6,2},{3,7},{7,3},{8,12},{12,8},{9,1... | collective-permute-start | bytes 589832 | tf_op jit(solution)/shard_map/ppermute | solution.py:565
  46.7 1.7 %collective-permute-start.11 = (f32[3,128,128]{2,1,0:T(8,128)S(1)}, f32[3,128,128]{2,1,0:T(8,128)S(1)}, u32[]{:S(2)}, u32[]{:S(2)}) collective-permute-start(f32[3,128,128]{2,1,0:T(8,128)S(1)} %collective-permute-done.10.refs_2_), channel_id=1, source_target_pairs={{0,4},{4,0},{1,5},{5,1},{2,6},{6,2},{3,7},{7,3},{8,12},{12,8},{9,1... | collective-permute-start | bytes 589832 | tf_op jit(solution)/shard_map/ppermute | solution.py:565
  47.2 1.5 %collective-permute-start.9 = (f32[3,128,128]{2,1,0:T(8,128)S(1)}, f32[3,128,128]{2,1,0:T(8,128)S(1)}, u32[]{:S(2)}, u32[]{:S(2)}) collective-permute-start(f32[3,128,128]{2,1,0:T(8,128)S(1)} %collective-permute-done.8.refs_1_), channel_id=1, source_target_pairs={{0,4},{4,0},{1,5},{5,1},{2,6},{6,2},{3,7},{7,3},{8,12},{12,8},{9,1... | collective-permute-start | bytes 589832 | tf_op jit(solution)/shard_map/ppermute | solution.py:565
  49.0 1.8 %collective-permute-start.18 = (f32[3,2,128,128]{3,2,1,0:T(8,128)S(1)}, f32[3,2,128,128]{3,2,1,0:T(8,128)S(1)}, u32[]{:S(2)}, u32[]{:S(2)}) collective-permute-start(f32[3,2,128,128]{3,2,1,0:T(8,128)S(1)} %get-tuple-element.53), channel_id=1, source_target_pairs={{0,4},{4,0},{1,5},{5,1},{2,6},{6,2},{3,7},{7,3},{8,12},{12,8},{9,1... | collective-permute-start | bytes 1179656 | tf_op jit(solution)/shard_map/ppermute | solution.py:576
where the time goes:
time: 52.2 us; the launch traced here: 51.6 us
  waiting for transfers between devices  21.3 us (41%)
  starting transfers between devices  20.2 us (39%)
  Pallas kernels  9.23 us (18%)
  between operations  0.8 us (2%)
    pallas_call x9, Pallas kernels, call(): pl.pallas_call(functools.partial(body, axes), out_shape=out_shape, in_spe...  9.23 us
    ppermute x6, waiting for transfers between devices, moved(): return lax.ppermute(piece, 'chip', [(i, i ^ offset) for i in range(4)])  8.5 us
    ppermute x3, starting transfers between devices, local(): lax.ppermute(packed, 'chip', [(i, i + r) for i in range(chips - r)])  8.12 us
    ppermute x1, waiting for transfers between devices, local(): arrived = lax.ppermute(message, 'space', route)  6.68 us
    ppermute x6, starting transfers between devices, moved(): return lax.ppermute(piece, 'chip', [(i, i ^ offset) for i in range(4)])  6.24 us
    ppermute x3, waiting for transfers between devices, local(): lax.ppermute(packed, 'chip', [(i, i + r) for i in range(chips - r)])  4.41 us
    ppermute x1, starting transfers between devices, local(): received = lax.ppermute(message, 'space', route)  2.29 us
    ppermute x1, starting transfers between devices, local(): arrived = lax.ppermute(message, 'space', route)  1.29 us
  transfers between devices with their start and end apart: 19, of which 9 were waited for; matrix products, arithmetic and copies ran while one was open for 0% of the time, Pallas kernels for 16%

commit v1 on v0

--- a/solution.py
+++ b/solution.py
@@ -17,6 +17,7 @@
 SQUARINGS = 6
 DONE = 1e-4
 STEPS_MAX = 60
+ROWS = 16
 WORK = 1
 WORK2 = 2
 WORK3 = 0.1
@@ -362,55 +363,64 @@
         packed_ref[2] = imag_of(d1)
 
 
-def unpack(pack, out):
+def unpack(pack, out, scale):
     size = pack.shape[-1]
     row = lax.broadcasted_iota(jnp.int32, (size, size), 0)
     column = lax.broadcasted_iota(jnp.int32, (size, size), 1)
-    mixed = pack[0]
+    mixed = pack[0] * scale
     turned = mixed.T
     out[0, 0] = jnp.where(row > column, mixed, jnp.where(row < column, -turned, 0.0))
     out[0, 1] = jnp.where(row > column, turned, mixed)
-    out[1] = pack[1:]
-    out[2, 0] = -pack[1].T
-    out[2, 1] = pack[2].T
-
-
-def add_term(out, spectral, blocks, scale):
-    for b in range(3):
-        w_re, w_im = blocks[b, 0], blocks[b, 1]
-        g_re, g_im = scale * spectral[b, 0], scale * spectral[b, 1]
-        out[b, 0] -= g_re * w_im + g_im * w_re
-        out[b, 1] += g_re * w_re - g_im * w_im
+    re, im = pack[1] * scale, pack[2] * scale
+    out[1, 0], out[1, 1] = re, im
+    out[2, 0], out[2, 1] = -re.T, im.T
+
+
+def unpack_all(axes, same, packs, spectral):
+    chips, cores, _ = axes
+    chip, core = lax.axis_index("chip"), lax.axis_index("core")
+    spectral[chips] = jnp.zeros(spectral.shape[1:], F32)
+    for offset in range(chips):
+        lower = jnp.bitwise_xor(chip, offset)
+
+        @pl.when(lower <= chip)
+        def _():
+            index = lower * cores + (core if same else 1 - core)
+            energy = energy_at(index.astype(F32), chips * cores)
+            occupation = 1.0 / (1.0 + jnp.exp(jnp.full((1, 1), energy / THERMAL, F32)))
+            unpack(packs[offset], spectral.at[offset], jnp.where(core == 0, -occupation, 1.0 - occupation))
 
 
 def add_terms(axes, same, only, pieces, outs, spectral):
     chips, cores, _ = axes
     chip, core = lax.axis_index("chip"), lax.axis_index("core")
-    for offset in range(chips):
-        kappa = jnp.bitwise_xor(chip, offset) if len(pieces) > 1 else jnp.int32(offset)
-        for c in range(cores):
-            p = c if same else 1 - c
-            for k in range(cores):
-                r = kappa + (p + k) // 2
-                to = 0 if (p + k) % 2 == c else 1
-                if to not in only:
-                    continue
-
-                @pl.when(jnp.logical_and(core == c, r <= chip))
-                def _():
-                    index = (chip - r) * cores + p
-                    energy = energy_at(index.astype(F32), chips * cores)
-                    occupation = 1.0 / (1.0 + jnp.exp(jnp.full((1, 1), energy / THERMAL, F32)))
-                    scale = -occupation if c == 0 else 1.0 - occupation
-                    add_term(outs[to], spectral.at[r], screened_at(pieces, offset, kappa, k), scale)
-
-
-def unpack_all(chips, packs, spectral):
-    chip = lax.axis_index("chip")
-    for r in range(chips):
-        @pl.when(chip >= r)
-        def _():
-            unpack(packs[r], spectral.at[r])
+    size = spectral.shape[-1]
+    for c in range(cores):
+        p = c if same else 1 - c
+
+        @pl.when(core == c)
+        def _():
+            for to in only:
+                k = (c + to + p) % 2
+                terms = []
+                for offset in range(chips):
+                    kappa = jnp.bitwise_xor(chip, offset) if len(pieces) > 1 else jnp.int32(offset)
+                    d = chip - kappa - (p + k) // 2
+                    place_of = jnp.where(d >= 0, jnp.bitwise_xor(chip, d), chips)
+                    terms.append((place_of, screened_at(pieces, offset, kappa, k)))
+
+                @pl.loop(0, size // ROWS)
+                def _(tile):
+                    rows = pl.ds(pl.multiple_of(tile * ROWS, ROWS), ROWS)
+                    for b in range(3):
+                        re, im = outs[to][b, 0, rows], outs[to][b, 1, rows]
+                        for place_of, blocks in terms:
+                            g_re, g_im = spectral[place_of, b, 0, rows], spectral[place_of, b, 1, rows]
+                            w_re, w_im = blocks[b, 0, rows], blocks[b, 1, rows]
+                            re = re - g_re * w_im - g_im * w_re
+                            im = im + g_re * w_re - g_im * w_im
+                        outs[to][b, 0, rows] = re
+                        outs[to][b, 1, rows] = im
 
 
 def same_core_kernel(axes, *refs):
@@ -418,7 +428,7 @@
     packs, pieces, outs, spectral = refs[:chips], refs[chips:-3], refs[-3:-1], refs[-1]
     for out in outs:
         out[...] = jnp.zeros_like(out)
-    unpack_all(chips, packs, spectral)
+    unpack_all(axes, True, packs, spectral)
     add_terms(axes, True, (0, 1), pieces, outs, spectral)
 
 
@@ -426,7 +436,7 @@
     chips = axes[0]
     packs, before, pieces, out, spectral = refs[:chips], refs[chips], refs[chips + 1 : -2], refs[-2], refs[-1]
     out[...] = before[...]
-    unpack_all(chips, packs, spectral)
+    unpack_all(axes, False, packs, spectral)
     add_terms(axes, False, (1,), pieces, (None, out), spectral)
 
 
@@ -560,11 +570,11 @@
         message, _, diagonal, upper, lower = results
     green_out, packed = results[:2]
     own = [packed] + [
-        lax.ppermute(packed, "chip", [(i, i + r) for i in range(chips - r)]) for r in range(1, chips)
+        lax.ppermute(packed, "chip", [(i, i ^ offset) for i in range(chips)]) for offset in range(1, chips)
     ]
     other = [lax.ppermute(pack, "core", swap) for pack in own]
     kind = jax.ShapeDtypeStruct(screened.shape[3:], F32)
-    unpacked = (chips, 3, 2, size, size)
+    unpacked = (chips + 1, 3, 2, size, size)
     mine, theirs = call(
         same_core_kernel, (kind,) * 2, *own, *exchange.pieces,
         scratch_shapes=[pltpu.VMEM(unpacked, F32)],

time: 52.2 us -> 51.6 us (0.989)
  starting transfers between devices: 20.2 us -> 16.1 us
  waiting for transfers between devices: 21.3 us -> 24.1 us
  Pallas kernels: 9.23 us -> 10.1 us
    ppermute x3, starting transfers between devices: 8.12 us -> 3.97 us  [local(): lax.ppermute(packed, 'chip', [(i, i ^ offset) for i in range(chips)])]
    ppermute x3, waiting for transfers between devices: 4.41 us -> 8.03 us  [local(): lax.ppermute(packed, 'chip', [(i, i ^ offset) for i in range(chips)])]
    pallas_call x9, Pallas kernels: 9.23 us -> 10.1 us  [call(): pl.pallas_call(functools.partial(body, axes), out_shape=out_shape, in_spe...]
  transfers between devices with their start and end apart: 19 -> 19, of which waited for: 9 -> 8; matrix products, arithmetic and copies ran while one was open for 0% -> 0% of each run, Pallas kernels for 16% -> 17%
where the time goes in v1:
time: 51.6 us; the launch traced here: 51.2 us
  waiting for transfers between devices  24.1 us (47%)
  starting transfers between devices  16.1 us (31%)
  Pallas kernels  10.1 us (20%)
  between operations  0.77 us (1%)
    pallas_call x9, Pallas kernels, call(): pl.pallas_call(functools.partial(body, axes), out_shape=out_shape, in_spe...  10.1 us
    ppermute x6, waiting for transfers between devices, moved(): return lax.ppermute(piece, 'chip', [(i, i ^ offset) for i in range(4)])  8.58 us
    ppermute x3, waiting for transfers between devices, local(): lax.ppermute(packed, 'chip', [(i, i ^ offset) for i in range(chips)])  8.03 us
    ppermute x1, waiting for transfers between devices, local(): arrived = lax.ppermute(message, 'space', route)  6.51 us
    ppermute x6, starting transfers between devices, moved(): return lax.ppermute(piece, 'chip', [(i, i ^ offset) for i in range(4)])  6.32 us
    ppermute x3, starting transfers between devices, local(): lax.ppermute(packed, 'chip', [(i, i ^ offset) for i in range(chips)])  3.97 us
    ppermute x1, starting transfers between devices, local(): received = lax.ppermute(message, 'space', route)  2.29 us
    ppermute x1, starting transfers between devices, local(): arrived = lax.ppermute(message, 'space', route)  1.29 us
  transfers between devices with their start and end apart: 19, of which 8 were waited for; matrix products, arithmetic and copies ran while one was open for 0% of the time, Pallas kernels for 17%

profile of v1, /device:TPU:0, one launch (start us, length us, event | category | flops | bytes accessed | tf_op | source)
XLA Modules:
  0.0 51.2 jit_solution(6234532287214343889)
XLA Ops:
  0.6 0.5 %collective-permute-start = (f32[2,3,2,128,128]{4,3,2,1,0:T(8,128)}, f32[2,3,2,128,128]{4,3,2,1,0:T(8,128)S(1)}, u32[]{:S(2)}, u32[]{:S(2)}) collective-permute-start(f32[2,3,2,128,128]{4,3,2,1,0:T(8,128)} %bitcast.7), channel_id=1, source_target_pairs={{0,4},{4,0},{1,5},{5,1},{2,6},{6,2},{3,7},{7,3},{8,12},{12,8},{9,1... | collective-permute-start | bytes 2359304 | tf_op jit(solution)/shard_map/ppermute | solution.py:468
  1.2 3.8 %shard_map.59 = (f32[128,256]{1,0:T(8,128)S(1)}, f32[128,256]{1,0:T(8,128)S(1)}, f32[128,256]{1,0:T(8,128)S(1)}, f32[128,256]{1,0:T(8,128)S(1)}, f32[128,256]{1,0:T(8,128)S(1)}, /*index=5*/f32[8,128]{1,0:T(8,128)S(1)}) custom-call(f32[1,2,128,128]{3,2,1,0:T(8,128)} %onsite_far.1, f32[1,2,128,128]{3,2,1,0:T(8,128)} %hopping_far.1, ...), custom_call_target="tpu_custom_call" | custom-call | flops 1342177280 | bytes 2097152 | tf_op jit(solution)/shard_map/pallas_call | solution.py:499
  5.1 2.3 %collective-permute-start.4 = (f32[128,256]{1,0:T(8,128)S(1)}, f32[128,256]{1,0:T(8,128)S(1)}, u32[]{:S(2)}, u32[]{:S(2)}) collective-permute-start(f32[128,256]{1,0:T(8,128)S(1)} %get-tuple-element.32.arguments_4_), channel_id=1, source_target_pairs={{0,1},{3,2},{4,5},{7,6},{8,9},{11,10},{12,13},{15,14},{16,17},{19,... | collective-permute-start | bytes 393224 | tf_op jit(solution)/shard_map/ppermute | solution.py:529
  7.6 2.6 %collective-permute-start.14 = (f32[3,2,128,128]{3,2,1,0:T(8,128)S(1)}, f32[3,2,128,128]{3,2,1,0:T(8,128)S(1)}, u32[]{:S(2)}, u32[]{:S(2)}) collective-permute-start(f32[3,2,128,128]{3,2,1,0:T(8,128)S(1)} %get-tuple-element.56.refs_4_.refs_5_.refs_0_), channel_id=1, source_target_pairs={{0,8},{8,0},{16,24},{24,16},{1,9},{9,1},{17,25},{25,17},{2,10},{10... | collective-permute-start | bytes 1179656 | tf_op jit(solution)/shard_map/ppermute | solution.py:472
  10.1 0.9 %collective-permute-start.15 = (f32[3,2,128,128]{3,2,1,0:T(8,128)S(1)}, f32[3,2,128,128]{3,2,1,0:T(8,128)S(1)}, u32[]{:S(2)}, u32[]{:S(2)}) collective-permute-start(f32[3,2,128,128]{3,2,1,0:T(8,128)S(1)} %get-tuple-element.57.refs_5_.refs_6_.refs_1_), channel_id=1, source_target_pairs={{0,16},{8,24},{16,0},{24,8},{1,17},{9,25},{17,1},{25,9},{2,18},{10... | collective-permute-start | bytes 1179656 | tf_op jit(solution)/shard_map/ppermute | solution.py:472
  11.0 1.1 %collective-permute-start.3 = (f32[3,2,128,128]{3,2,1,0:T(8,128)S(1)}, f32[3,2,128,128]{3,2,1,0:T(8,128)S(1)}, u32[]{:S(2)}, u32[]{:S(2)}) collective-permute-start(f32[3,2,128,128]{3,2,1,0:T(8,128)S(1)} %get-tuple-element.56.refs_4_.refs_5_.refs_0_), channel_id=1, source_target_pairs={{0,16},{8,24},{16,0},{24,8},{1,17},{9,25},{17,1},{25,9},{2,18},{10... | collective-permute-start | bytes 1179656 | tf_op jit(solution)/shard_map/ppermute | solution.py:472
  12.3 0.7 %shard_map.60 = (f32[128,256]{1,0:T(8,128)S(1)}, f32[128,256]{1,0:T(8,128)S(1)}, f32[128,256]{1,0:T(8,128)S(1)}, f32[128,256]{1,0:T(8,128)S(1)}, f32[128,256]{1,0:T(8,128)S(1)}, /*index=5*/f32[8,128]{1,0:T(8,128)}) custom-call(f32[8,128]{1,0:T(8,128)S(1)} %collective-permute-done.1.arguments_0_, f32[128,256]{1,0:T(8,128)S(1)} %collective-permute-done.4.arguments_1_, ...), custom_call_target="tpu_custom_call" | custom-call | flops 2684354560 | bytes 2097152 | tf_op jit(solution)/shard_map/pallas_call | solution.py:499
  12.9 0.7 %collective-permute-start.5 = (f32[128,256]{1,0:T(8,128)S(1)}, f32[128,256]{1,0:T(8,128)S(1)}, u32[]{:S(2)}, u32[]{:S(2)}) collective-permute-start(f32[128,256]{1,0:T(8,128)S(1)} %get-tuple-element.37), channel_id=1, source_target_pairs={{1,2},{2,1},{5,6},{6,5},{9,10},{10,9},{13,14},{14,13},{17,18},{18,... | collective-permute-start | bytes 393224 | tf_op jit(solution)/shard_map/ppermute | solution.py:538
  13.6 6.5 %collective-permute-done.14.refs_6_.refs_7_.refs_2_ = f32[3,2,128,128]{3,2,1,0:T(8,128)S(1)} collective-permute-done((f32[3,2,128,128]{3,2,1,0:T(8,128)S(1)}, f32[3,2,128,128]{3,2,1,0:T(8,128)S(1)}, u32[]{:S(2)}, u32[]{:S(2)}) %collective-permute-start.14) | collective-permute-done | bytes 393248 | tf_op jit(solution)/shard_map/ppermute | solution.py:472
  20.0 2.1 %collective-permute-done.15.refs_9_.refs_10_.refs_5_ = f32[3,2,128,128]{3,2,1,0:T(8,128)S(1)} collective-permute-done((f32[3,2,128,128]{3,2,1,0:T(8,128)S(1)}, f32[3,2,128,128]{3,2,1,0:T(8,128)S(1)}, u32[]{:S(2)}, u32[]{:S(2)}) %collective-permute-start.15) | collective-permute-done | bytes 393248 | tf_op jit(solution)/shard_map/ppermute | solution.py:472
  22.1 0.9 %collective-permute-start.16 = (f32[3,2,128,128]{3,2,1,0:T(8,128)S(1)}, f32[3,2,128,128]{3,2,1,0:T(8,128)S(1)}, u32[]{:S(2)}, u32[]{:S(2)}) collective-permute-start(f32[3,2,128,128]{3,2,1,0:T(8,128)S(1)} %collective-permute-done.14.refs_6_.refs_7_.refs_2_), channel_id=1, source_target_pairs={{0,16},{8,24},{16,0},{24,8},{1,17},{9,25},{17,1},{25,9},{2,18},{10... | collective-permute-start | bytes 1179656 | tf_op jit(solution)/shard_map/ppermute | solution.py:472
  23.1 1.3 %collective-permute-start.6 = (f32[128,256]{1,0:T(8,128)S(1)}, f32[128,256]{1,0:T(8,128)S(1)}, u32[]{:S(2)}, u32[]{:S(2)}) collective-permute-start(f32[128,256]{1,0:T(8,128)S(1)} %get-tuple-element.40), channel_id=1, source_target_pairs={{1,0},{2,3},{5,4},{6,7},{9,8},{10,11},{13,12},{14,15},{17,16},{18,... | collective-permute-start | bytes 393224 | tf_op jit(solution)/shard_map/ppermute | solution.py:546
  24.4 0.6 %shard_map.62 = (f32[128,256]{1,0:T(8,128)S(1)}, f32[128,256]{1,0:T(8,128)S(1)}, f32[4,128,256]{2,1,0:T(8,128)S(1)}) custom-call(f32[128,256]{1,0:T(8,128)S(1)} %collective-permute-done.5.received, f32[128,256]{1,0:T(8,128)S(1)} %get-tuple-element.41.diagonal.arguments_4_, f32[128,256]{1,0:T(8,128)S(1)} %get-tuple-element.42.u_in, ...), custom_call_target="tpu_custom_call" | custom-call | flops 134217728 | bytes 2097152 | tf_op jit(solution)/shard_map/pallas_call | solution.py:499
  24.9 0.8 %collective-permute-start.17 = (f32[3,2,128,128]{3,2,1,0:T(8,128)S(1)}, f32[3,2,128,128]{3,2,1,0:T(8,128)S(1)}, u32[]{:S(2)}, u32[]{:S(2)}) collective-permute-start(f32[3,2,128,128]{3,2,1,0:T(8,128)S(1)} %collective-permute-done.15.refs_9_.refs_10_.refs_5_), channel_id=1, source_target_pairs={{0,8},{8,0},{16,24},{24,16},{1,9},{9,1},{17,25},{25,17},{2,10},{10... | collective-permute-start | bytes 1179656 | tf_op jit(solution)/shard_map/ppermute | solution.py:472
  25.7 6.5 %collective-permute-done.6.arguments_2_ = f32[128,256]{1,0:T(8,128)S(1)} collective-permute-done((f32[128,256]{1,0:T(8,128)S(1)}, f32[128,256]{1,0:T(8,128)S(1)}, u32[]{:S(2)}, u32[]{:S(2)}) %collective-permute-start.6) | collective-permute-done | bytes 131104 | tf_op jit(solution)/shard_map/ppermute | solution.py:546
  32.2 1.9 %shard_map.63 = (f32[3,2,128,128]{3,2,1,0:T(8,128)}, f32[3,128,128]{2,1,0:T(8,128)S(1)}, f32[128,256]{1,0:T(8,128)}, f32[128,256]{1,0:T(8,128)}, f32[128,256]{1,0:T(8,128)}) custom-call(f32[3,2,128,128]{3,2,1,0:T(8,128)S(1)} %collective-permute-done.2.arguments_0_.refs_7_.refs_8_.refs_3_, ...), custom_call_target="tpu_custom_call" | custom-call | flops 134217728 | bytes 2097152 | tf_op jit(solution)/shard_map/pallas_call | solution.py:499
  34.2 2.4 %collective-permute-start.12 = (f32[3,128,128]{2,1,0:T(8,128)S(1)}, f32[3,128,128]{2,1,0:T(8,128)S(1)}, u32[]{:S(2)}, u32[]{:S(2)}) collective-permute-start(f32[3,128,128]{2,1,0:T(8,128)S(1)} %get-tuple-element.49.refs_0_), channel_id=1, source_target_pairs={{0,24},{8,16},{16,8},{24,0},{1,25},{9,17},{17,9},{25,1},{2,26},{10... | collective-permute-start | bytes 589832 | tf_op jit(solution)/shard_map/ppermute | solution.py:573
  36.6 1.5 %collective-permute-start.10 = (f32[3,128,128]{2,1,0:T(8,128)S(1)}, f32[3,128,128]{2,1,0:T(8,128)S(1)}, u32[]{:S(2)}, u32[]{:S(2)}) collective-permute-start(f32[3,128,128]{2,1,0:T(8,128)S(1)} %get-tuple-element.49.refs_0_), channel_id=1, source_target_pairs={{0,16},{8,24},{16,0},{24,8},{1,17},{9,25},{17,1},{25,9},{2,18},{10... | collective-permute-start | bytes 589832 | tf_op jit(solution)/shard_map/ppermute | solution.py:573
  38.1 4.8 %collective-permute-done.12.refs_3_ = f32[3,128,128]{2,1,0:T(8,128)S(1)} collective-permute-done((f32[3,128,128]{2,1,0:T(8,128)S(1)}, f32[3,128,128]{2,1,0:T(8,128)S(1)}, u32[]{:S(2)}, u32[]{:S(2)}) %collective-permute-start.12) | collective-permute-done | bytes 196640 | tf_op jit(solution)/shard_map/ppermute | solution.py:573
  43.0 3.2 %collective-permute-done.10.refs_2_ = f32[3,128,128]{2,1,0:T(8,128)S(1)} collective-permute-done((f32[3,128,128]{2,1,0:T(8,128)S(1)}, f32[3,128,128]{2,1,0:T(8,128)S(1)}, u32[]{:S(2)}, u32[]{:S(2)}) %collective-permute-start.10) | collective-permute-done | bytes 196640 | tf_op jit(solution)/shard_map/ppermute | solution.py:573
  46.2 0.5 collective-permute-start.11
  46.8 0.8 %shard_map.64 = (f32[3,2,128,128]{3,2,1,0:T(8,128)S(1)}, f32[3,2,128,128]{3,2,1,0:T(8,128)S(1)}) custom-call(f32[3,128,128]{2,1,0:T(8,128)S(1)} %get-tuple-element.49.refs_0_, f32[3,128,128]{2,1,0:T(8,128)S(1)} %collective-permute-done.8.refs_1_, f32[3,128,128]{2,1,0:T(8,128)S(1)} %collective-permute-done.10.refs_2_, ...), custom_call_target="tpu_custom_call" | custom-call | flops 13421772 | bytes 2097152 | tf_op jit(solution)/shard_map/pallas_call | solution.py:499
  49.0 1.1 %shard_map.66._ = f32[2,3,2,128,128]{4,3,2,1,0:T(8,128)} custom-call(f32[5,3,2,128,128]{4,3,2,1,0:T(8,128)S(1)} %get-tuple-element.54.spectral, f32[3,2,128,128]{3,2,1,0:T(8,128)S(1)} %get-tuple-element.55.before, f32[3,2,128,128]{3,2,1,0:T(8,128)S(1)} %get-tuple-element.56.refs_4_.refs_5_.refs_0_, ...), custom_call_target="tpu_custom_call" | custom-call | flops 1342177280 | bytes 2097152 | tf_op jit(solution)/shard_map/pallas_call | solution.py:499
  50.4 0.8 %shard_map.67 = f32[2,3,2,128,128]{4,3,2,1,0:T(8,128)} custom-call(f32[3,2,128,128]{3,2,1,0:T(8,128)S(1)} %collective-permute-done.18.received, f32[2,3,2,128,128]{4,3,2,1,0:T(8,128)} %shard_map.66._), custom_call_target="tpu_custom_call", output_to_operand_aliasing={{}: (1, {})} | custom-call | flops 1342177280 | bytes 2097152 | tf_op jit(solution)/shard_map/pallas_call | solution.py:499
  (27 shorter events, 2.2 us)
Async XLA Ops:
  0.6 6.8 %copy-start = (f32[1,1,2,3,2,128,128]{6,5,4,3,2,1,0:T(8,128)S(1)}, f32[1,1,2,3,2,128,128]{6,5,4,3,2,1,0:T(8,128)}, u32[]{:S(2)}) copy-start(f32[1,1,2,3,2,128,128]{6,5,4,3,2,1,0:T(8,128)} %param.7) | copy-start | bytes 2359300
  0.6 6.8 %collective-permute-start = (f32[2,3,2,128,128]{4,3,2,1,0:T(8,128)}, f32[2,3,2,128,128]{4,3,2,1,0:T(8,128)S(1)}, u32[]{:S(2)}, u32[]{:S(2)}) collective-permute-start(f32[2,3,2,128,128]{4,3,2,1,0:T(8,128)} %bitcast.7), channel_id=1, source_target_pairs={{0,4},{4,0},{1,5},{5,1},{2,6},{6,2},{3,7},{7,3},{8,12},{12,8},{9,1... | collective-permute-start | bytes 2359304 | tf_op jit(solution)/shard_map/ppermute | solution.py:468
  5.0 2.5 %collective-permute-start.1 = (f32[8,128]{1,0:T(8,128)S(1)}, f32[8,128]{1,0:T(8,128)S(1)}, u32[]{:S(2)}, u32[]{:S(2)}) collective-permute-start(f32[8,128]{1,0:T(8,128)S(1)} %get-tuple-element.29), channel_id=1, source_target_pairs={{0,4},{4,0},{1,5},{5,1},{2,6},{6,2},{3,7},{7,3},{8,12},{12,8},{9,1... | collective-permute-start | bytes 12296 | tf_op jit(solution)/shard_map/ppermute | solution.py:524
  5.1 7.1 %collective-permute-start.4 = (f32[128,256]{1,0:T(8,128)S(1)}, f32[128,256]{1,0:T(8,128)S(1)}, u32[]{:S(2)}, u32[]{:S(2)}) collective-permute-start(f32[128,256]{1,0:T(8,128)S(1)} %get-tuple-element.32.arguments_4_), channel_id=1, source_target_pairs={{0,1},{3,2},{4,5},{7,6},{8,9},{11,10},{12,13},{15,14},{16,17},{19,... | collective-permute-start | bytes 393224 | tf_op jit(solution)/shard_map/ppermute | solution.py:529
  7.6 12.5 %collective-permute-start.14 = (f32[3,2,128,128]{3,2,1,0:T(8,128)S(1)}, f32[3,2,128,128]{3,2,1,0:T(8,128)S(1)}, u32[]{:S(2)}, u32[]{:S(2)}) collective-permute-start(f32[3,2,128,128]{3,2,1,0:T(8,128)S(1)} %get-tuple-element.56.refs_4_.refs_5_.refs_0_), channel_id=1, source_target_pairs={{0,8},{8,0},{16,24},{24,16},{1,9},{9,1},{17,25},{25,17},{2,10},{10... | collective-permute-start | bytes 1179656 | tf_op jit(solution)/shard_map/ppermute | solution.py:472
  10.1 12.0 %collective-permute-start.15 = (f32[3,2,128,128]{3,2,1,0:T(8,128)S(1)}, f32[3,2,128,128]{3,2,1,0:T(8,128)S(1)}, u32[]{:S(2)}, u32[]{:S(2)}) collective-permute-start(f32[3,2,128,128]{3,2,1,0:T(8,128)S(1)} %get-tuple-element.57.refs_5_.refs_6_.refs_1_), channel_id=1, source_target_pairs={{0,16},{8,24},{16,0},{24,8},{1,17},{9,25},{17,1},{25,9},{2,18},{10... | collective-permute-start | bytes 1179656 | tf_op jit(solution)/shard_map/ppermute | solution.py:472
  11.0 21.2 %collective-permute-start.3 = (f32[3,2,128,128]{3,2,1,0:T(8,128)S(1)}, f32[3,2,128,128]{3,2,1,0:T(8,128)S(1)}, u32[]{:S(2)}, u32[]{:S(2)}) collective-permute-start(f32[3,2,128,128]{3,2,1,0:T(8,128)S(1)} %get-tuple-element.56.refs_4_.refs_5_.refs_0_), channel_id=1, source_target_pairs={{0,16},{8,24},{16,0},{24,8},{1,17},{9,25},{17,1},{25,9},{2,18},{10... | collective-permute-start | bytes 1179656 | tf_op jit(solution)/shard_map/ppermute | solution.py:472
  12.2 20.1 %collective-permute-start.2 = (f32[3,2,128,128]{3,2,1,0:T(8,128)S(1)}, f32[3,2,128,128]{3,2,1,0:T(8,128)S(1)}, u32[]{:S(2)}, u32[]{:S(2)}) collective-permute-start(f32[3,2,128,128]{3,2,1,0:T(8,128)S(1)} %get-tuple-element.57.refs_5_.refs_6_.refs_1_), channel_id=1, source_target_pairs={{0,8},{8,0},{16,24},{24,16},{1,9},{9,1},{17,25},{25,17},{2,10},{10... | collective-permute-start | bytes 1179656 | tf_op jit(solution)/shard_map/ppermute | solution.py:472
  12.9 10.1 %collective-permute-start.5 = (f32[128,256]{1,0:T(8,128)S(1)}, f32[128,256]{1,0:T(8,128)S(1)}, u32[]{:S(2)}, u32[]{:S(2)}) collective-permute-start(f32[128,256]{1,0:T(8,128)S(1)} %get-tuple-element.37), channel_id=1, source_target_pairs={{1,2},{2,1},{5,6},{6,5},{9,10},{10,9},{13,14},{14,13},{17,18},{18,... | collective-permute-start | bytes 393224 | tf_op jit(solution)/shard_map/ppermute | solution.py:538
  22.1 24.5 %collective-permute-start.16 = (f32[3,2,128,128]{3,2,1,0:T(8,128)S(1)}, f32[3,2,128,128]{3,2,1,0:T(8,128)S(1)}, u32[]{:S(2)}, u32[]{:S(2)}) collective-permute-start(f32[3,2,128,128]{3,2,1,0:T(8,128)S(1)} %collective-permute-done.14.refs_6_.refs_7_.refs_2_), channel_id=1, source_target_pairs={{0,16},{8,24},{16,0},{24,8},{1,17},{9,25},{17,1},{25,9},{2,18},{10... | collective-permute-start | bytes 1179656 | tf_op jit(solution)/shard_map/ppermute | solution.py:472
  23.1 9.2 %collective-permute-start.6 = (f32[128,256]{1,0:T(8,128)S(1)}, f32[128,256]{1,0:T(8,128)S(1)}, u32[]{:S(2)}, u32[]{:S(2)}) collective-permute-start(f32[128,256]{1,0:T(8,128)S(1)} %get-tuple-element.40), channel_id=1, source_target_pairs={{1,0},{2,3},{5,4},{6,7},{9,8},{10,11},{13,12},{14,15},{17,16},{18,... | collective-permute-start | bytes 393224 | tf_op jit(solution)/shard_map/ppermute | solution.py:546
  24.9 21.8 %collective-permute-start.17 = (f32[3,2,128,128]{3,2,1,0:T(8,128)S(1)}, f32[3,2,128,128]{3,2,1,0:T(8,128)S(1)}, u32[]{:S(2)}, u32[]{:S(2)}) collective-permute-start(f32[3,2,128,128]{3,2,1,0:T(8,128)S(1)} %collective-permute-done.15.refs_9_.refs_10_.refs_5_), channel_id=1, source_target_pairs={{0,8},{8,0},{16,24},{24,16},{1,9},{9,1},{17,25},{25,17},{2,10},{10... | collective-permute-start | bytes 1179656 | tf_op jit(solution)/shard_map/ppermute | solution.py:472
  34.2 8.8 %collective-permute-start.12 = (f32[3,128,128]{2,1,0:T(8,128)S(1)}, f32[3,128,128]{2,1,0:T(8,128)S(1)}, u32[]{:S(2)}, u32[]{:S(2)}) collective-permute-start(f32[3,128,128]{2,1,0:T(8,128)S(1)} %get-tuple-element.49.refs_0_), channel_id=1, source_target_pairs={{0,24},{8,16},{16,8},{24,0},{1,25},{9,17},{17,9},{25,1},{2,26},{10... | collective-permute-start | bytes 589832 | tf_op jit(solution)/shard_map/ppermute | solution.py:573
  36.6 9.6 %collective-permute-start.10 = (f32[3,128,128]{2,1,0:T(8,128)S(1)}, f32[3,128,128]{2,1,0:T(8,128)S(1)}, u32[]{:S(2)}, u32[]{:S(2)}) collective-permute-start(f32[3,128,128]{2,1,0:T(8,128)S(1)} %get-tuple-element.49.refs_0_), channel_id=1, source_target_pairs={{0,16},{8,24},{16,0},{24,8},{1,17},{9,25},{17,1},{25,9},{2,18},{10... | collective-permute-start | bytes 589832 | tf_op jit(solution)/shard_map/ppermute | solution.py:573
  38.1 8.0 %collective-permute-start.8 = (f32[3,128,128]{2,1,0:T(8,128)S(1)}, f32[3,128,128]{2,1,0:T(8,128)S(1)}, u32[]{:S(2)}, u32[]{:S(2)}) collective-permute-start(f32[3,128,128]{2,1,0:T(8,128)S(1)} %get-tuple-element.49.refs_0_), channel_id=1, source_target_pairs={{0,8},{8,0},{16,24},{24,16},{1,9},{9,1},{17,25},{25,17},{2,10},{10... | collective-permute-start | bytes 589832 | tf_op jit(solution)/shard_map/ppermute | solution.py:573
  43.0 4.6 %collective-permute-start.7 = (f32[3,128,128]{2,1,0:T(8,128)S(1)}, f32[3,128,128]{2,1,0:T(8,128)S(1)}, u32[]{:S(2)}, u32[]{:S(2)}) collective-permute-start(f32[3,128,128]{2,1,0:T(8,128)S(1)} %get-tuple-element.49.refs_0_), channel_id=1, source_target_pairs={{0,4},{4,0},{1,5},{5,1},{2,6},{6,2},{3,7},{7,3},{8,12},{12,8},{9,1... | collective-permute-start | bytes 589832 | tf_op jit(solution)/shard_map/ppermute | solution.py:575
  46.2 1.4 %collective-permute-start.13 = (f32[3,128,128]{2,1,0:T(8,128)S(1)}, f32[3,128,128]{2,1,0:T(8,128)S(1)}, u32[]{:S(2)}, u32[]{:S(2)}) collective-permute-start(f32[3,128,128]{2,1,0:T(8,128)S(1)} %collective-permute-done.12.refs_3_), channel_id=1, source_target_pairs={{0,4},{4,0},{1,5},{5,1},{2,6},{6,2},{3,7},{7,3},{8,12},{12,8},{9,1... | collective-permute-start | bytes 589832 | tf_op jit(solution)/shard_map/ppermute | solution.py:575
  46.2 1.7 %collective-permute-start.11 = (f32[3,128,128]{2,1,0:T(8,128)S(1)}, f32[3,128,128]{2,1,0:T(8,128)S(1)}, u32[]{:S(2)}, u32[]{:S(2)}) collective-permute-start(f32[3,128,128]{2,1,0:T(8,128)S(1)} %collective-permute-done.10.refs_2_), channel_id=1, source_target_pairs={{0,4},{4,0},{1,5},{5,1},{2,6},{6,2},{3,7},{7,3},{8,12},{12,8},{9,1... | collective-permute-start | bytes 589832 | tf_op jit(solution)/shard_map/ppermute | solution.py:575
  46.7 1.5 %collective-permute-start.9 = (f32[3,128,128]{2,1,0:T(8,128)S(1)}, f32[3,128,128]{2,1,0:T(8,128)S(1)}, u32[]{:S(2)}, u32[]{:S(2)}) collective-permute-start(f32[3,128,128]{2,1,0:T(8,128)S(1)} %collective-permute-done.8.refs_1_), channel_id=1, source_target_pairs={{0,4},{4,0},{1,5},{5,1},{2,6},{6,2},{3,7},{7,3},{8,12},{12,8},{9,1... | collective-permute-start | bytes 589832 | tf_op jit(solution)/shard_map/ppermute | solution.py:575
  48.7 1.8 %collective-permute-start.18 = (f32[3,2,128,128]{3,2,1,0:T(8,128)S(1)}, f32[3,2,128,128]{3,2,1,0:T(8,128)S(1)}, u32[]{:S(2)}, u32[]{:S(2)}) collective-permute-start(f32[3,2,128,128]{3,2,1,0:T(8,128)S(1)} %get-tuple-element.53), channel_id=1, source_target_pairs={{0,4},{4,0},{1,5},{5,1},{2,6},{6,2},{3,7},{7,3},{8,12},{12,8},{9,1... | collective-permute-start | bytes 1179656 | tf_op jit(solution)/shard_map/ppermute | solution.py:586

commit v2 on v1

--- a/solution.py
+++ b/solution.py
@@ -210,8 +210,7 @@
         message_ref[...] = product(h, product(green_ref[...], hd))
 
 
-def inward_kernel(axes, level, _, received, system, green, message, u, outside, h, hd, system_ref, green_ref, message_ref, u_ref, outside_ref, token_ref):
-    token_ref[...] = jnp.zeros_like(token_ref)
+def inward_kernel(axes, level, _, received, system, green, message, u, outside, h, hd, system_ref, green_ref, message_ref, u_ref, outside_ref):
     _, depth, left = place(axes)
 
     @pl.when(depth == level)
@@ -271,7 +270,8 @@
         message_ref[...] = jnp.zeros_like(message_ref)
 
 
-def waiting_kernel(axes, received, diagonal, u_in, u_out, outside, h, hd, upper_ref, lower_ref, ready_ref):
+def waiting_kernel(axes, waited, *refs):
+    received, diagonal, u_in, u_out, outside, h, hd, upper_ref, lower_ref, ready_ref = refs[waited:]
     position, depth, left = place(axes)
     energy = energy_point(axes)
     magnitude = energy * energy + BROADEN * BROADEN
@@ -310,16 +310,12 @@
         lower_ref[...] = jnp.zeros_like(lower_ref)
 
 
-def outward_kernel(axes, level, final, waited, *refs):
-    outward(axes, level, final, *refs[waited:])
-
-
-def outward(axes, level, final, received, ready, diagonal, upper, lower, h, hd, *outputs):
+def outward_kernel(axes, level, final, received, ready, diagonal, upper, lower, h, hd, *outputs):
     _, depth, left = place(axes)
     if final:
-        green_out, packed_ref, green_ref, upper_ref, lower_ref = outputs
+        packed_ref, green_ref, upper_ref, lower_ref = outputs
     else:
-        message_ref, _, green_ref, upper_ref, lower_ref = outputs
+        message_ref, green_ref, upper_ref, lower_ref = outputs
         message_ref[...] = jnp.zeros_like(message_ref)
 
     @pl.when(depth != level)
@@ -351,9 +347,6 @@
     if final:
         size = diagonal.shape[0]
         blocks = (green_ref[...], upper_ref[...], lower_ref[...])
-        for b, block in enumerate(blocks):
-            green_out[b, 0] = real_of(block)
-            green_out[b, 1] = imag_of(block)
         d0 = blocks[0] - dagger(blocks[0])
         d1 = blocks[1] - dagger(blocks[2])
         row = lax.broadcasted_iota(jnp.int32, (size, size), 0)
@@ -361,6 +354,19 @@
         packed_ref[0] = jnp.where(row > column, real_of(d0), imag_of(d0))
         packed_ref[1] = real_of(d1)
         packed_ref[2] = imag_of(d1)
+
+
+def store_kernel(axes, diagonal, upper, lower, out, arrivals):
+    size = diagonal.shape[0]
+    copies = [
+        pltpu.make_async_copy(block.at[:, pl.ds(part * size, size)], out.at[b, part], arrivals.at[2 * b + part])
+        for b, block in enumerate((diagonal, upper, lower))
+        for part in range(2)
+    ]
+    for copy in copies:
+        copy.start()
+    for copy in copies:
+        copy.wait()
 
 
 def unpack(pack, out, scale):
@@ -527,14 +533,14 @@
     for level in range(1, half):
         route = [(level - 1, level), (cells_all - level, cells_all - 1 - level)]
         received = lax.ppermute(message, "space", route)
-        system, green, message, u_out, outside, next_mark = call(
+        system, green, message, u_out, outside = call(
             functools.partial(swapped, inward_kernel, level),
-            (matrix,) * 5 + (token,),
+            (matrix,) * 5,
             mark, received, system, green, message, u_out, outside, h, hd,
             work=WORK2,
         )
         if level == half - 1:
-            exchange.go_on(next_mark)
+            exchange.go_on(message)
     received = lax.ppermute(message, "space", [(half - 1, half), (half, half - 1)])
     diagonal, message, u_in = call(
         middle_kernel, (matrix,) * 3, received, system, green, h, hd,
@@ -546,33 +552,34 @@
         arrived = lax.ppermute(message, "space", route)
         if upper is None:
             upper, lower, ready = call(
-                waiting_kernel,
+                functools.partial(swapped, waiting_kernel, len(exchange.later)),
                 (matrix, matrix, jax.ShapeDtypeStruct((4, size, 2 * size), F32)),
-                received, diagonal, u_in, u_out, outside, h, hd,
+                *exchange.later, received, diagonal, u_in, u_out, outside, h, hd,
+                space=[pl.ANY] * len(exchange.later) + [pltpu.VMEM] * 7,
                 work=WORK4,
             )
         final = level == 0
-        shapes = (matrix,) * 3
-        if final:
-            shapes = (
-                jax.ShapeDtypeStruct((3, 2, size, size), F32),
-                jax.ShapeDtypeStruct((3, size, size), F32),
-            ) + shapes
-        else:
-            shapes = (matrix, token) + shapes
+        shapes = (jax.ShapeDtypeStruct((3, size, size), F32) if final else matrix,) + (matrix,) * 3
         results = call(
-            functools.partial(swapped, outward_kernel, level, final, len(exchange.later)),
+            functools.partial(swapped, outward_kernel, level, final),
             shapes,
-            *exchange.later, arrived, ready, diagonal, upper, lower, h, hd,
-            space=[pl.ANY] * len(exchange.later) + [pltpu.VMEM] * 7,
+            arrived, ready, diagonal, upper, lower, h, hd,
             work=WORK6,
         )
-        message, _, diagonal, upper, lower = results
-    green_out, packed = results[:2]
+        message, diagonal, upper, lower = results
+    packed = message
+    green_out = call(
+        store_kernel,
+        jax.ShapeDtypeStruct((3, 2, size, size), F32),
+        diagonal, upper, lower,
+        out_space=pl.ANY,
+        scratch_shapes=[pltpu.SemaphoreType.DMA((6,))],
+    )
     own = [packed] + [
         lax.ppermute(packed, "chip", [(i, i ^ offset) for i in range(chips)]) for offset in range(1, chips)
     ]
-    other = [lax.ppermute(pack, "core", swap) for pack in own]
+    kept, green_out = lax.optimization_barrier((packed, green_out))
+    other = [lax.ppermute(pack, "core", swap) for pack in [kept] + own[1:]]
     kind = jax.ShapeDtypeStruct(screened.shape[3:], F32)
     unpacked = (chips + 1, 3, 2, size, size)
     mine, theirs = call(

time: 51.6 us -> 50.8 us (0.984)
  Pallas kernels: 10.1 us -> 9.53 us
    ppermute x6, waiting for transfers between devices: 8.58 us -> 14 us  [moved(): return lax.ppermute(piece, 'chip', [(i, i ^ offset) for i in range(4)])]
    ppermute x1, waiting for transfers between devices: 6.51 us -> 1.14 us  [local(): arrived = lax.ppermute(message, 'space', route)]
    pallas_call x9 -> x10, Pallas kernels: 10.1 us -> 9.53 us  [call(): pl.pallas_call(functools.partial(body, axes), out_shape=out_shape, in_spe...]
  transfers between devices with their start and end apart: 19 -> 19, of which waited for: 8 -> 9; matrix products, arithmetic and copies ran while one was open for 0% -> 0% of each run, Pallas kernels for 17% -> 16%
where the time goes in v2:
time: 50.8 us; the launch traced here: 50.6 us
  waiting for transfers between devices  24.6 us (48%)
  starting transfers between devices  15.6 us (31%)
  Pallas kernels  9.53 us (19%)
  between operations  0.79 us (2%)
    ppermute x6, waiting for transfers between devices, moved(): return lax.ppermute(piece, 'chip', [(i, i ^ offset) for i in range(4)])  14 us
    pallas_call x10, Pallas kernels, call(): pl.pallas_call(functools.partial(body, axes), out_shape=out_shape, in_spe...  9.53 us
    ppermute x3, waiting for transfers between devices, local(): lax.ppermute(packed, 'chip', [(i, i ^ offset) for i in range(chips)])  8.41 us
    ppermute x6, starting transfers between devices, moved(): return lax.ppermute(piece, 'chip', [(i, i ^ offset) for i in range(4)])  6.24 us
    ppermute x3, starting transfers between devices, local(): lax.ppermute(packed, 'chip', [(i, i ^ offset) for i in range(chips)])  3.55 us
    ppermute x1, starting transfers between devices, local(): received = lax.ppermute(message, 'space', route)  2.29 us
    ppermute x1, starting transfers between devices, local(): arrived = lax.ppermute(message, 'space', route)  1.29 us
    ppermute x1, waiting for transfers between devices, local(): arrived = lax.ppermute(message, 'space', route)  1.14 us
  transfers between devices with their start and end apart: 19, of which 9 were waited for; matrix products, arithmetic and copies ran while one was open for 0% of the time, Pallas kernels for 16%

profile of v2, /device:TPU:0, one launch (start us, length us, event | category | flops | bytes accessed | tf_op | source)
XLA Modules:
  0.0 50.6 jit_solution(6855549056644200003)
XLA Ops:
  0.6 0.5 %collective-permute-start.4 = (f32[2,3,2,128,128]{4,3,2,1,0:T(8,128)}, f32[2,3,2,128,128]{4,3,2,1,0:T(8,128)S(1)}, u32[]{:S(2)}, u32[]{:S(2)}) collective-permute-start(f32[2,3,2,128,128]{4,3,2,1,0:T(8,128)} %bitcast.7), channel_id=1, source_target_pairs={{0,4},{4,0},{1,5},{5,1},{2,6},{6,2},{3,7},{7,3},{8,12},{12,8},{9,1... | collective-permute-start | bytes 2359304 | tf_op jit(solution)/shard_map/ppermute | solution.py:474
  1.2 3.8 %shard_map.59 = (f32[128,256]{1,0:T(8,128)S(1)}, f32[128,256]{1,0:T(8,128)S(1)}, f32[128,256]{1,0:T(8,128)S(1)}, f32[128,256]{1,0:T(8,128)S(1)}, f32[128,256]{1,0:T(8,128)S(1)}, /*index=5*/f32[8,128]{1,0:T(8,128)S(1)}) custom-call(f32[1,2,128,128]{3,2,1,0:T(8,128)} %onsite_far.1, f32[1,2,128,128]{3,2,1,0:T(8,128)} %hopping_far.1, ...), custom_call_target="tpu_custom_call" | custom-call | flops 1342177280 | bytes 2097152 | tf_op jit(solution)/shard_map/pallas_call | solution.py:505
  5.1 2.3 %collective-permute-start.1 = (f32[128,256]{1,0:T(8,128)S(1)}, f32[128,256]{1,0:T(8,128)S(1)}, u32[]{:S(2)}, u32[]{:S(2)}) collective-permute-start(f32[128,256]{1,0:T(8,128)S(1)} %get-tuple-element.34.arguments_4_), channel_id=1, source_target_pairs={{0,1},{3,2},{4,5},{7,6},{8,9},{11,10},{12,13},{15,14},{16,17},{19,... | collective-permute-start | bytes 393224 | tf_op jit(solution)/shard_map/ppermute | solution.py:535
  7.6 1.9 %collective-permute-start.14 = (f32[3,2,128,128]{3,2,1,0:T(8,128)S(1)}, f32[3,2,128,128]{3,2,1,0:T(8,128)S(1)}, u32[]{:S(2)}, u32[]{:S(2)}) collective-permute-start(f32[3,2,128,128]{3,2,1,0:T(8,128)S(1)} %get-tuple-element.64.refs_4_.refs_5_.refs_0_), channel_id=1, source_target_pairs={{0,8},{8,0},{16,24},{24,16},{1,9},{9,1},{17,25},{25,17},{2,10},{10... | collective-permute-start | bytes 1179656 | tf_op jit(solution)/shard_map/ppermute | solution.py:478
  9.5 1.5 %collective-permute-start.15 = (f32[3,2,128,128]{3,2,1,0:T(8,128)S(1)}, f32[3,2,128,128]{3,2,1,0:T(8,128)S(1)}, u32[]{:S(2)}, u32[]{:S(2)}) collective-permute-start(f32[3,2,128,128]{3,2,1,0:T(8,128)S(1)} %get-tuple-element.65.refs_5_.refs_6_.refs_1_), channel_id=1, source_target_pairs={{0,16},{8,24},{16,0},{24,8},{1,17},{9,25},{17,1},{25,9},{2,18},{10... | collective-permute-start | bytes 1179656 | tf_op jit(solution)/shard_map/ppermute | solution.py:478
  11.8 0.7 %collective-permute-start.2 = (f32[128,256]{1,0:T(8,128)S(1)}, f32[128,256]{1,0:T(8,128)S(1)}, u32[]{:S(2)}, u32[]{:S(2)}) collective-permute-start(f32[128,256]{1,0:T(8,128)S(1)} %get-tuple-element.39), channel_id=1, source_target_pairs={{1,2},{2,1},{5,6},{6,5},{9,10},{10,9},{13,14},{14,13},{17,18},{18,... | collective-permute-start | bytes 393224 | tf_op jit(solution)/shard_map/ppermute | solution.py:544
  12.4 7.1 %collective-permute-done.14.refs_6_.refs_7_.refs_2_ = f32[3,2,128,128]{3,2,1,0:T(8,128)S(1)} collective-permute-done((f32[3,2,128,128]{3,2,1,0:T(8,128)S(1)}, f32[3,2,128,128]{3,2,1,0:T(8,128)S(1)}, u32[]{:S(2)}, u32[]{:S(2)}) %collective-permute-start.14) | collective-permute-done | bytes 393248 | tf_op jit(solution)/shard_map/ppermute | solution.py:478
  19.6 1.9 %collective-permute-done.15.refs_9_.refs_10_.refs_5_ = f32[3,2,128,128]{3,2,1,0:T(8,128)S(1)} collective-permute-done((f32[3,2,128,128]{3,2,1,0:T(8,128)S(1)}, f32[3,2,128,128]{3,2,1,0:T(8,128)S(1)}, u32[]{:S(2)}, u32[]{:S(2)}) %collective-permute-start.15) | collective-permute-done | bytes 393248 | tf_op jit(solution)/shard_map/ppermute | solution.py:478
  21.5 1.5 %collective-permute-start.16 = (f32[3,2,128,128]{3,2,1,0:T(8,128)S(1)}, f32[3,2,128,128]{3,2,1,0:T(8,128)S(1)}, u32[]{:S(2)}, u32[]{:S(2)}) collective-permute-start(f32[3,2,128,128]{3,2,1,0:T(8,128)S(1)} %collective-permute-done.14.refs_6_.refs_7_.refs_2_), channel_id=1, source_target_pairs={{0,16},{8,24},{16,0},{24,8},{1,17},{9,25},{17,1},{25,9},{2,18},{10... | collective-permute-start | bytes 1179656 | tf_op jit(solution)/shard_map/ppermute | solution.py:478
  23.1 1.3 %collective-permute-start.3 = (f32[128,256]{1,0:T(8,128)S(1)}, f32[128,256]{1,0:T(8,128)S(1)}, u32[]{:S(2)}, u32[]{:S(2)}) collective-permute-start(f32[128,256]{1,0:T(8,128)S(1)} %get-tuple-element.42), channel_id=1, source_target_pairs={{1,0},{2,3},{5,4},{6,7},{9,8},{10,11},{13,12},{14,15},{17,16},{18,... | collective-permute-start | bytes 393224 | tf_op jit(solution)/shard_map/ppermute | solution.py:552
  24.4 0.6 %collective-permute-start.17 = (f32[3,2,128,128]{3,2,1,0:T(8,128)S(1)}, f32[3,2,128,128]{3,2,1,0:T(8,128)S(1)}, u32[]{:S(2)}, u32[]{:S(2)}) collective-permute-start(f32[3,2,128,128]{3,2,1,0:T(8,128)S(1)} %collective-permute-done.15.refs_9_.refs_10_.refs_5_), channel_id=1, source_target_pairs={{0,8},{8,0},{16,24},{24,16},{1,9},{9,1},{17,25},{25,17},{2,10},{10... | collective-permute-start | bytes 1179656 | tf_op jit(solution)/shard_map/ppermute | solution.py:478
  25.0 5.0 %collective-permute-done.6.arguments_1_.refs_8_.refs_9_.refs_4_ = f32[3,2,128,128]{3,2,1,0:T(8,128)S(1)} collective-permute-done((f32[3,2,128,128]{3,2,1,0:T(8,128)S(1)}, f32[3,2,128,128]{3,2,1,0:T(8,128)S(1)}, u32[]{:S(2)}, u32[]{:S(2)}) %collective-permute-start.6) | collective-permute-done | bytes 393248 | tf_op jit(solution)/shard_map/ppermute | solution.py:478
  29.9 0.5 %shard_map.62 = (f32[128,256]{1,0:T(8,128)S(1)}, f32[128,256]{1,0:T(8,128)S(1)}, f32[4,128,256]{2,1,0:T(8,128)S(1)}) custom-call(f32[3,2,128,128]{3,2,1,0:T(8,128)S(1)} %collective-permute-done.5.arguments_0_.refs_7_.refs_8_.refs_3_, f32[3,2,128,128]{3,2,1,0:T(8,128)S(1)} %collective-permute-done.6.arguments_1_.refs_8_.refs_9_.refs_4_, ...), custom_call_target="tpu_custom_call" | custom-call | flops 134217728 | bytes 2097152 | tf_op jit(solution)/shard_map/pallas_call | solution.py:505
  30.5 1.1 %collective-permute-done.3.arguments_0_ = f32[128,256]{1,0:T(8,128)S(1)} collective-permute-done((f32[128,256]{1,0:T(8,128)S(1)}, f32[128,256]{1,0:T(8,128)S(1)}, u32[]{:S(2)}, u32[]{:S(2)}) %collective-permute-start.3) | collective-permute-done | bytes 131104 | tf_op jit(solution)/shard_map/ppermute | solution.py:552
  31.6 1.2 %shard_map.63 = (f32[3,128,128]{2,1,0:T(8,128)S(1)}, f32[128,256]{1,0:T(8,128)S(1)}, f32[128,256]{1,0:T(8,128)S(1)}, f32[128,256]{1,0:T(8,128)S(1)}) custom-call(f32[128,256]{1,0:T(8,128)S(1)} %collective-permute-done.3.arguments_0_, f32[4,128,256]{2,1,0:T(8,128)S(1)} %get-tuple-element.49.arguments_1_, ...), custom_call_target="tpu_custom_call" | custom-call | flops 134217728 | bytes 2097152 | tf_op jit(solution)/shard_map/pallas_call | solution.py:505
  32.8 2.5 %collective-permute-start.12 = (f32[3,128,128]{2,1,0:T(8,128)S(1)}, f32[3,128,128]{2,1,0:T(8,128)S(1)}, u32[]{:S(2)}, u32[]{:S(2)}) collective-permute-start(f32[3,128,128]{2,1,0:T(8,128)S(1)} %get-tuple-element.57.refs_0_), channel_id=1, source_target_pairs={{0,24},{8,16},{16,8},{24,0},{1,25},{9,17},{17,9},{25,1},{2,26},{10... | collective-permute-start | bytes 589832 | tf_op jit(solution)/shard_map/ppermute | solution.py:579
  35.9 0.5 %collective-permute-start.8 = (f32[3,128,128]{2,1,0:T(8,128)S(1)}, f32[3,128,128]{2,1,0:T(8,128)S(1)}, u32[]{:S(2)}, u32[]{:S(2)}) collective-permute-start(f32[3,128,128]{2,1,0:T(8,128)S(1)} %get-tuple-element.57.refs_0_), channel_id=1, source_target_pairs={{0,8},{8,0},{16,24},{24,16},{1,9},{9,1},{17,25},{25,17},{2,10},{10... | collective-permute-start | bytes 589832 | tf_op jit(solution)/shard_map/ppermute | solution.py:579
  36.4 0.8 %shard_map.64 = f32[3,2,128,128]{3,2,1,0:T(8,128)} custom-call(f32[128,256]{1,0:T(8,128)S(1)} %get-tuple-element.53.diagonal, f32[128,256]{1,0:T(8,128)S(1)} %get-tuple-element.54.upper, f32[128,256]{1,0:T(8,128)S(1)} %get-tuple-element.55.lower), custom_call_target="tpu_custom_call" | custom-call | flops 1342177280 | bytes 2097152 | tf_op jit(solution)/shard_map/pallas_call | solution.py:505
  37.2 4.9 %collective-permute-done.12.refs_3_ = f32[3,128,128]{2,1,0:T(8,128)S(1)} collective-permute-done((f32[3,128,128]{2,1,0:T(8,128)S(1)}, f32[3,128,128]{2,1,0:T(8,128)S(1)}, u32[]{:S(2)}, u32[]{:S(2)}) %collective-permute-start.12) | collective-permute-done | bytes 196640 | tf_op jit(solution)/shard_map/ppermute | solution.py:579
  42.0 3.5 %collective-permute-done.10.refs_2_ = f32[3,128,128]{2,1,0:T(8,128)S(1)} collective-permute-done((f32[3,128,128]{2,1,0:T(8,128)S(1)}, f32[3,128,128]{2,1,0:T(8,128)S(1)}, u32[]{:S(2)}, u32[]{:S(2)}) %collective-permute-start.10) | collective-permute-done | bytes 196640 | tf_op jit(solution)/shard_map/ppermute | solution.py:579
  45.6 0.5 %collective-permute-start.11 = (f32[3,128,128]{2,1,0:T(8,128)S(1)}, f32[3,128,128]{2,1,0:T(8,128)S(1)}, u32[]{:S(2)}, u32[]{:S(2)}) collective-permute-start(f32[3,128,128]{2,1,0:T(8,128)S(1)} %collective-permute-done.10.refs_2_), channel_id=1, source_target_pairs={{0,4},{4,0},{1,5},{5,1},{2,6},{6,2},{3,7},{7,3},{8,12},{12,8},{9,1... | collective-permute-start | bytes 589832 | tf_op jit(solution)/shard_map/ppermute | solution.py:582
  46.2 0.8 %shard_map.65 = (f32[3,2,128,128]{3,2,1,0:T(8,128)S(1)}, f32[3,2,128,128]{3,2,1,0:T(8,128)S(1)}) custom-call(f32[3,128,128]{2,1,0:T(8,128)S(1)} %get-tuple-element.57.refs_0_, f32[3,128,128]{2,1,0:T(8,128)S(1)} %collective-permute-done.8.refs_1_, f32[3,128,128]{2,1,0:T(8,128)S(1)} %collective-permute-done.10.refs_2_, ...), custom_call_target="tpu_custom_call" | custom-call | flops 13421772 | bytes 2097152 | tf_op jit(solution)/shard_map/pallas_call | solution.py:505
  48.4 1.1 %shard_map.67._ = f32[2,3,2,128,128]{4,3,2,1,0:T(8,128)} custom-call(f32[5,3,2,128,128]{4,3,2,1,0:T(8,128)S(1)} %get-tuple-element.62.spectral, f32[3,2,128,128]{3,2,1,0:T(8,128)S(1)} %get-tuple-element.63.before, f32[3,2,128,128]{3,2,1,0:T(8,128)S(1)} %get-tuple-element.64.refs_4_.refs_5_.refs_0_, ...), custom_call_target="tpu_custom_call" | custom-call | flops 1342177280 | bytes 2097152 | tf_op jit(solution)/shard_map/pallas_call | solution.py:505
  49.9 0.8 %shard_map.68 = f32[2,3,2,128,128]{4,3,2,1,0:T(8,128)} custom-call(f32[3,2,128,128]{3,2,1,0:T(8,128)S(1)} %collective-permute-done.18.received, f32[2,3,2,128,128]{4,3,2,1,0:T(8,128)} %shard_map.67._), custom_call_target="tpu_custom_call", output_to_operand_aliasing={{}: (1, {})} | custom-call | flops 1342177280 | bytes 2097152 | tf_op jit(solution)/shard_map/pallas_call | solution.py:505
  (28 shorter events, 3.4 us)
Async XLA Ops:
  0.6 6.8 %copy-start = (f32[1,1,2,3,2,128,128]{6,5,4,3,2,1,0:T(8,128)S(1)}, f32[1,1,2,3,2,128,128]{6,5,4,3,2,1,0:T(8,128)}, u32[]{:S(2)}) copy-start(f32[1,1,2,3,2,128,128]{6,5,4,3,2,1,0:T(8,128)} %param.7) | copy-start | bytes 2359300
  0.6 6.8 %collective-permute-start.4 = (f32[2,3,2,128,128]{4,3,2,1,0:T(8,128)}, f32[2,3,2,128,128]{4,3,2,1,0:T(8,128)S(1)}, u32[]{:S(2)}, u32[]{:S(2)}) collective-permute-start(f32[2,3,2,128,128]{4,3,2,1,0:T(8,128)} %bitcast.7), channel_id=1, source_target_pairs={{0,4},{4,0},{1,5},{5,1},{2,6},{6,2},{3,7},{7,3},{8,12},{12,8},{9,1... | collective-permute-start | bytes 2359304 | tf_op jit(solution)/shard_map/ppermute | solution.py:474
  5.0 2.5 %collective-permute-start = (f32[8,128]{1,0:T(8,128)S(1)}, f32[8,128]{1,0:T(8,128)S(1)}, u32[]{:S(2)}, u32[]{:S(2)}) collective-permute-start(f32[8,128]{1,0:T(8,128)S(1)} %get-tuple-element.33), channel_id=1, source_target_pairs={{0,4},{4,0},{1,5},{5,1},{2,6},{6,2},{3,7},{7,3},{8,12},{12,8},{9,1... | collective-permute-start | bytes 12296 | tf_op jit(solution)/shard_map/ppermute | solution.py:530
  5.1 6.5 %collective-permute-start.1 = (f32[128,256]{1,0:T(8,128)S(1)}, f32[128,256]{1,0:T(8,128)S(1)}, u32[]{:S(2)}, u32[]{:S(2)}) collective-permute-start(f32[128,256]{1,0:T(8,128)S(1)} %get-tuple-element.34.arguments_4_), channel_id=1, source_target_pairs={{0,1},{3,2},{4,5},{7,6},{8,9},{11,10},{12,13},{15,14},{16,17},{19,... | collective-permute-start | bytes 393224 | tf_op jit(solution)/shard_map/ppermute | solution.py:535
  7.6 12.0 %collective-permute-start.14 = (f32[3,2,128,128]{3,2,1,0:T(8,128)S(1)}, f32[3,2,128,128]{3,2,1,0:T(8,128)S(1)}, u32[]{:S(2)}, u32[]{:S(2)}) collective-permute-start(f32[3,2,128,128]{3,2,1,0:T(8,128)S(1)} %get-tuple-element.64.refs_4_.refs_5_.refs_0_), channel_id=1, source_target_pairs={{0,8},{8,0},{16,24},{24,16},{1,9},{9,1},{17,25},{25,17},{2,10},{10... | collective-permute-start | bytes 1179656 | tf_op jit(solution)/shard_map/ppermute | solution.py:478
  9.5 12.0 %collective-permute-start.15 = (f32[3,2,128,128]{3,2,1,0:T(8,128)S(1)}, f32[3,2,128,128]{3,2,1,0:T(8,128)S(1)}, u32[]{:S(2)}, u32[]{:S(2)}) collective-permute-start(f32[3,2,128,128]{3,2,1,0:T(8,128)S(1)} %get-tuple-element.65.refs_5_.refs_6_.refs_1_), channel_id=1, source_target_pairs={{0,16},{8,24},{16,0},{24,8},{1,17},{9,25},{17,1},{25,9},{2,18},{10... | collective-permute-start | bytes 1179656 | tf_op jit(solution)/shard_map/ppermute | solution.py:478
  11.0 18.9 %collective-permute-start.6 = (f32[3,2,128,128]{3,2,1,0:T(8,128)S(1)}, f32[3,2,128,128]{3,2,1,0:T(8,128)S(1)}, u32[]{:S(2)}, u32[]{:S(2)}) collective-permute-start(f32[3,2,128,128]{3,2,1,0:T(8,128)S(1)} %get-tuple-element.64.refs_4_.refs_5_.refs_0_), channel_id=1, source_target_pairs={{0,16},{8,24},{16,0},{24,8},{1,17},{9,25},{17,1},{25,9},{2,18},{10... | collective-permute-start | bytes 1179656 | tf_op jit(solution)/shard_map/ppermute | solution.py:478
  11.5 18.4 %collective-permute-start.5 = (f32[3,2,128,128]{3,2,1,0:T(8,128)S(1)}, f32[3,2,128,128]{3,2,1,0:T(8,128)S(1)}, u32[]{:S(2)}, u32[]{:S(2)}) collective-permute-start(f32[3,2,128,128]{3,2,1,0:T(8,128)S(1)} %get-tuple-element.65.refs_5_.refs_6_.refs_1_), channel_id=1, source_target_pairs={{0,8},{8,0},{16,24},{24,16},{1,9},{9,1},{17,25},{25,17},{2,10},{10... | collective-permute-start | bytes 1179656 | tf_op jit(solution)/shard_map/ppermute | solution.py:478
  11.8 11.3 %collective-permute-start.2 = (f32[128,256]{1,0:T(8,128)S(1)}, f32[128,256]{1,0:T(8,128)S(1)}, u32[]{:S(2)}, u32[]{:S(2)}) collective-permute-start(f32[128,256]{1,0:T(8,128)S(1)} %get-tuple-element.39), channel_id=1, source_target_pairs={{1,2},{2,1},{5,6},{6,5},{9,10},{10,9},{13,14},{14,13},{17,18},{18,... | collective-permute-start | bytes 393224 | tf_op jit(solution)/shard_map/ppermute | solution.py:544
  21.5 24.6 %collective-permute-start.16 = (f32[3,2,128,128]{3,2,1,0:T(8,128)S(1)}, f32[3,2,128,128]{3,2,1,0:T(8,128)S(1)}, u32[]{:S(2)}, u32[]{:S(2)}) collective-permute-start(f32[3,2,128,128]{3,2,1,0:T(8,128)S(1)} %collective-permute-done.14.refs_6_.refs_7_.refs_2_), channel_id=1, source_target_pairs={{0,16},{8,24},{16,0},{24,8},{1,17},{9,25},{17,1},{25,9},{2,18},{10... | collective-permute-start | bytes 1179656 | tf_op jit(solution)/shard_map/ppermute | solution.py:478
  23.1 8.6 %collective-permute-start.3 = (f32[128,256]{1,0:T(8,128)S(1)}, f32[128,256]{1,0:T(8,128)S(1)}, u32[]{:S(2)}, u32[]{:S(2)}) collective-permute-start(f32[128,256]{1,0:T(8,128)S(1)} %get-tuple-element.42), channel_id=1, source_target_pairs={{1,0},{2,3},{5,4},{6,7},{9,8},{10,11},{13,12},{14,15},{17,16},{18,... | collective-permute-start | bytes 393224 | tf_op jit(solution)/shard_map/ppermute | solution.py:552
  24.4 21.8 %collective-permute-start.17 = (f32[3,2,128,128]{3,2,1,0:T(8,128)S(1)}, f32[3,2,128,128]{3,2,1,0:T(8,128)S(1)}, u32[]{:S(2)}, u32[]{:S(2)}) collective-permute-start(f32[3,2,128,128]{3,2,1,0:T(8,128)S(1)} %collective-permute-done.15.refs_9_.refs_10_.refs_5_), channel_id=1, source_target_pairs={{0,8},{8,0},{16,24},{24,16},{1,9},{9,1},{17,25},{25,17},{2,10},{10... | collective-permute-start | bytes 1179656 | tf_op jit(solution)/shard_map/ppermute | solution.py:478
  32.8 9.2 %collective-permute-start.12 = (f32[3,128,128]{2,1,0:T(8,128)S(1)}, f32[3,128,128]{2,1,0:T(8,128)S(1)}, u32[]{:S(2)}, u32[]{:S(2)}) collective-permute-start(f32[3,128,128]{2,1,0:T(8,128)S(1)} %get-tuple-element.57.refs_0_), channel_id=1, source_target_pairs={{0,24},{8,16},{16,8},{24,0},{1,25},{9,17},{17,9},{25,1},{2,26},{10... | collective-permute-start | bytes 589832 | tf_op jit(solution)/shard_map/ppermute | solution.py:579
  35.3 10.3 %collective-permute-start.10 = (f32[3,128,128]{2,1,0:T(8,128)S(1)}, f32[3,128,128]{2,1,0:T(8,128)S(1)}, u32[]{:S(2)}, u32[]{:S(2)}) collective-permute-start(f32[3,128,128]{2,1,0:T(8,128)S(1)} %get-tuple-element.57.refs_0_), channel_id=1, source_target_pairs={{0,16},{8,24},{16,0},{24,8},{1,17},{9,25},{17,1},{25,9},{2,18},{10... | collective-permute-start | bytes 589832 | tf_op jit(solution)/shard_map/ppermute | solution.py:579
  35.9 9.8 %collective-permute-start.8 = (f32[3,128,128]{2,1,0:T(8,128)S(1)}, f32[3,128,128]{2,1,0:T(8,128)S(1)}, u32[]{:S(2)}, u32[]{:S(2)}) collective-permute-start(f32[3,128,128]{2,1,0:T(8,128)S(1)} %get-tuple-element.57.refs_0_), channel_id=1, source_target_pairs={{0,8},{8,0},{16,24},{24,16},{1,9},{9,1},{17,25},{25,17},{2,10},{10... | collective-permute-start | bytes 589832 | tf_op jit(solution)/shard_map/ppermute | solution.py:579
  42.0 5.0 %collective-permute-start.7 = (f32[3,128,128]{2,1,0:T(8,128)S(1)}, f32[3,128,128]{2,1,0:T(8,128)S(1)}, u32[]{:S(2)}, u32[]{:S(2)}) collective-permute-start(f32[3,128,128]{2,1,0:T(8,128)S(1)} %get-tuple-element.57.refs_0_), channel_id=1, source_target_pairs={{0,4},{4,0},{1,5},{5,1},{2,6},{6,2},{3,7},{7,3},{8,12},{12,8},{9,1... | collective-permute-start | bytes 589832 | tf_op jit(solution)/shard_map/ppermute | solution.py:582
  45.6 1.4 %collective-permute-start.13 = (f32[3,128,128]{2,1,0:T(8,128)S(1)}, f32[3,128,128]{2,1,0:T(8,128)S(1)}, u32[]{:S(2)}, u32[]{:S(2)}) collective-permute-start(f32[3,128,128]{2,1,0:T(8,128)S(1)} %collective-permute-done.12.refs_3_), channel_id=1, source_target_pairs={{0,4},{4,0},{1,5},{5,1},{2,6},{6,2},{3,7},{7,3},{8,12},{12,8},{9,1... | collective-permute-start | bytes 589832 | tf_op jit(solution)/shard_map/ppermute | solution.py:582
  45.6 1.7 %collective-permute-start.11 = (f32[3,128,128]{2,1,0:T(8,128)S(1)}, f32[3,128,128]{2,1,0:T(8,128)S(1)}, u32[]{:S(2)}, u32[]{:S(2)}) collective-permute-start(f32[3,128,128]{2,1,0:T(8,128)S(1)} %collective-permute-done.10.refs_2_), channel_id=1, source_target_pairs={{0,4},{4,0},{1,5},{5,1},{2,6},{6,2},{3,7},{7,3},{8,12},{12,8},{9,1... | collective-permute-start | bytes 589832 | tf_op jit(solution)/shard_map/ppermute | solution.py:582
  46.1 1.5 %collective-permute-start.9 = (f32[3,128,128]{2,1,0:T(8,128)S(1)}, f32[3,128,128]{2,1,0:T(8,128)S(1)}, u32[]{:S(2)}, u32[]{:S(2)}) collective-permute-start(f32[3,128,128]{2,1,0:T(8,128)S(1)} %collective-permute-done.8.refs_1_), channel_id=1, source_target_pairs={{0,4},{4,0},{1,5},{5,1},{2,6},{6,2},{3,7},{7,3},{8,12},{12,8},{9,1... | collective-permute-start | bytes 589832 | tf_op jit(solution)/shard_map/ppermute | solution.py:582
  48.1 1.8 %collective-permute-start.18 = (f32[3,2,128,128]{3,2,1,0:T(8,128)S(1)}, f32[3,2,128,128]{3,2,1,0:T(8,128)S(1)}, u32[]{:S(2)}, u32[]{:S(2)}) collective-permute-start(f32[3,2,128,128]{3,2,1,0:T(8,128)S(1)} %get-tuple-element.61), channel_id=1, source_target_pairs={{0,4},{4,0},{1,5},{5,1},{2,6},{6,2},{3,7},{7,3},{8,12},{12,8},{9,1... | collective-permute-start | bytes 1179656 | tf_op jit(solution)/shard_map/ppermute | solution.py:593

commit v3 on v2

--- a/solution.py
+++ b/solution.py
@@ -19,11 +19,11 @@
 STEPS_MAX = 60
 ROWS = 16
 WORK = 1
-WORK2 = 2
-WORK3 = 0.1
-WORK4 = 0.1
+WORK2 = 8
+WORK3 = 2
+WORK4 = 1
 WORK5 = 0.01
-WORK6 = 0.1
+WORK6 = 1
 
 
 def schedule():
@@ -458,7 +458,8 @@
 def screened_at(pieces, offset, kappa, k):
     if len(pieces) == 1:
         return pieces[0].at[kappa, k]
-    return pieces[2 * offset + k]
+    one, two, first, second, along_x, along_y = pieces
+    return ((one, two), (first, along_x.at[0]), (along_y.at[0], second), (along_y.at[1], along_x.at[1]))[offset][k]
 
 
 def join_kernel(axes, received, _, out, arrival):
@@ -483,15 +484,15 @@
         one, two = jnp.where(core == 0, own[0], got[1]), jnp.where(core == 0, got[0], own[1])
         if self.paired:
             self.along = [self.moved(one, 1), self.moved(two, 2)]
-            self.later = [self.moved(two, 1), self.moved(one, 2)]
-            self.pieces = [one, two, self.along[0], self.later[0], self.later[1], self.along[1]]
+            self.pair = [one, two]
         else:
             self.pieces = [lax.all_gather(jnp.stack([one, two]), "chip", axis=0)]
 
     def go_on(self, after):
         if self.paired:
-            first, second, _ = lax.optimization_barrier((*self.along, after))
-            self.pieces += [self.moved(first, 2), self.moved(second, 1)]
+            one, two, first, second, _ = lax.optimization_barrier((*self.pair, *self.along, after))
+            self.later = [self.moved(jnp.stack([two, second]), 1), self.moved(jnp.stack([one, first]), 2)]
+            self.pieces = [*self.pair, *self.along, *self.later]
 
 
 def local(axes, onsite, hopping, sigma_old, screened):
@@ -552,10 +553,9 @@
         arrived = lax.ppermute(message, "space", route)
         if upper is None:
             upper, lower, ready = call(
-                functools.partial(swapped, waiting_kernel, len(exchange.later)),
+                functools.partial(swapped, waiting_kernel, 0),
                 (matrix, matrix, jax.ShapeDtypeStruct((4, size, 2 * size), F32)),
-                *exchange.later, received, diagonal, u_in, u_out, outside, h, hd,
-                space=[pl.ANY] * len(exchange.later) + [pltpu.VMEM] * 7,
+                received, diagonal, u_in, u_out, outside, h, hd,
                 work=WORK4,
             )
         final = level == 0

time: 50.8 us -> 53.2 us (1.047); the launches traced: 50.6 us -> 52.5 us
  waiting for transfers between devices: 24.6 us -> 27 us
  starting transfers between devices: 15.6 us -> 14.9 us
    ppermute x1, waiting for transfers between devices: 1.14 us -> 7.21 us  [local(): arrived = lax.ppermute(message, 'space', route)]
    ppermute x6 -> x4, waiting for transfers between devices: 14 us -> 8.57 us  [moved(): return lax.ppermute(piece, 'chip', [(i, i ^ offset) for i in range(4)])]
    ppermute x3, waiting for transfers between devices: 8.41 us -> 10.5 us  [local(): lax.ppermute(packed, 'chip', [(i, i ^ offset) for i in range(chips)])]
    ppermute x6 -> x4, starting transfers between devices: 6.24 us -> 5.58 us  [moved(): return lax.ppermute(piece, 'chip', [(i, i ^ offset) for i in range(4)])]
  transfers between devices with their start and end apart: 19 -> 17, of which waited for: 9 -> 9; matrix products, arithmetic and copies ran while one was open for 0% -> 0% of each run, Pallas kernels for 16% -> 16%
where the time goes in v3:
time: 53.2 us; the launch traced here: 52.5 us
  waiting for transfers between devices  27 us (51%)
  starting transfers between devices  14.9 us (28%)
  Pallas kernels  9.56 us (18%)
  between operations  0.81 us (2%)
    ppermute x3, waiting for transfers between devices, local(): lax.ppermute(packed, 'chip', [(i, i ^ offset) for i in range(chips)])  10.5 us
    pallas_call x10, Pallas kernels, call(): pl.pallas_call(functools.partial(body, axes), out_shape=out_shape, in_spe...  9.56 us
    ppermute x4, waiting for transfers between devices, moved(): return lax.ppermute(piece, 'chip', [(i, i ^ offset) for i in range(4)])  8.57 us
    ppermute x1, waiting for transfers between devices, local(): arrived = lax.ppermute(message, 'space', route)  7.21 us
    ppermute x4, starting transfers between devices, moved(): return lax.ppermute(piece, 'chip', [(i, i ^ offset) for i in range(4)])  5.58 us
    ppermute x3, starting transfers between devices, local(): lax.ppermute(packed, 'chip', [(i, i ^ offset) for i in range(chips)])  3.55 us
    ppermute x1, starting transfers between devices, local(): received = lax.ppermute(message, 'space', route)  2.29 us
    ppermute x1, starting transfers between devices, local(): arrived = lax.ppermute(message, 'space', route)  1.29 us
  transfers between devices with their start and end apart: 17, of which 9 were waited for; matrix products, arithmetic and copies ran while one was open for 0% of the time, Pallas kernels for 16%

profile of v3, /device:TPU:0, one launch (start us, length us, event | category | flops | bytes accessed | tf_op | source)
XLA Modules:
  0.0 52.5 jit_solution(5806096581171104799)
XLA Ops:
  0.6 0.5 collective-permute-start.11
  1.2 3.8 %shard_map.59 = (f32[128,256]{1,0:T(8,128)S(1)}, f32[128,256]{1,0:T(8,128)S(1)}, f32[128,256]{1,0:T(8,128)S(1)}, f32[128,256]{1,0:T(8,128)S(1)}, f32[128,256]{1,0:T(8,128)S(1)}, /*index=5*/f32[8,128]{1,0:T(8,128)S(1)}) custom-call(f32[1,2,128,128]{3,2,1,0:T(8,128)} %onsite_far.1, f32[1,2,128,128]{3,2,1,0:T(8,128)} %hopping_far.1, ...), custom_call_target="tpu_custom_call" | custom-call | flops 1342177280 | bytes 2097152 | tf_op jit(solution)/shard_map/pallas_call | solution.py:506
  5.1 2.3 %collective-permute-start.1 = (f32[128,256]{1,0:T(8,128)S(1)}, f32[128,256]{1,0:T(8,128)S(1)}, u32[]{:S(2)}, u32[]{:S(2)}) collective-permute-start(f32[128,256]{1,0:T(8,128)S(1)} %get-tuple-element.36.arguments_4_), channel_id=1, source_target_pairs={{0,1},{3,2},{4,5},{7,6},{8,9},{11,10},{12,13},{15,14},{16,17},{19,... | collective-permute-start | bytes 393224 | tf_op jit(solution)/shard_map/ppermute | solution.py:536
  7.6 2.0 %collective-permute-start.13 = (f32[3,2,128,128]{3,2,1,0:T(8,128)S(1)}, f32[3,2,128,128]{3,2,1,0:T(8,128)S(1)}, u32[]{:S(2)}, u32[]{:S(2)}) collective-permute-start(f32[3,2,128,128]{3,2,1,0:T(8,128)S(1)} %get-tuple-element.60.refs_5_.refs_6_.refs_1_), channel_id=1, source_target_pairs={{0,16},{8,24},{16,0},{24,8},{1,17},{9,25},{17,1},{25,9},{2,18},{10... | collective-permute-start | bytes 1179656 | tf_op jit(solution)/shard_map/ppermute | solution.py:479
  9.5 1.5 %collective-permute-start.12 = (f32[3,2,128,128]{3,2,1,0:T(8,128)S(1)}, f32[3,2,128,128]{3,2,1,0:T(8,128)S(1)}, u32[]{:S(2)}, u32[]{:S(2)}) collective-permute-start(f32[3,2,128,128]{3,2,1,0:T(8,128)S(1)} %get-tuple-element.62.refs_4_.refs_5_.refs_0_), channel_id=1, source_target_pairs={{0,8},{8,0},{16,24},{24,16},{1,9},{9,1},{17,25},{25,17},{2,10},{10... | collective-permute-start | bytes 1179656 | tf_op jit(solution)/shard_map/ppermute | solution.py:479
  11.1 0.7 %collective-permute-start.2 = (f32[128,256]{1,0:T(8,128)S(1)}, f32[128,256]{1,0:T(8,128)S(1)}, u32[]{:S(2)}, u32[]{:S(2)}) collective-permute-start(f32[128,256]{1,0:T(8,128)S(1)} %get-tuple-element.41), channel_id=1, source_target_pairs={{1,2},{2,1},{5,6},{6,5},{9,10},{10,9},{13,14},{14,13},{17,18},{18,... | collective-permute-start | bytes 393224 | tf_op jit(solution)/shard_map/ppermute | solution.py:545
  11.8 7.1 %collective-permute-done.13.refs_7_.refs_8_.refs_3_ = f32[3,2,128,128]{3,2,1,0:T(8,128)S(1)} collective-permute-done((f32[3,2,128,128]{3,2,1,0:T(8,128)S(1)}, f32[3,2,128,128]{3,2,1,0:T(8,128)S(1)}, u32[]{:S(2)}, u32[]{:S(2)}) %collective-permute-start.13) | collective-permute-done | bytes 393248 | tf_op jit(solution)/shard_map/ppermute | solution.py:479
  18.9 1.5 %collective-permute-done.12.refs_6_.refs_7_.refs_2_ = f32[3,2,128,128]{3,2,1,0:T(8,128)S(1)} collective-permute-done((f32[3,2,128,128]{3,2,1,0:T(8,128)S(1)}, f32[3,2,128,128]{3,2,1,0:T(8,128)S(1)}, u32[]{:S(2)}, u32[]{:S(2)}) %collective-permute-start.12) | collective-permute-done | bytes 393248 | tf_op jit(solution)/shard_map/ppermute | solution.py:479
  20.9 1.7 %collective-permute-start.14 = (f32[2,3,2,128,128]{4,3,2,1,0:T(8,128)S(1)}, f32[2,3,2,128,128]{4,3,2,1,0:T(8,128)S(1)}, u32[]{:S(2)}, u32[]{:S(2)}) collective-permute-start(f32[2,3,2,128,128]{4,3,2,1,0:T(8,128)S(1)} %pad_maximum_fusion), channel_id=1, source_target_pairs={{0,8},{8,0},{16,24},{24,16},{1,9},{9,1},{17,25},{25,17},{2,10},{10... | collective-permute-start | bytes 2359304 | tf_op jit(solution)/shard_map/ppermute | solution.py:479
  22.6 1.3 %collective-permute-start.3 = (f32[128,256]{1,0:T(8,128)S(1)}, f32[128,256]{1,0:T(8,128)S(1)}, u32[]{:S(2)}, u32[]{:S(2)}) collective-permute-start(f32[128,256]{1,0:T(8,128)S(1)} %get-tuple-element.44), channel_id=1, source_target_pairs={{1,0},{2,3},{5,4},{6,7},{9,8},{10,11},{13,12},{14,15},{17,16},{18,... | collective-permute-start | bytes 393224 | tf_op jit(solution)/shard_map/ppermute | solution.py:553
  23.9 0.6 %shard_map.62 = (f32[128,256]{1,0:T(8,128)S(1)}, f32[128,256]{1,0:T(8,128)S(1)}, f32[4,128,256]{2,1,0:T(8,128)S(1)}) custom-call(f32[128,256]{1,0:T(8,128)S(1)} %collective-permute-done.2.received.arguments_0_, f32[128,256]{1,0:T(8,128)S(1)} %get-tuple-element.45.arguments_1_.arguments_2_, f32[128,256]{1,0:T(8,128)S(1)} %get-tuple-element.46.arguments_2_, ...), custom_call_target="tpu_custom_call" | custom-call | flops 1342177280 | bytes 2097152 | tf_op jit(solution)/shard_map/pallas_call | solution.py:506
  24.5 7.2 %collective-permute-done.3.arguments_0_ = f32[128,256]{1,0:T(8,128)S(1)} collective-permute-done((f32[128,256]{1,0:T(8,128)S(1)}, f32[128,256]{1,0:T(8,128)S(1)}, u32[]{:S(2)}, u32[]{:S(2)}) %collective-permute-start.3) | collective-permute-done | bytes 131104 | tf_op jit(solution)/shard_map/ppermute | solution.py:553
  31.7 1.2 %shard_map.63 = (f32[3,128,128]{2,1,0:T(8,128)S(1)}, f32[128,256]{1,0:T(8,128)S(1)}, f32[128,256]{1,0:T(8,128)S(1)}, f32[128,256]{1,0:T(8,128)S(1)}) custom-call(f32[128,256]{1,0:T(8,128)S(1)} %collective-permute-done.3.arguments_0_, f32[4,128,256]{2,1,0:T(8,128)S(1)} %get-tuple-element.49.arguments_1_, ...), custom_call_target="tpu_custom_call" | custom-call | flops 1342177280 | bytes 2097152 | tf_op jit(solution)/shard_map/pallas_call | solution.py:506
  32.9 2.4 %collective-permute-start.9 = (f32[3,128,128]{2,1,0:T(8,128)S(1)}, f32[3,128,128]{2,1,0:T(8,128)S(1)}, u32[]{:S(2)}, u32[]{:S(2)}) collective-permute-start(f32[3,128,128]{2,1,0:T(8,128)S(1)} %get-tuple-element.57.refs_0_), channel_id=1, source_target_pairs={{0,24},{8,16},{16,8},{24,0},{1,25},{9,17},{17,9},{25,1},{2,26},{10... | collective-permute-start | bytes 589832 | tf_op jit(solution)/shard_map/ppermute | solution.py:579
  35.3 0.5 collective-permute-start.7
  35.9 0.6 %collective-permute-start.5 = (f32[3,128,128]{2,1,0:T(8,128)S(1)}, f32[3,128,128]{2,1,0:T(8,128)S(1)}, u32[]{:S(2)}, u32[]{:S(2)}) collective-permute-start(f32[3,128,128]{2,1,0:T(8,128)S(1)} %get-tuple-element.57.refs_0_), channel_id=1, source_target_pairs={{0,8},{8,0},{16,24},{24,16},{1,9},{9,1},{17,25},{25,17},{2,10},{10... | collective-permute-start | bytes 589832 | tf_op jit(solution)/shard_map/ppermute | solution.py:579
  36.5 0.8 %shard_map.64 = f32[3,2,128,128]{3,2,1,0:T(8,128)} custom-call(f32[128,256]{1,0:T(8,128)S(1)} %get-tuple-element.53.diagonal, f32[128,256]{1,0:T(8,128)S(1)} %get-tuple-element.54.upper, f32[128,256]{1,0:T(8,128)S(1)} %get-tuple-element.55.lower), custom_call_target="tpu_custom_call" | custom-call | flops 1342177280 | bytes 2097152 | tf_op jit(solution)/shard_map/pallas_call | solution.py:506
  37.3 9.3 %collective-permute-done.9.refs_3_ = f32[3,128,128]{2,1,0:T(8,128)S(1)} collective-permute-done((f32[3,128,128]{2,1,0:T(8,128)S(1)}, f32[3,128,128]{2,1,0:T(8,128)S(1)}, u32[]{:S(2)}, u32[]{:S(2)}) %collective-permute-start.9) | collective-permute-done | bytes 196640 | tf_op jit(solution)/shard_map/ppermute | solution.py:579
  46.6 0.7 %collective-permute-done.7.refs_2_ = f32[3,128,128]{2,1,0:T(8,128)S(1)} collective-permute-done((f32[3,128,128]{2,1,0:T(8,128)S(1)}, f32[3,128,128]{2,1,0:T(8,128)S(1)}, u32[]{:S(2)}, u32[]{:S(2)}) %collective-permute-start.7) | collective-permute-done | bytes 196640 | tf_op jit(solution)/shard_map/ppermute | solution.py:579
  47.8 0.5 collective-permute-start.6
  48.2 0.8 %shard_map.65 = (f32[3,2,128,128]{3,2,1,0:T(8,128)S(1)}, f32[3,2,128,128]{3,2,1,0:T(8,128)S(1)}) custom-call(f32[3,128,128]{2,1,0:T(8,128)S(1)} %get-tuple-element.57.refs_0_, f32[3,128,128]{2,1,0:T(8,128)S(1)} %collective-permute-done.5.refs_1_, f32[3,128,128]{2,1,0:T(8,128)S(1)} %collective-permute-done.7.refs_2_, ...), custom_call_target="tpu_custom_call" | custom-call | flops 13421772 | bytes 2097152 | tf_op jit(solution)/shard_map/pallas_call | solution.py:506
  49.4 0.5 shard_map.66
  50.2 1.1 %shard_map.67._ = f32[2,3,2,128,128]{4,3,2,1,0:T(8,128)} custom-call(f32[5,3,2,128,128]{4,3,2,1,0:T(8,128)S(1)} %get-tuple-element.66.spectral, f32[3,2,128,128]{3,2,1,0:T(8,128)S(1)} %get-tuple-element.67.before, f32[3,2,128,128]{3,2,1,0:T(8,128)S(1)} %get-tuple-element.62.refs_4_.refs_5_.refs_0_, ...), custom_call_target="tpu_custom_call" | custom-call | flops 1342177280 | bytes 2097152 | tf_op jit(solution)/shard_map/pallas_call | solution.py:506
  51.7 0.8 %shard_map.68 = f32[2,3,2,128,128]{4,3,2,1,0:T(8,128)} custom-call(f32[3,2,128,128]{3,2,1,0:T(8,128)S(1)} %collective-permute-done.16.received, f32[2,3,2,128,128]{4,3,2,1,0:T(8,128)} %shard_map.67._), custom_call_target="tpu_custom_call", output_to_operand_aliasing={{}: (1, {})} | custom-call | flops 1342177280 | bytes 2097152 | tf_op jit(solution)/shard_map/pallas_call | solution.py:506
  (26 shorter events, 2.5 us)
Async XLA Ops:
  0.6 6.8 %copy-start = (f32[1,1,2,3,2,128,128]{6,5,4,3,2,1,0:T(8,128)S(1)}, f32[1,1,2,3,2,128,128]{6,5,4,3,2,1,0:T(8,128)}, u32[]{:S(2)}) copy-start(f32[1,1,2,3,2,128,128]{6,5,4,3,2,1,0:T(8,128)} %param.7) | copy-start | bytes 2359300
  0.6 6.8 %collective-permute-start.11 = (f32[2,3,2,128,128]{4,3,2,1,0:T(8,128)}, f32[2,3,2,128,128]{4,3,2,1,0:T(8,128)S(1)}, u32[]{:S(2)}, u32[]{:S(2)}) collective-permute-start(f32[2,3,2,128,128]{4,3,2,1,0:T(8,128)} %bitcast.15), channel_id=1, source_target_pairs={{0,4},{4,0},{1,5},{5,1},{2,6},{6,2},{3,7},{7,3},{8,12},{12,8},{9,1... | collective-permute-start | bytes 2359304 | tf_op jit(solution)/shard_map/ppermute | solution.py:475
  5.0 2.5 %collective-permute-start = (f32[8,128]{1,0:T(8,128)S(1)}, f32[8,128]{1,0:T(8,128)S(1)}, u32[]{:S(2)}, u32[]{:S(2)}) collective-permute-start(f32[8,128]{1,0:T(8,128)S(1)} %get-tuple-element.35), channel_id=1, source_target_pairs={{0,4},{4,0},{1,5},{5,1},{2,6},{6,2},{3,7},{7,3},{8,12},{12,8},{9,1... | collective-permute-start | bytes 12296 | tf_op jit(solution)/shard_map/ppermute | solution.py:531
  5.1 5.9 %collective-permute-start.1 = (f32[128,256]{1,0:T(8,128)S(1)}, f32[128,256]{1,0:T(8,128)S(1)}, u32[]{:S(2)}, u32[]{:S(2)}) collective-permute-start(f32[128,256]{1,0:T(8,128)S(1)} %get-tuple-element.36.arguments_4_), channel_id=1, source_target_pairs={{0,1},{3,2},{4,5},{7,6},{8,9},{11,10},{12,13},{15,14},{16,17},{19,... | collective-permute-start | bytes 393224 | tf_op jit(solution)/shard_map/ppermute | solution.py:536
  7.6 11.3 %collective-permute-start.13 = (f32[3,2,128,128]{3,2,1,0:T(8,128)S(1)}, f32[3,2,128,128]{3,2,1,0:T(8,128)S(1)}, u32[]{:S(2)}, u32[]{:S(2)}) collective-permute-start(f32[3,2,128,128]{3,2,1,0:T(8,128)S(1)} %get-tuple-element.60.refs_5_.refs_6_.refs_1_), channel_id=1, source_target_pairs={{0,16},{8,24},{16,0},{24,8},{1,17},{9,25},{17,1},{25,9},{2,18},{10... | collective-permute-start | bytes 1179656 | tf_op jit(solution)/shard_map/ppermute | solution.py:479
  9.5 10.8 %collective-permute-start.12 = (f32[3,2,128,128]{3,2,1,0:T(8,128)S(1)}, f32[3,2,128,128]{3,2,1,0:T(8,128)S(1)}, u32[]{:S(2)}, u32[]{:S(2)}) collective-permute-start(f32[3,2,128,128]{3,2,1,0:T(8,128)S(1)} %get-tuple-element.62.refs_4_.refs_5_.refs_0_), channel_id=1, source_target_pairs={{0,8},{8,0},{16,24},{24,16},{1,9},{9,1},{17,25},{25,17},{2,10},{10... | collective-permute-start | bytes 1179656 | tf_op jit(solution)/shard_map/ppermute | solution.py:479
  11.1 11.5 %collective-permute-start.2 = (f32[128,256]{1,0:T(8,128)S(1)}, f32[128,256]{1,0:T(8,128)S(1)}, u32[]{:S(2)}, u32[]{:S(2)}) collective-permute-start(f32[128,256]{1,0:T(8,128)S(1)} %get-tuple-element.41), channel_id=1, source_target_pairs={{1,2},{2,1},{5,6},{6,5},{9,10},{10,9},{13,14},{14,13},{17,18},{18,... | collective-permute-start | bytes 393224 | tf_op jit(solution)/shard_map/ppermute | solution.py:545
  20.4 27.4 %collective-permute-start.15 = (f32[2,3,2,128,128]{4,3,2,1,0:T(8,128)S(1)}, f32[2,3,2,128,128]{4,3,2,1,0:T(8,128)S(1)}, u32[]{:S(2)}, u32[]{:S(2)}) collective-permute-start(f32[2,3,2,128,128]{4,3,2,1,0:T(8,128)S(1)} %pad_maximum_fusion.1), channel_id=1, source_target_pairs={{0,16},{8,24},{16,0},{24,8},{1,17},{9,25},{17,1},{25,9},{2,18},{10... | collective-permute-start | bytes 2359304 | tf_op jit(solution)/shard_map/ppermute | solution.py:479
  20.9 27.4 %collective-permute-start.14 = (f32[2,3,2,128,128]{4,3,2,1,0:T(8,128)S(1)}, f32[2,3,2,128,128]{4,3,2,1,0:T(8,128)S(1)}, u32[]{:S(2)}, u32[]{:S(2)}) collective-permute-start(f32[2,3,2,128,128]{4,3,2,1,0:T(8,128)S(1)} %pad_maximum_fusion), channel_id=1, source_target_pairs={{0,8},{8,0},{16,24},{24,16},{1,9},{9,1},{17,25},{25,17},{2,10},{10... | collective-permute-start | bytes 2359304 | tf_op jit(solution)/shard_map/ppermute | solution.py:479
  22.6 9.1 %collective-permute-start.3 = (f32[128,256]{1,0:T(8,128)S(1)}, f32[128,256]{1,0:T(8,128)S(1)}, u32[]{:S(2)}, u32[]{:S(2)}) collective-permute-start(f32[128,256]{1,0:T(8,128)S(1)} %get-tuple-element.44), channel_id=1, source_target_pairs={{1,0},{2,3},{5,4},{6,7},{9,8},{10,11},{13,12},{14,15},{17,16},{18,... | collective-permute-start | bytes 393224 | tf_op jit(solution)/shard_map/ppermute | solution.py:553
  32.9 13.6 %collective-permute-start.9 = (f32[3,128,128]{2,1,0:T(8,128)S(1)}, f32[3,128,128]{2,1,0:T(8,128)S(1)}, u32[]{:S(2)}, u32[]{:S(2)}) collective-permute-start(f32[3,128,128]{2,1,0:T(8,128)S(1)} %get-tuple-element.57.refs_0_), channel_id=1, source_target_pairs={{0,24},{8,16},{16,8},{24,0},{1,25},{9,17},{17,9},{25,1},{2,26},{10... | collective-permute-start | bytes 589832 | tf_op jit(solution)/shard_map/ppermute | solution.py:579
  35.3 11.9 %collective-permute-start.7 = (f32[3,128,128]{2,1,0:T(8,128)S(1)}, f32[3,128,128]{2,1,0:T(8,128)S(1)}, u32[]{:S(2)}, u32[]{:S(2)}) collective-permute-start(f32[3,128,128]{2,1,0:T(8,128)S(1)} %get-tuple-element.57.refs_0_), channel_id=1, source_target_pairs={{0,16},{8,24},{16,0},{24,8},{1,17},{9,25},{17,1},{25,9},{2,18},{10... | collective-permute-start | bytes 589832 | tf_op jit(solution)/shard_map/ppermute | solution.py:579
  35.9 11.9 %collective-permute-start.5 = (f32[3,128,128]{2,1,0:T(8,128)S(1)}, f32[3,128,128]{2,1,0:T(8,128)S(1)}, u32[]{:S(2)}, u32[]{:S(2)}) collective-permute-start(f32[3,128,128]{2,1,0:T(8,128)S(1)} %get-tuple-element.57.refs_0_), channel_id=1, source_target_pairs={{0,8},{8,0},{16,24},{24,16},{1,9},{9,1},{17,25},{25,17},{2,10},{10... | collective-permute-start | bytes 589832 | tf_op jit(solution)/shard_map/ppermute | solution.py:579
  46.6 2.5 %collective-permute-start.4 = (f32[3,128,128]{2,1,0:T(8,128)S(1)}, f32[3,128,128]{2,1,0:T(8,128)S(1)}, u32[]{:S(2)}, u32[]{:S(2)}) collective-permute-start(f32[3,128,128]{2,1,0:T(8,128)S(1)} %get-tuple-element.57.refs_0_), channel_id=1, source_target_pairs={{0,4},{4,0},{1,5},{5,1},{2,6},{6,2},{3,7},{7,3},{8,12},{12,8},{9,1... | collective-permute-start | bytes 589832 | tf_op jit(solution)/shard_map/ppermute | solution.py:582
  47.3 1.8 %collective-permute-start.10 = (f32[3,128,128]{2,1,0:T(8,128)S(1)}, f32[3,128,128]{2,1,0:T(8,128)S(1)}, u32[]{:S(2)}, u32[]{:S(2)}) collective-permute-start(f32[3,128,128]{2,1,0:T(8,128)S(1)} %collective-permute-done.9.refs_3_), channel_id=1, source_target_pairs={{0,4},{4,0},{1,5},{5,1},{2,6},{6,2},{3,7},{7,3},{8,12},{12,8},{9,1... | collective-permute-start | bytes 589832 | tf_op jit(solution)/shard_map/ppermute | solution.py:582
  47.7 1.4 %collective-permute-start.8 = (f32[3,128,128]{2,1,0:T(8,128)S(1)}, f32[3,128,128]{2,1,0:T(8,128)S(1)}, u32[]{:S(2)}, u32[]{:S(2)}) collective-permute-start(f32[3,128,128]{2,1,0:T(8,128)S(1)} %collective-permute-done.7.refs_2_), channel_id=1, source_target_pairs={{0,4},{4,0},{1,5},{5,1},{2,6},{6,2},{3,7},{7,3},{8,12},{12,8},{9,1... | collective-permute-start | bytes 589832 | tf_op jit(solution)/shard_map/ppermute | solution.py:582
  47.8 1.7 %collective-permute-start.6 = (f32[3,128,128]{2,1,0:T(8,128)S(1)}, f32[3,128,128]{2,1,0:T(8,128)S(1)}, u32[]{:S(2)}, u32[]{:S(2)}) collective-permute-start(f32[3,128,128]{2,1,0:T(8,128)S(1)} %collective-permute-done.5.refs_1_), channel_id=1, source_target_pairs={{0,4},{4,0},{1,5},{5,1},{2,6},{6,2},{3,7},{7,3},{8,12},{12,8},{9,1... | collective-permute-start | bytes 589832 | tf_op jit(solution)/shard_map/ppermute | solution.py:582
  49.9 1.8 %collective-permute-start.16 = (f32[3,2,128,128]{3,2,1,0:T(8,128)S(1)}, f32[3,2,128,128]{3,2,1,0:T(8,128)S(1)}, u32[]{:S(2)}, u32[]{:S(2)}) collective-permute-start(f32[3,2,128,128]{3,2,1,0:T(8,128)S(1)} %get-tuple-element.65), channel_id=1, source_target_pairs={{0,4},{4,0},{1,5},{5,1},{2,6},{6,2},{3,7},{7,3},{8,12},{12,8},{9,1... | collective-permute-start | bytes 1179656 | tf_op jit(solution)/shard_map/ppermute | solution.py:593

commit v4 on v2

--- a/solution.py
+++ b/solution.py
@@ -270,8 +270,7 @@
         message_ref[...] = jnp.zeros_like(message_ref)
 
 
-def waiting_kernel(axes, waited, *refs):
-    received, diagonal, u_in, u_out, outside, h, hd, upper_ref, lower_ref, ready_ref = refs[waited:]
+def waiting_kernel(axes, received, diagonal, u_in, u_out, outside, h, hd, upper_ref, lower_ref, ready_ref):
     position, depth, left = place(axes)
     energy = energy_point(axes)
     magnitude = energy * energy + BROADEN * BROADEN
@@ -310,7 +309,11 @@
         lower_ref[...] = jnp.zeros_like(lower_ref)
 
 
-def outward_kernel(axes, level, final, received, ready, diagonal, upper, lower, h, hd, *outputs):
+def outward_kernel(axes, level, final, waited, *refs):
+    outward(axes, level, final, *refs[waited:])
+
+
+def outward(axes, level, final, received, ready, diagonal, upper, lower, h, hd, *outputs):
     _, depth, left = place(axes)
     if final:
         packed_ref, green_ref, upper_ref, lower_ref = outputs
@@ -552,18 +555,18 @@
         arrived = lax.ppermute(message, "space", route)
         if upper is None:
             upper, lower, ready = call(
-                functools.partial(swapped, waiting_kernel, len(exchange.later)),
+                waiting_kernel,
                 (matrix, matrix, jax.ShapeDtypeStruct((4, size, 2 * size), F32)),
-                *exchange.later, received, diagonal, u_in, u_out, outside, h, hd,
-                space=[pl.ANY] * len(exchange.later) + [pltpu.VMEM] * 7,
+                received, diagonal, u_in, u_out, outside, h, hd,
                 work=WORK4,
             )
         final = level == 0
         shapes = (jax.ShapeDtypeStruct((3, size, size), F32) if final else matrix,) + (matrix,) * 3
         results = call(
-            functools.partial(swapped, outward_kernel, level, final),
+            functools.partial(swapped, outward_kernel, level, final, len(exchange.later)),
             shapes,
-            arrived, ready, diagonal, upper, lower, h, hd,
+            *exchange.later, arrived, ready, diagonal, upper, lower, h, hd,
+            space=[pl.ANY] * len(exchange.later) + [pltpu.VMEM] * 7,
             work=WORK6,
         )
         message, diagonal, upper, lower = results

time: 50.8 us -> 51.1 us (level)
    ppermute x6, waiting for transfers between devices: 14 us -> 9.16 us  [moved(): return lax.ppermute(piece, 'chip', [(i, i ^ offset) for i in range(4)])]
    ppermute x1, waiting for transfers between devices: 1.14 us -> 5.93 us  [local(): arrived = lax.ppermute(message, 'space', route)]
    ppermute x3, waiting for transfers between devices: 8.41 us -> 8.98 us  [local(): lax.ppermute(packed, 'chip', [(i, i ^ offset) for i in range(chips)])]
  transfers between devices with their start and end apart: 19 -> 19, of which waited for: 9 -> 8; matrix products, arithmetic and copies ran while one was open for 0% -> 0% of each run, Pallas kernels for 16% -> 16%
where the time goes in v4:
time: 51.1 us; the launch traced here: 51.2 us
  waiting for transfers between devices  25 us (49%)
  starting transfers between devices  15.7 us (31%)
  Pallas kernels  9.56 us (19%)
  between operations  0.79 us (2%)
    pallas_call x10, Pallas kernels, call(): pl.pallas_call(functools.partial(body, axes), out_shape=out_shape, in_spe...  9.56 us
    ppermute x6, waiting for transfers between devices, moved(): return lax.ppermute(piece, 'chip', [(i, i ^ offset) for i in range(4)])  9.16 us
    ppermute x3, waiting for transfers between devices, local(): lax.ppermute(packed, 'chip', [(i, i ^ offset) for i in range(chips)])  8.98 us
    ppermute x6, starting transfers between devices, moved(): return lax.ppermute(piece, 'chip', [(i, i ^ offset) for i in range(4)])  6.32 us
    ppermute x1, waiting for transfers between devices, local(): arrived = lax.ppermute(message, 'space', route)  5.93 us
    ppermute x3, starting transfers between devices, local(): lax.ppermute(packed, 'chip', [(i, i ^ offset) for i in range(chips)])  3.55 us
    ppermute x1, starting transfers between devices, local(): received = lax.ppermute(message, 'space', route)  2.29 us
    ppermute x1, starting transfers between devices, local(): arrived = lax.ppermute(message, 'space', route)  1.29 us
  transfers between devices with their start and end apart: 19, of which 8 were waited for; matrix products, arithmetic and copies ran while one was open for 0% of the time, Pallas kernels for 16%

profile of v4, /device:TPU:0, one launch (start us, length us, event | category | flops | bytes accessed | tf_op | source)
XLA Modules:
  0.0 51.2 jit_solution(11408185419954779201)
XLA Ops:
  0.6 0.5 %collective-permute-start = (f32[2,3,2,128,128]{4,3,2,1,0:T(8,128)}, f32[2,3,2,128,128]{4,3,2,1,0:T(8,128)S(1)}, u32[]{:S(2)}, u32[]{:S(2)}) collective-permute-start(f32[2,3,2,128,128]{4,3,2,1,0:T(8,128)} %bitcast.7), channel_id=1, source_target_pairs={{0,4},{4,0},{1,5},{5,1},{2,6},{6,2},{3,7},{7,3},{8,12},{12,8},{9,1... | collective-permute-start | bytes 2359304 | tf_op jit(solution)/shard_map/ppermute | solution.py:477
  1.2 3.8 %shard_map.59 = (f32[128,256]{1,0:T(8,128)S(1)}, f32[128,256]{1,0:T(8,128)S(1)}, f32[128,256]{1,0:T(8,128)S(1)}, f32[128,256]{1,0:T(8,128)S(1)}, f32[128,256]{1,0:T(8,128)S(1)}, /*index=5*/f32[8,128]{1,0:T(8,128)S(1)}) custom-call(f32[1,2,128,128]{3,2,1,0:T(8,128)} %onsite_far.1, f32[1,2,128,128]{3,2,1,0:T(8,128)} %hopping_far.1, ...), custom_call_target="tpu_custom_call" | custom-call | flops 1342177280 | bytes 2097152 | tf_op jit(solution)/shard_map/pallas_call | solution.py:508
  5.1 2.3 %collective-permute-start.4 = (f32[128,256]{1,0:T(8,128)S(1)}, f32[128,256]{1,0:T(8,128)S(1)}, u32[]{:S(2)}, u32[]{:S(2)}) collective-permute-start(f32[128,256]{1,0:T(8,128)S(1)} %get-tuple-element.36.arguments_4_), channel_id=1, source_target_pairs={{0,1},{3,2},{4,5},{7,6},{8,9},{11,10},{12,13},{15,14},{16,17},{19,... | collective-permute-start | bytes 393224 | tf_op jit(solution)/shard_map/ppermute | solution.py:538
  7.6 2.6 %collective-permute-start.14 = (f32[3,2,128,128]{3,2,1,0:T(8,128)S(1)}, f32[3,2,128,128]{3,2,1,0:T(8,128)S(1)}, u32[]{:S(2)}, u32[]{:S(2)}) collective-permute-start(f32[3,2,128,128]{3,2,1,0:T(8,128)S(1)} %get-tuple-element.64.refs_4_.refs_5_.refs_0_), channel_id=1, source_target_pairs={{0,8},{8,0},{16,24},{24,16},{1,9},{9,1},{17,25},{25,17},{2,10},{10... | collective-permute-start | bytes 1179656 | tf_op jit(solution)/shard_map/ppermute | solution.py:481
  10.1 0.9 %collective-permute-start.15 = (f32[3,2,128,128]{3,2,1,0:T(8,128)S(1)}, f32[3,2,128,128]{3,2,1,0:T(8,128)S(1)}, u32[]{:S(2)}, u32[]{:S(2)}) collective-permute-start(f32[3,2,128,128]{3,2,1,0:T(8,128)S(1)} %get-tuple-element.65.refs_5_.refs_6_.refs_1_), channel_id=1, source_target_pairs={{0,16},{8,24},{16,0},{24,8},{1,17},{9,25},{17,1},{25,9},{2,18},{10... | collective-permute-start | bytes 1179656 | tf_op jit(solution)/shard_map/ppermute | solution.py:481
  11.0 1.1 %collective-permute-start.3 = (f32[3,2,128,128]{3,2,1,0:T(8,128)S(1)}, f32[3,2,128,128]{3,2,1,0:T(8,128)S(1)}, u32[]{:S(2)}, u32[]{:S(2)}) collective-permute-start(f32[3,2,128,128]{3,2,1,0:T(8,128)S(1)} %get-tuple-element.64.refs_4_.refs_5_.refs_0_), channel_id=1, source_target_pairs={{0,16},{8,24},{16,0},{24,8},{1,17},{9,25},{17,1},{25,9},{2,18},{10... | collective-permute-start | bytes 1179656 | tf_op jit(solution)/shard_map/ppermute | solution.py:481
  12.3 0.7 %collective-permute-start.5 = (f32[128,256]{1,0:T(8,128)S(1)}, f32[128,256]{1,0:T(8,128)S(1)}, u32[]{:S(2)}, u32[]{:S(2)}) collective-permute-start(f32[128,256]{1,0:T(8,128)S(1)} %get-tuple-element.41), channel_id=1, source_target_pairs={{1,2},{2,1},{5,6},{6,5},{9,10},{10,9},{13,14},{14,13},{17,18},{18,... | collective-permute-start | bytes 393224 | tf_op jit(solution)/shard_map/ppermute | solution.py:547
  13.0 7.0 %collective-permute-done.14.refs_6_.refs_7_.refs_2_ = f32[3,2,128,128]{3,2,1,0:T(8,128)S(1)} collective-permute-done((f32[3,2,128,128]{3,2,1,0:T(8,128)S(1)}, f32[3,2,128,128]{3,2,1,0:T(8,128)S(1)}, u32[]{:S(2)}, u32[]{:S(2)}) %collective-permute-start.14) | collective-permute-done | bytes 393248 | tf_op jit(solution)/shard_map/ppermute | solution.py:481
  20.0 2.1 %collective-permute-done.15.refs_9_.refs_10_.refs_5_ = f32[3,2,128,128]{3,2,1,0:T(8,128)S(1)} collective-permute-done((f32[3,2,128,128]{3,2,1,0:T(8,128)S(1)}, f32[3,2,128,128]{3,2,1,0:T(8,128)S(1)}, u32[]{:S(2)}, u32[]{:S(2)}) %collective-permute-start.15) | collective-permute-done | bytes 393248 | tf_op jit(solution)/shard_map/ppermute | solution.py:481
  22.1 0.9 %collective-permute-start.16 = (f32[3,2,128,128]{3,2,1,0:T(8,128)S(1)}, f32[3,2,128,128]{3,2,1,0:T(8,128)S(1)}, u32[]{:S(2)}, u32[]{:S(2)}) collective-permute-start(f32[3,2,128,128]{3,2,1,0:T(8,128)S(1)} %collective-permute-done.14.refs_6_.refs_7_.refs_2_), channel_id=1, source_target_pairs={{0,16},{8,24},{16,0},{24,8},{1,17},{9,25},{17,1},{25,9},{2,18},{10... | collective-permute-start | bytes 1179656 | tf_op jit(solution)/shard_map/ppermute | solution.py:481
  23.1 1.3 %collective-permute-start.6 = (f32[128,256]{1,0:T(8,128)S(1)}, f32[128,256]{1,0:T(8,128)S(1)}, u32[]{:S(2)}, u32[]{:S(2)}) collective-permute-start(f32[128,256]{1,0:T(8,128)S(1)} %get-tuple-element.44), channel_id=1, source_target_pairs={{1,0},{2,3},{5,4},{6,7},{9,8},{10,11},{13,12},{14,15},{17,16},{18,... | collective-permute-start | bytes 393224 | tf_op jit(solution)/shard_map/ppermute | solution.py:555
  24.4 0.6 %shard_map.62 = (f32[128,256]{1,0:T(8,128)S(1)}, f32[128,256]{1,0:T(8,128)S(1)}, f32[4,128,256]{2,1,0:T(8,128)S(1)}) custom-call(f32[128,256]{1,0:T(8,128)S(1)} %collective-permute-done.5.received, f32[128,256]{1,0:T(8,128)S(1)} %get-tuple-element.45.diagonal.arguments_4_, f32[128,256]{1,0:T(8,128)S(1)} %get-tuple-element.46.u_in, ...), custom_call_target="tpu_custom_call" | custom-call | flops 134217728 | bytes 2097152 | tf_op jit(solution)/shard_map/pallas_call | solution.py:508
  24.9 0.8 %collective-permute-start.17 = (f32[3,2,128,128]{3,2,1,0:T(8,128)S(1)}, f32[3,2,128,128]{3,2,1,0:T(8,128)S(1)}, u32[]{:S(2)}, u32[]{:S(2)}) collective-permute-start(f32[3,2,128,128]{3,2,1,0:T(8,128)S(1)} %collective-permute-done.15.refs_9_.refs_10_.refs_5_), channel_id=1, source_target_pairs={{0,8},{8,0},{16,24},{24,16},{1,9},{9,1},{17,25},{25,17},{2,10},{10... | collective-permute-start | bytes 1179656 | tf_op jit(solution)/shard_map/ppermute | solution.py:481
  25.7 5.9 %collective-permute-done.6.arguments_2_ = f32[128,256]{1,0:T(8,128)S(1)} collective-permute-done((f32[128,256]{1,0:T(8,128)S(1)}, f32[128,256]{1,0:T(8,128)S(1)}, u32[]{:S(2)}, u32[]{:S(2)}) %collective-permute-start.6) | collective-permute-done | bytes 131104 | tf_op jit(solution)/shard_map/ppermute | solution.py:555
  31.6 1.2 %shard_map.63 = (f32[3,128,128]{2,1,0:T(8,128)S(1)}, f32[128,256]{1,0:T(8,128)S(1)}, f32[128,256]{1,0:T(8,128)S(1)}, f32[128,256]{1,0:T(8,128)S(1)}) custom-call(f32[3,2,128,128]{3,2,1,0:T(8,128)S(1)} %collective-permute-done.2.arguments_0_.refs_7_.refs_8_.refs_3_, f32[3,2,128,128]{3,2,1,0:T(8,128)S(1)} %collective-permute-done.3.arguments_1_.refs_8_.refs_9_.refs_4_, ...), custom_call_target="tpu_custom_call" | custom-call | flops 134217728 | bytes 2097152 | tf_op jit(solution)/shard_map/pallas_call | solution.py:508
  32.8 2.5 %collective-permute-start.12 = (f32[3,128,128]{2,1,0:T(8,128)S(1)}, f32[3,128,128]{2,1,0:T(8,128)S(1)}, u32[]{:S(2)}, u32[]{:S(2)}) collective-permute-start(f32[3,128,128]{2,1,0:T(8,128)S(1)} %get-tuple-element.57.refs_0_), channel_id=1, source_target_pairs={{0,24},{8,16},{16,8},{24,0},{1,25},{9,17},{17,9},{25,1},{2,26},{10... | collective-permute-start | bytes 589832 | tf_op jit(solution)/shard_map/ppermute | solution.py:582
  35.9 0.5 %collective-permute-start.8 = (f32[3,128,128]{2,1,0:T(8,128)S(1)}, f32[3,128,128]{2,1,0:T(8,128)S(1)}, u32[]{:S(2)}, u32[]{:S(2)}) collective-permute-start(f32[3,128,128]{2,1,0:T(8,128)S(1)} %get-tuple-element.57.refs_0_), channel_id=1, source_target_pairs={{0,8},{8,0},{16,24},{24,16},{1,9},{9,1},{17,25},{25,17},{2,10},{10... | collective-permute-start | bytes 589832 | tf_op jit(solution)/shard_map/ppermute | solution.py:582
  36.4 0.8 %shard_map.64 = f32[3,2,128,128]{3,2,1,0:T(8,128)} custom-call(f32[128,256]{1,0:T(8,128)S(1)} %get-tuple-element.53.diagonal, f32[128,256]{1,0:T(8,128)S(1)} %get-tuple-element.54.upper, f32[128,256]{1,0:T(8,128)S(1)} %get-tuple-element.55.lower), custom_call_target="tpu_custom_call" | custom-call | flops 1342177280 | bytes 2097152 | tf_op jit(solution)/shard_map/pallas_call | solution.py:508
  37.2 5.0 %collective-permute-done.12.refs_3_ = f32[3,128,128]{2,1,0:T(8,128)S(1)} collective-permute-done((f32[3,128,128]{2,1,0:T(8,128)S(1)}, f32[3,128,128]{2,1,0:T(8,128)S(1)}, u32[]{:S(2)}, u32[]{:S(2)}) %collective-permute-start.12) | collective-permute-done | bytes 196640 | tf_op jit(solution)/shard_map/ppermute | solution.py:582
  42.2 4.0 %collective-permute-done.10.refs_2_ = f32[3,128,128]{2,1,0:T(8,128)S(1)} collective-permute-done((f32[3,128,128]{2,1,0:T(8,128)S(1)}, f32[3,128,128]{2,1,0:T(8,128)S(1)}, u32[]{:S(2)}, u32[]{:S(2)}) %collective-permute-start.10) | collective-permute-done | bytes 196640 | tf_op jit(solution)/shard_map/ppermute | solution.py:582
  46.2 0.5 collective-permute-start.11
  46.8 0.8 %shard_map.65 = (f32[3,2,128,128]{3,2,1,0:T(8,128)S(1)}, f32[3,2,128,128]{3,2,1,0:T(8,128)S(1)}) custom-call(f32[3,128,128]{2,1,0:T(8,128)S(1)} %get-tuple-element.57.refs_0_, f32[3,128,128]{2,1,0:T(8,128)S(1)} %collective-permute-done.8.refs_1_, f32[3,128,128]{2,1,0:T(8,128)S(1)} %collective-permute-done.10.refs_2_, ...), custom_call_target="tpu_custom_call" | custom-call | flops 13421772 | bytes 2097152 | tf_op jit(solution)/shard_map/pallas_call | solution.py:508
  49.0 1.1 %shard_map.67._ = f32[2,3,2,128,128]{4,3,2,1,0:T(8,128)} custom-call(f32[5,3,2,128,128]{4,3,2,1,0:T(8,128)S(1)} %get-tuple-element.62.spectral, f32[3,2,128,128]{3,2,1,0:T(8,128)S(1)} %get-tuple-element.63.before, f32[3,2,128,128]{3,2,1,0:T(8,128)S(1)} %get-tuple-element.64.refs_4_.refs_5_.refs_0_, ...), custom_call_target="tpu_custom_call" | custom-call | flops 1342177280 | bytes 2097152 | tf_op jit(solution)/shard_map/pallas_call | solution.py:508
  50.4 0.8 %shard_map.68 = f32[2,3,2,128,128]{4,3,2,1,0:T(8,128)} custom-call(f32[3,2,128,128]{3,2,1,0:T(8,128)S(1)} %collective-permute-done.18.received, f32[2,3,2,128,128]{4,3,2,1,0:T(8,128)} %shard_map.67._), custom_call_target="tpu_custom_call", output_to_operand_aliasing={{}: (1, {})} | custom-call | flops 1342177280 | bytes 2097152 | tf_op jit(solution)/shard_map/pallas_call | solution.py:508
  (28 shorter events, 2.8 us)
Async XLA Ops:
  0.6 6.8 %copy-start = (f32[1,1,2,3,2,128,128]{6,5,4,3,2,1,0:T(8,128)S(1)}, f32[1,1,2,3,2,128,128]{6,5,4,3,2,1,0:T(8,128)}, u32[]{:S(2)}) copy-start(f32[1,1,2,3,2,128,128]{6,5,4,3,2,1,0:T(8,128)} %param.7) | copy-start | bytes 2359300
  0.6 6.8 %collective-permute-start = (f32[2,3,2,128,128]{4,3,2,1,0:T(8,128)}, f32[2,3,2,128,128]{4,3,2,1,0:T(8,128)S(1)}, u32[]{:S(2)}, u32[]{:S(2)}) collective-permute-start(f32[2,3,2,128,128]{4,3,2,1,0:T(8,128)} %bitcast.7), channel_id=1, source_target_pairs={{0,4},{4,0},{1,5},{5,1},{2,6},{6,2},{3,7},{7,3},{8,12},{12,8},{9,1... | collective-permute-start | bytes 2359304 | tf_op jit(solution)/shard_map/ppermute | solution.py:477
  5.0 2.5 %collective-permute-start.1 = (f32[8,128]{1,0:T(8,128)S(1)}, f32[8,128]{1,0:T(8,128)S(1)}, u32[]{:S(2)}, u32[]{:S(2)}) collective-permute-start(f32[8,128]{1,0:T(8,128)S(1)} %get-tuple-element.33), channel_id=1, source_target_pairs={{0,4},{4,0},{1,5},{5,1},{2,6},{6,2},{3,7},{7,3},{8,12},{12,8},{9,1... | collective-permute-start | bytes 12296 | tf_op jit(solution)/shard_map/ppermute | solution.py:533
  5.1 7.1 %collective-permute-start.4 = (f32[128,256]{1,0:T(8,128)S(1)}, f32[128,256]{1,0:T(8,128)S(1)}, u32[]{:S(2)}, u32[]{:S(2)}) collective-permute-start(f32[128,256]{1,0:T(8,128)S(1)} %get-tuple-element.36.arguments_4_), channel_id=1, source_target_pairs={{0,1},{3,2},{4,5},{7,6},{8,9},{11,10},{12,13},{15,14},{16,17},{19,... | collective-permute-start | bytes 393224 | tf_op jit(solution)/shard_map/ppermute | solution.py:538
  7.6 12.5 %collective-permute-start.14 = (f32[3,2,128,128]{3,2,1,0:T(8,128)S(1)}, f32[3,2,128,128]{3,2,1,0:T(8,128)S(1)}, u32[]{:S(2)}, u32[]{:S(2)}) collective-permute-start(f32[3,2,128,128]{3,2,1,0:T(8,128)S(1)} %get-tuple-element.64.refs_4_.refs_5_.refs_0_), channel_id=1, source_target_pairs={{0,8},{8,0},{16,24},{24,16},{1,9},{9,1},{17,25},{25,17},{2,10},{10... | collective-permute-start | bytes 1179656 | tf_op jit(solution)/shard_map/ppermute | solution.py:481
  10.1 12.0 %collective-permute-start.15 = (f32[3,2,128,128]{3,2,1,0:T(8,128)S(1)}, f32[3,2,128,128]{3,2,1,0:T(8,128)S(1)}, u32[]{:S(2)}, u32[]{:S(2)}) collective-permute-start(f32[3,2,128,128]{3,2,1,0:T(8,128)S(1)} %get-tuple-element.65.refs_5_.refs_6_.refs_1_), channel_id=1, source_target_pairs={{0,16},{8,24},{16,0},{24,8},{1,17},{9,25},{17,1},{25,9},{2,18},{10... | collective-permute-start | bytes 1179656 | tf_op jit(solution)/shard_map/ppermute | solution.py:481
  11.0 20.6 %collective-permute-start.3 = (f32[3,2,128,128]{3,2,1,0:T(8,128)S(1)}, f32[3,2,128,128]{3,2,1,0:T(8,128)S(1)}, u32[]{:S(2)}, u32[]{:S(2)}) collective-permute-start(f32[3,2,128,128]{3,2,1,0:T(8,128)S(1)} %get-tuple-element.64.refs_4_.refs_5_.refs_0_), channel_id=1, source_target_pairs={{0,16},{8,24},{16,0},{24,8},{1,17},{9,25},{17,1},{25,9},{2,18},{10... | collective-permute-start | bytes 1179656 | tf_op jit(solution)/shard_map/ppermute | solution.py:481
  12.2 19.5 %collective-permute-start.2 = (f32[3,2,128,128]{3,2,1,0:T(8,128)S(1)}, f32[3,2,128,128]{3,2,1,0:T(8,128)S(1)}, u32[]{:S(2)}, u32[]{:S(2)}) collective-permute-start(f32[3,2,128,128]{3,2,1,0:T(8,128)S(1)} %get-tuple-element.65.refs_5_.refs_6_.refs_1_), channel_id=1, source_target_pairs={{0,8},{8,0},{16,24},{24,16},{1,9},{9,1},{17,25},{25,17},{2,10},{10... | collective-permute-start | bytes 1179656 | tf_op jit(solution)/shard_map/ppermute | solution.py:481
  12.3 10.7 %collective-permute-start.5 = (f32[128,256]{1,0:T(8,128)S(1)}, f32[128,256]{1,0:T(8,128)S(1)}, u32[]{:S(2)}, u32[]{:S(2)}) collective-permute-start(f32[128,256]{1,0:T(8,128)S(1)} %get-tuple-element.41), channel_id=1, source_target_pairs={{1,2},{2,1},{5,6},{6,5},{9,10},{10,9},{13,14},{14,13},{17,18},{18,... | collective-permute-start | bytes 393224 | tf_op jit(solution)/shard_map/ppermute | solution.py:547
  22.1 24.5 %collective-permute-start.16 = (f32[3,2,128,128]{3,2,1,0:T(8,128)S(1)}, f32[3,2,128,128]{3,2,1,0:T(8,128)S(1)}, u32[]{:S(2)}, u32[]{:S(2)}) collective-permute-start(f32[3,2,128,128]{3,2,1,0:T(8,128)S(1)} %collective-permute-done.14.refs_6_.refs_7_.refs_2_), channel_id=1, source_target_pairs={{0,16},{8,24},{16,0},{24,8},{1,17},{9,25},{17,1},{25,9},{2,18},{10... | collective-permute-start | bytes 1179656 | tf_op jit(solution)/shard_map/ppermute | solution.py:481
  23.1 8.6 %collective-permute-start.6 = (f32[128,256]{1,0:T(8,128)S(1)}, f32[128,256]{1,0:T(8,128)S(1)}, u32[]{:S(2)}, u32[]{:S(2)}) collective-permute-start(f32[128,256]{1,0:T(8,128)S(1)} %get-tuple-element.44), channel_id=1, source_target_pairs={{1,0},{2,3},{5,4},{6,7},{9,8},{10,11},{13,12},{14,15},{17,16},{18,... | collective-permute-start | bytes 393224 | tf_op jit(solution)/shard_map/ppermute | solution.py:555
  24.9 21.8 %collective-permute-start.17 = (f32[3,2,128,128]{3,2,1,0:T(8,128)S(1)}, f32[3,2,128,128]{3,2,1,0:T(8,128)S(1)}, u32[]{:S(2)}, u32[]{:S(2)}) collective-permute-start(f32[3,2,128,128]{3,2,1,0:T(8,128)S(1)} %collective-permute-done.15.refs_9_.refs_10_.refs_5_), channel_id=1, source_target_pairs={{0,8},{8,0},{16,24},{24,16},{1,9},{9,1},{17,25},{25,17},{2,10},{10... | collective-permute-start | bytes 1179656 | tf_op jit(solution)/shard_map/ppermute | solution.py:481
  32.8 9.4 %collective-permute-start.12 = (f32[3,128,128]{2,1,0:T(8,128)S(1)}, f32[3,128,128]{2,1,0:T(8,128)S(1)}, u32[]{:S(2)}, u32[]{:S(2)}) collective-permute-start(f32[3,128,128]{2,1,0:T(8,128)S(1)} %get-tuple-element.57.refs_0_), channel_id=1, source_target_pairs={{0,24},{8,16},{16,8},{24,0},{1,25},{9,17},{17,9},{25,1},{2,26},{10... | collective-permute-start | bytes 589832 | tf_op jit(solution)/shard_map/ppermute | solution.py:582
  35.4 10.8 %collective-permute-start.10 = (f32[3,128,128]{2,1,0:T(8,128)S(1)}, f32[3,128,128]{2,1,0:T(8,128)S(1)}, u32[]{:S(2)}, u32[]{:S(2)}) collective-permute-start(f32[3,128,128]{2,1,0:T(8,128)S(1)} %get-tuple-element.57.refs_0_), channel_id=1, source_target_pairs={{0,16},{8,24},{16,0},{24,8},{1,17},{9,25},{17,1},{25,9},{2,18},{10... | collective-permute-start | bytes 589832 | tf_op jit(solution)/shard_map/ppermute | solution.py:582
  35.9 10.3 %collective-permute-start.8 = (f32[3,128,128]{2,1,0:T(8,128)S(1)}, f32[3,128,128]{2,1,0:T(8,128)S(1)}, u32[]{:S(2)}, u32[]{:S(2)}) collective-permute-start(f32[3,128,128]{2,1,0:T(8,128)S(1)} %get-tuple-element.57.refs_0_), channel_id=1, source_target_pairs={{0,8},{8,0},{16,24},{24,16},{1,9},{9,1},{17,25},{25,17},{2,10},{10... | collective-permute-start | bytes 589832 | tf_op jit(solution)/shard_map/ppermute | solution.py:582
  42.2 5.4 %collective-permute-start.7 = (f32[3,128,128]{2,1,0:T(8,128)S(1)}, f32[3,128,128]{2,1,0:T(8,128)S(1)}, u32[]{:S(2)}, u32[]{:S(2)}) collective-permute-start(f32[3,128,128]{2,1,0:T(8,128)S(1)} %get-tuple-element.57.refs_0_), channel_id=1, source_target_pairs={{0,4},{4,0},{1,5},{5,1},{2,6},{6,2},{3,7},{7,3},{8,12},{12,8},{9,1... | collective-permute-start | bytes 589832 | tf_op jit(solution)/shard_map/ppermute | solution.py:585
  46.2 1.4 %collective-permute-start.13 = (f32[3,128,128]{2,1,0:T(8,128)S(1)}, f32[3,128,128]{2,1,0:T(8,128)S(1)}, u32[]{:S(2)}, u32[]{:S(2)}) collective-permute-start(f32[3,128,128]{2,1,0:T(8,128)S(1)} %collective-permute-done.12.refs_3_), channel_id=1, source_target_pairs={{0,4},{4,0},{1,5},{5,1},{2,6},{6,2},{3,7},{7,3},{8,12},{12,8},{9,1... | collective-permute-start | bytes 589832 | tf_op jit(solution)/shard_map/ppermute | solution.py:585
  46.2 1.7 %collective-permute-start.11 = (f32[3,128,128]{2,1,0:T(8,128)S(1)}, f32[3,128,128]{2,1,0:T(8,128)S(1)}, u32[]{:S(2)}, u32[]{:S(2)}) collective-permute-start(f32[3,128,128]{2,1,0:T(8,128)S(1)} %collective-permute-done.10.refs_2_), channel_id=1, source_target_pairs={{0,4},{4,0},{1,5},{5,1},{2,6},{6,2},{3,7},{7,3},{8,12},{12,8},{9,1... | collective-permute-start | bytes 589832 | tf_op jit(solution)/shard_map/ppermute | solution.py:585
  46.7 1.5 %collective-permute-start.9 = (f32[3,128,128]{2,1,0:T(8,128)S(1)}, f32[3,128,128]{2,1,0:T(8,128)S(1)}, u32[]{:S(2)}, u32[]{:S(2)}) collective-permute-start(f32[3,128,128]{2,1,0:T(8,128)S(1)} %collective-permute-done.8.refs_1_), channel_id=1, source_target_pairs={{0,4},{4,0},{1,5},{5,1},{2,6},{6,2},{3,7},{7,3},{8,12},{12,8},{9,1... | collective-permute-start | bytes 589832 | tf_op jit(solution)/shard_map/ppermute | solution.py:585
  48.7 1.8 %collective-permute-start.18 = (f32[3,2,128,128]{3,2,1,0:T(8,128)S(1)}, f32[3,2,128,128]{3,2,1,0:T(8,128)S(1)}, u32[]{:S(2)}, u32[]{:S(2)}) collective-permute-start(f32[3,2,128,128]{3,2,1,0:T(8,128)S(1)} %get-tuple-element.61), channel_id=1, source_target_pairs={{0,4},{4,0},{1,5},{5,1},{2,6},{6,2},{3,7},{7,3},{8,12},{12,8},{9,1... | collective-permute-start | bytes 1179656 | tf_op jit(solution)/shard_map/ppermute | solution.py:596

commit v5 on v4

--- a/solution.py
+++ b/solution.py
@@ -493,7 +493,8 @@
 
     def go_on(self, after):
         if self.paired:
-            first, second, _ = lax.optimization_barrier((*self.along, after))
+            first, _ = lax.optimization_barrier((self.along[0], after))
+            second, _ = lax.optimization_barrier((self.along[1], after))
             self.pieces += [self.moved(first, 2), self.moved(second, 1)]
 
 

time: 51.1 us -> 52.1 us (1.020)
  starting transfers between devices: 15.7 us -> 16.5 us
    ppermute x6, waiting for transfers between devices: 9.16 us -> 13.7 us  [moved(): return lax.ppermute(piece, 'chip', [(i, i ^ offset) for i in range(4)])]
    ppermute x1, waiting for transfers between devices: 5.93 us -> 1.57 us  [local(): arrived = lax.ppermute(message, 'space', route)]
where the time goes in v5:
time: 52.1 us; the launch traced here: 51.9 us
  waiting for transfers between devices  25 us (48%)
  starting transfers between devices  16.5 us (32%)
  Pallas kernels  9.56 us (18%)
  between operations  0.8 us (2%)
    ppermute x6, waiting for transfers between devices, moved(): return lax.ppermute(piece, 'chip', [(i, i ^ offset) for i in range(4)])  13.7 us
    pallas_call x10, Pallas kernels, call(): pl.pallas_call(functools.partial(body, axes), out_shape=out_shape, in_spe...  9.56 us
    ppermute x3, waiting for transfers between devices, local(): lax.ppermute(packed, 'chip', [(i, i ^ offset) for i in range(chips)])  8.95 us
    ppermute x6, starting transfers between devices, moved(): return lax.ppermute(piece, 'chip', [(i, i ^ offset) for i in range(4)])  6.16 us
    ppermute x3, starting transfers between devices, local(): lax.ppermute(packed, 'chip', [(i, i ^ offset) for i in range(chips)])  4.05 us
    ppermute x1, starting transfers between devices, local(): received = lax.ppermute(message, 'space', route)  2.29 us
    ppermute x1, waiting for transfers between devices, local(): arrived = lax.ppermute(message, 'space', route)  1.57 us
    ppermute x1, starting transfers between devices, local(): arrived = lax.ppermute(message, 'space', route)  1.29 us
  transfers between devices with their start and end apart: 19, of which 8 were waited for; matrix products, arithmetic and copies ran while one was open for 0% of the time, Pallas kernels for 16%

profile of v5, /device:TPU:0, one launch (start us, length us, event | category | flops | bytes accessed | tf_op | source)
XLA Modules:
  0.0 51.9 jit_solution(17122058918417187893)
XLA Ops:
  0.6 0.5 collective-permute-start
  1.2 3.8 %shard_map.59 = (f32[128,256]{1,0:T(8,128)S(1)}, f32[128,256]{1,0:T(8,128)S(1)}, f32[128,256]{1,0:T(8,128)S(1)}, f32[128,256]{1,0:T(8,128)S(1)}, f32[128,256]{1,0:T(8,128)S(1)}, /*index=5*/f32[8,128]{1,0:T(8,128)S(1)}) custom-call(f32[1,2,128,128]{3,2,1,0:T(8,128)} %onsite_far.1, f32[1,2,128,128]{3,2,1,0:T(8,128)} %hopping_far.1, ...), custom_call_target="tpu_custom_call" | custom-call | flops 1342177280 | bytes 2097152 | tf_op jit(solution)/shard_map/pallas_call | solution.py:509
  5.1 2.3 %collective-permute-start.4 = (f32[128,256]{1,0:T(8,128)S(1)}, f32[128,256]{1,0:T(8,128)S(1)}, u32[]{:S(2)}, u32[]{:S(2)}) collective-permute-start(f32[128,256]{1,0:T(8,128)S(1)} %get-tuple-element.36.arguments_4_), channel_id=1, source_target_pairs={{0,1},{3,2},{4,5},{7,6},{8,9},{11,10},{12,13},{15,14},{16,17},{19,... | collective-permute-start | bytes 393224 | tf_op jit(solution)/shard_map/ppermute | solution.py:539
  7.6 1.9 %collective-permute-start.14 = (f32[3,2,128,128]{3,2,1,0:T(8,128)S(1)}, f32[3,2,128,128]{3,2,1,0:T(8,128)S(1)}, u32[]{:S(2)}, u32[]{:S(2)}) collective-permute-start(f32[3,2,128,128]{3,2,1,0:T(8,128)S(1)} %get-tuple-element.64.refs_4_.refs_5_.refs_0_), channel_id=1, source_target_pairs={{0,8},{8,0},{16,24},{24,16},{1,9},{9,1},{17,25},{25,17},{2,10},{10... | collective-permute-start | bytes 1179656 | tf_op jit(solution)/shard_map/ppermute | solution.py:481
  9.5 1.5 %collective-permute-start.3 = (f32[3,2,128,128]{3,2,1,0:T(8,128)S(1)}, f32[3,2,128,128]{3,2,1,0:T(8,128)S(1)}, u32[]{:S(2)}, u32[]{:S(2)}) collective-permute-start(f32[3,2,128,128]{3,2,1,0:T(8,128)S(1)} %get-tuple-element.64.refs_4_.refs_5_.refs_0_), channel_id=1, source_target_pairs={{0,16},{8,24},{16,0},{24,8},{1,17},{9,25},{17,1},{25,9},{2,18},{10... | collective-permute-start | bytes 1179656 | tf_op jit(solution)/shard_map/ppermute | solution.py:481
  11.0 0.5 collective-permute-start.15
  11.8 0.7 %collective-permute-start.5 = (f32[128,256]{1,0:T(8,128)S(1)}, f32[128,256]{1,0:T(8,128)S(1)}, u32[]{:S(2)}, u32[]{:S(2)}) collective-permute-start(f32[128,256]{1,0:T(8,128)S(1)} %get-tuple-element.41), channel_id=1, source_target_pairs={{1,2},{2,1},{5,6},{6,5},{9,10},{10,9},{13,14},{14,13},{17,18},{18,... | collective-permute-start | bytes 393224 | tf_op jit(solution)/shard_map/ppermute | solution.py:548
  12.4 7.1 %collective-permute-done.14.refs_6_.refs_7_.refs_2_ = f32[3,2,128,128]{3,2,1,0:T(8,128)S(1)} collective-permute-done((f32[3,2,128,128]{3,2,1,0:T(8,128)S(1)}, f32[3,2,128,128]{3,2,1,0:T(8,128)S(1)}, u32[]{:S(2)}, u32[]{:S(2)}) %collective-permute-start.14) | collective-permute-done | bytes 393248 | tf_op jit(solution)/shard_map/ppermute | solution.py:481
  19.6 1.9 %collective-permute-start.16 = (f32[3,2,128,128]{3,2,1,0:T(8,128)S(1)}, f32[3,2,128,128]{3,2,1,0:T(8,128)S(1)}, u32[]{:S(2)}, u32[]{:S(2)}) collective-permute-start(f32[3,2,128,128]{3,2,1,0:T(8,128)S(1)} %collective-permute-done.14.refs_6_.refs_7_.refs_2_), channel_id=1, source_target_pairs={{0,16},{8,24},{16,0},{24,8},{1,17},{9,25},{17,1},{25,9},{2,18},{10... | collective-permute-start | bytes 1179656 | tf_op jit(solution)/shard_map/ppermute | solution.py:481
  21.5 1.3 %collective-permute-start.6 = (f32[128,256]{1,0:T(8,128)S(1)}, f32[128,256]{1,0:T(8,128)S(1)}, u32[]{:S(2)}, u32[]{:S(2)}) collective-permute-start(f32[128,256]{1,0:T(8,128)S(1)} %get-tuple-element.44), channel_id=1, source_target_pairs={{1,0},{2,3},{5,4},{6,7},{9,8},{10,11},{13,12},{14,15},{17,16},{18,... | collective-permute-start | bytes 393224 | tf_op jit(solution)/shard_map/ppermute | solution.py:556
  22.8 0.6 %shard_map.62 = (f32[128,256]{1,0:T(8,128)S(1)}, f32[128,256]{1,0:T(8,128)S(1)}, f32[4,128,256]{2,1,0:T(8,128)S(1)}) custom-call(f32[128,256]{1,0:T(8,128)S(1)} %collective-permute-done.5.received, f32[128,256]{1,0:T(8,128)S(1)} %get-tuple-element.45.diagonal.arguments_4_, f32[128,256]{1,0:T(8,128)S(1)} %get-tuple-element.46.u_in, ...), custom_call_target="tpu_custom_call" | custom-call | flops 134217728 | bytes 2097152 | tf_op jit(solution)/shard_map/pallas_call | solution.py:509
  23.4 6.5 %collective-permute-done.15.refs_9_.refs_10_.refs_5_ = f32[3,2,128,128]{3,2,1,0:T(8,128)S(1)} collective-permute-done((f32[3,2,128,128]{3,2,1,0:T(8,128)S(1)}, f32[3,2,128,128]{3,2,1,0:T(8,128)S(1)}, u32[]{:S(2)}, u32[]{:S(2)}) %collective-permute-start.15) | collective-permute-done | bytes 393248 | tf_op jit(solution)/shard_map/ppermute | solution.py:481
  30.1 1.6 %collective-permute-done.6.arguments_2_ = f32[128,256]{1,0:T(8,128)S(1)} collective-permute-done((f32[128,256]{1,0:T(8,128)S(1)}, f32[128,256]{1,0:T(8,128)S(1)}, u32[]{:S(2)}, u32[]{:S(2)}) %collective-permute-start.6) | collective-permute-done | bytes 131104 | tf_op jit(solution)/shard_map/ppermute | solution.py:556
  31.6 1.2 %shard_map.63 = (f32[3,128,128]{2,1,0:T(8,128)S(1)}, f32[128,256]{1,0:T(8,128)S(1)}, f32[128,256]{1,0:T(8,128)S(1)}, f32[128,256]{1,0:T(8,128)S(1)}) custom-call(f32[3,2,128,128]{3,2,1,0:T(8,128)S(1)} %collective-permute-done.2.arguments_0_.refs_7_.refs_8_.refs_3_, f32[3,2,128,128]{3,2,1,0:T(8,128)S(1)} %collective-permute-done.3.arguments_1_.refs_8_.refs_9_.refs_4_, ...), custom_call_target="tpu_custom_call" | custom-call | flops 134217728 | bytes 2097152 | tf_op jit(solution)/shard_map/pallas_call | solution.py:509
  32.8 2.5 %collective-permute-start.12 = (f32[3,128,128]{2,1,0:T(8,128)S(1)}, f32[3,128,128]{2,1,0:T(8,128)S(1)}, u32[]{:S(2)}, u32[]{:S(2)}) collective-permute-start(f32[3,128,128]{2,1,0:T(8,128)S(1)} %get-tuple-element.57.refs_0_), channel_id=1, source_target_pairs={{0,24},{8,16},{16,8},{24,0},{1,25},{9,17},{17,9},{25,1},{2,26},{10... | collective-permute-start | bytes 589832 | tf_op jit(solution)/shard_map/ppermute | solution.py:583
  35.4 1.5 %collective-permute-start.10 = (f32[3,128,128]{2,1,0:T(8,128)S(1)}, f32[3,128,128]{2,1,0:T(8,128)S(1)}, u32[]{:S(2)}, u32[]{:S(2)}) collective-permute-start(f32[3,128,128]{2,1,0:T(8,128)S(1)} %get-tuple-element.57.refs_0_), channel_id=1, source_target_pairs={{0,16},{8,24},{16,0},{24,8},{1,17},{9,25},{17,1},{25,9},{2,18},{10... | collective-permute-start | bytes 589832 | tf_op jit(solution)/shard_map/ppermute | solution.py:583
  36.9 0.8 %shard_map.64 = f32[3,2,128,128]{3,2,1,0:T(8,128)} custom-call(f32[128,256]{1,0:T(8,128)S(1)} %get-tuple-element.53.diagonal, f32[128,256]{1,0:T(8,128)S(1)} %get-tuple-element.54.upper, f32[128,256]{1,0:T(8,128)S(1)} %get-tuple-element.55.lower), custom_call_target="tpu_custom_call" | custom-call | flops 1342177280 | bytes 2097152 | tf_op jit(solution)/shard_map/pallas_call | solution.py:509
  37.7 8.3 %collective-permute-done.12.refs_3_ = f32[3,128,128]{2,1,0:T(8,128)S(1)} collective-permute-done((f32[3,128,128]{2,1,0:T(8,128)S(1)}, f32[3,128,128]{2,1,0:T(8,128)S(1)}, u32[]{:S(2)}, u32[]{:S(2)}) %collective-permute-start.12) | collective-permute-done | bytes 196640 | tf_op jit(solution)/shard_map/ppermute | solution.py:583
  46.0 0.5 collective-permute-start.13
  46.5 0.7 %collective-permute-done.8.refs_1_ = f32[3,128,128]{2,1,0:T(8,128)S(1)} collective-permute-done((f32[3,128,128]{2,1,0:T(8,128)S(1)}, f32[3,128,128]{2,1,0:T(8,128)S(1)}, u32[]{:S(2)}, u32[]{:S(2)}) %collective-permute-start.8) | collective-permute-done | bytes 196640 | tf_op jit(solution)/shard_map/ppermute | solution.py:583
  47.2 0.5 collective-permute-start.9
  47.7 0.8 %shard_map.65 = (f32[3,2,128,128]{3,2,1,0:T(8,128)S(1)}, f32[3,2,128,128]{3,2,1,0:T(8,128)S(1)}) custom-call(f32[3,128,128]{2,1,0:T(8,128)S(1)} %get-tuple-element.57.refs_0_, f32[3,128,128]{2,1,0:T(8,128)S(1)} %collective-permute-done.8.refs_1_, f32[3,128,128]{2,1,0:T(8,128)S(1)} %collective-permute-done.10.refs_2_, ...), custom_call_target="tpu_custom_call" | custom-call | flops 13421772 | bytes 2097152 | tf_op jit(solution)/shard_map/pallas_call | solution.py:509
  49.7 1.1 %shard_map.67._ = f32[2,3,2,128,128]{4,3,2,1,0:T(8,128)} custom-call(f32[5,3,2,128,128]{4,3,2,1,0:T(8,128)S(1)} %get-tuple-element.62.spectral, f32[3,2,128,128]{3,2,1,0:T(8,128)S(1)} %get-tuple-element.63.before, f32[3,2,128,128]{3,2,1,0:T(8,128)S(1)} %get-tuple-element.64.refs_4_.refs_5_.refs_0_, ...), custom_call_target="tpu_custom_call" | custom-call | flops 1342177280 | bytes 2097152 | tf_op jit(solution)/shard_map/pallas_call | solution.py:509
  51.1 0.8 %shard_map.68 = f32[2,3,2,128,128]{4,3,2,1,0:T(8,128)} custom-call(f32[3,2,128,128]{3,2,1,0:T(8,128)S(1)} %collective-permute-done.18.received, f32[2,3,2,128,128]{4,3,2,1,0:T(8,128)} %shard_map.67._), custom_call_target="tpu_custom_call", output_to_operand_aliasing={{}: (1, {})} | custom-call | flops 1342177280 | bytes 2097152 | tf_op jit(solution)/shard_map/pallas_call | solution.py:509
  (28 shorter events, 2.2 us)
Async XLA Ops:
  0.6 6.8 %copy-start = (f32[1,1,2,3,2,128,128]{6,5,4,3,2,1,0:T(8,128)S(1)}, f32[1,1,2,3,2,128,128]{6,5,4,3,2,1,0:T(8,128)}, u32[]{:S(2)}) copy-start(f32[1,1,2,3,2,128,128]{6,5,4,3,2,1,0:T(8,128)} %param.7) | copy-start | bytes 2359300
  0.6 6.8 %collective-permute-start = (f32[2,3,2,128,128]{4,3,2,1,0:T(8,128)}, f32[2,3,2,128,128]{4,3,2,1,0:T(8,128)S(1)}, u32[]{:S(2)}, u32[]{:S(2)}) collective-permute-start(f32[2,3,2,128,128]{4,3,2,1,0:T(8,128)} %bitcast.7), channel_id=1, source_target_pairs={{0,4},{4,0},{1,5},{5,1},{2,6},{6,2},{3,7},{7,3},{8,12},{12,8},{9,1... | collective-permute-start | bytes 2359304 | tf_op jit(solution)/shard_map/ppermute | solution.py:477
  5.0 2.5 %collective-permute-start.1 = (f32[8,128]{1,0:T(8,128)S(1)}, f32[8,128]{1,0:T(8,128)S(1)}, u32[]{:S(2)}, u32[]{:S(2)}) collective-permute-start(f32[8,128]{1,0:T(8,128)S(1)} %get-tuple-element.33), channel_id=1, source_target_pairs={{0,4},{4,0},{1,5},{5,1},{2,6},{6,2},{3,7},{7,3},{8,12},{12,8},{9,1... | collective-permute-start | bytes 12296 | tf_op jit(solution)/shard_map/ppermute | solution.py:534
  5.1 6.5 %collective-permute-start.4 = (f32[128,256]{1,0:T(8,128)S(1)}, f32[128,256]{1,0:T(8,128)S(1)}, u32[]{:S(2)}, u32[]{:S(2)}) collective-permute-start(f32[128,256]{1,0:T(8,128)S(1)} %get-tuple-element.36.arguments_4_), channel_id=1, source_target_pairs={{0,1},{3,2},{4,5},{7,6},{8,9},{11,10},{12,13},{15,14},{16,17},{19,... | collective-permute-start | bytes 393224 | tf_op jit(solution)/shard_map/ppermute | solution.py:539
  7.6 12.0 %collective-permute-start.14 = (f32[3,2,128,128]{3,2,1,0:T(8,128)S(1)}, f32[3,2,128,128]{3,2,1,0:T(8,128)S(1)}, u32[]{:S(2)}, u32[]{:S(2)}) collective-permute-start(f32[3,2,128,128]{3,2,1,0:T(8,128)S(1)} %get-tuple-element.64.refs_4_.refs_5_.refs_0_), channel_id=1, source_target_pairs={{0,8},{8,0},{16,24},{24,16},{1,9},{9,1},{17,25},{25,17},{2,10},{10... | collective-permute-start | bytes 1179656 | tf_op jit(solution)/shard_map/ppermute | solution.py:481
  9.5 22.1 %collective-permute-start.3 = (f32[3,2,128,128]{3,2,1,0:T(8,128)S(1)}, f32[3,2,128,128]{3,2,1,0:T(8,128)S(1)}, u32[]{:S(2)}, u32[]{:S(2)}) collective-permute-start(f32[3,2,128,128]{3,2,1,0:T(8,128)S(1)} %get-tuple-element.64.refs_4_.refs_5_.refs_0_), channel_id=1, source_target_pairs={{0,16},{8,24},{16,0},{24,8},{1,17},{9,25},{17,1},{25,9},{2,18},{10... | collective-permute-start | bytes 1179656 | tf_op jit(solution)/shard_map/ppermute | solution.py:481
  11.0 18.9 %collective-permute-start.15 = (f32[3,2,128,128]{3,2,1,0:T(8,128)S(1)}, f32[3,2,128,128]{3,2,1,0:T(8,128)S(1)}, u32[]{:S(2)}, u32[]{:S(2)}) collective-permute-start(f32[3,2,128,128]{3,2,1,0:T(8,128)S(1)} %get-tuple-element.65.refs_5_.refs_6_.refs_1_), channel_id=1, source_target_pairs={{0,16},{8,24},{16,0},{24,8},{1,17},{9,25},{17,1},{25,9},{2,18},{10... | collective-permute-start | bytes 1179656 | tf_op jit(solution)/shard_map/ppermute | solution.py:481
  11.5 20.1 %collective-permute-start.2 = (f32[3,2,128,128]{3,2,1,0:T(8,128)S(1)}, f32[3,2,128,128]{3,2,1,0:T(8,128)S(1)}, u32[]{:S(2)}, u32[]{:S(2)}) collective-permute-start(f32[3,2,128,128]{3,2,1,0:T(8,128)S(1)} %get-tuple-element.65.refs_5_.refs_6_.refs_1_), channel_id=1, source_target_pairs={{0,8},{8,0},{16,24},{24,16},{1,9},{9,1},{17,25},{25,17},{2,10},{10... | collective-permute-start | bytes 1179656 | tf_op jit(solution)/shard_map/ppermute | solution.py:481
  11.8 9.7 %collective-permute-start.5 = (f32[128,256]{1,0:T(8,128)S(1)}, f32[128,256]{1,0:T(8,128)S(1)}, u32[]{:S(2)}, u32[]{:S(2)}) collective-permute-start(f32[128,256]{1,0:T(8,128)S(1)} %get-tuple-element.41), channel_id=1, source_target_pairs={{1,2},{2,1},{5,6},{6,5},{9,10},{10,9},{13,14},{14,13},{17,18},{18,... | collective-permute-start | bytes 393224 | tf_op jit(solution)/shard_map/ppermute | solution.py:548
  19.6 27.6 %collective-permute-start.16 = (f32[3,2,128,128]{3,2,1,0:T(8,128)S(1)}, f32[3,2,128,128]{3,2,1,0:T(8,128)S(1)}, u32[]{:S(2)}, u32[]{:S(2)}) collective-permute-start(f32[3,2,128,128]{3,2,1,0:T(8,128)S(1)} %collective-permute-done.14.refs_6_.refs_7_.refs_2_), channel_id=1, source_target_pairs={{0,16},{8,24},{16,0},{24,8},{1,17},{9,25},{17,1},{25,9},{2,18},{10... | collective-permute-start | bytes 1179656 | tf_op jit(solution)/shard_map/ppermute | solution.py:481
  21.5 10.1 %collective-permute-start.6 = (f32[128,256]{1,0:T(8,128)S(1)}, f32[128,256]{1,0:T(8,128)S(1)}, u32[]{:S(2)}, u32[]{:S(2)}) collective-permute-start(f32[128,256]{1,0:T(8,128)S(1)} %get-tuple-element.44), channel_id=1, source_target_pairs={{1,0},{2,3},{5,4},{6,7},{9,8},{10,11},{13,12},{14,15},{17,16},{18,... | collective-permute-start | bytes 393224 | tf_op jit(solution)/shard_map/ppermute | solution.py:556
  29.9 17.7 %collective-permute-start.17 = (f32[3,2,128,128]{3,2,1,0:T(8,128)S(1)}, f32[3,2,128,128]{3,2,1,0:T(8,128)S(1)}, u32[]{:S(2)}, u32[]{:S(2)}) collective-permute-start(f32[3,2,128,128]{3,2,1,0:T(8,128)S(1)} %collective-permute-done.15.refs_9_.refs_10_.refs_5_), channel_id=1, source_target_pairs={{0,8},{8,0},{16,24},{24,16},{1,9},{9,1},{17,25},{25,17},{2,10},{10... | collective-permute-start | bytes 1179656 | tf_op jit(solution)/shard_map/ppermute | solution.py:481
  32.8 13.1 %collective-permute-start.12 = (f32[3,128,128]{2,1,0:T(8,128)S(1)}, f32[3,128,128]{2,1,0:T(8,128)S(1)}, u32[]{:S(2)}, u32[]{:S(2)}) collective-permute-start(f32[3,128,128]{2,1,0:T(8,128)S(1)} %get-tuple-element.57.refs_0_), channel_id=1, source_target_pairs={{0,24},{8,16},{16,8},{24,0},{1,25},{9,17},{17,9},{25,1},{2,26},{10... | collective-permute-start | bytes 589832 | tf_op jit(solution)/shard_map/ppermute | solution.py:583
  35.4 10.6 %collective-permute-start.10 = (f32[3,128,128]{2,1,0:T(8,128)S(1)}, f32[3,128,128]{2,1,0:T(8,128)S(1)}, u32[]{:S(2)}, u32[]{:S(2)}) collective-permute-start(f32[3,128,128]{2,1,0:T(8,128)S(1)} %get-tuple-element.57.refs_0_), channel_id=1, source_target_pairs={{0,16},{8,24},{16,0},{24,8},{1,17},{9,25},{17,1},{25,9},{2,18},{10... | collective-permute-start | bytes 589832 | tf_op jit(solution)/shard_map/ppermute | solution.py:583
  36.9 10.3 %collective-permute-start.8 = (f32[3,128,128]{2,1,0:T(8,128)S(1)}, f32[3,128,128]{2,1,0:T(8,128)S(1)}, u32[]{:S(2)}, u32[]{:S(2)}) collective-permute-start(f32[3,128,128]{2,1,0:T(8,128)S(1)} %get-tuple-element.57.refs_0_), channel_id=1, source_target_pairs={{0,8},{8,0},{16,24},{24,16},{1,9},{9,1},{17,25},{25,17},{2,10},{10... | collective-permute-start | bytes 589832 | tf_op jit(solution)/shard_map/ppermute | solution.py:583
  46.0 2.5 %collective-permute-start.7 = (f32[3,128,128]{2,1,0:T(8,128)S(1)}, f32[3,128,128]{2,1,0:T(8,128)S(1)}, u32[]{:S(2)}, u32[]{:S(2)}) collective-permute-start(f32[3,128,128]{2,1,0:T(8,128)S(1)} %get-tuple-element.57.refs_0_), channel_id=1, source_target_pairs={{0,4},{4,0},{1,5},{5,1},{2,6},{6,2},{3,7},{7,3},{8,12},{12,8},{9,1... | collective-permute-start | bytes 589832 | tf_op jit(solution)/shard_map/ppermute | solution.py:586
  46.0 2.5 %collective-permute-start.13 = (f32[3,128,128]{2,1,0:T(8,128)S(1)}, f32[3,128,128]{2,1,0:T(8,128)S(1)}, u32[]{:S(2)}, u32[]{:S(2)}) collective-permute-start(f32[3,128,128]{2,1,0:T(8,128)S(1)} %collective-permute-done.12.refs_3_), channel_id=1, source_target_pairs={{0,4},{4,0},{1,5},{5,1},{2,6},{6,2},{3,7},{7,3},{8,12},{12,8},{9,1... | collective-permute-start | bytes 589832 | tf_op jit(solution)/shard_map/ppermute | solution.py:586
  47.1 1.4 %collective-permute-start.11 = (f32[3,128,128]{2,1,0:T(8,128)S(1)}, f32[3,128,128]{2,1,0:T(8,128)S(1)}, u32[]{:S(2)}, u32[]{:S(2)}) collective-permute-start(f32[3,128,128]{2,1,0:T(8,128)S(1)} %collective-permute-done.10.refs_2_), channel_id=1, source_target_pairs={{0,4},{4,0},{1,5},{5,1},{2,6},{6,2},{3,7},{7,3},{8,12},{12,8},{9,1... | collective-permute-start | bytes 589832 | tf_op jit(solution)/shard_map/ppermute | solution.py:586
  47.2 1.7 %collective-permute-start.9 = (f32[3,128,128]{2,1,0:T(8,128)S(1)}, f32[3,128,128]{2,1,0:T(8,128)S(1)}, u32[]{:S(2)}, u32[]{:S(2)}) collective-permute-start(f32[3,128,128]{2,1,0:T(8,128)S(1)} %collective-permute-done.8.refs_1_), channel_id=1, source_target_pairs={{0,4},{4,0},{1,5},{5,1},{2,6},{6,2},{3,7},{7,3},{8,12},{12,8},{9,1... | collective-permute-start | bytes 589832 | tf_op jit(solution)/shard_map/ppermute | solution.py:586
  49.4 1.8 %collective-permute-start.18 = (f32[3,2,128,128]{3,2,1,0:T(8,128)S(1)}, f32[3,2,128,128]{3,2,1,0:T(8,128)S(1)}, u32[]{:S(2)}, u32[]{:S(2)}) collective-permute-start(f32[3,2,128,128]{3,2,1,0:T(8,128)S(1)} %get-tuple-element.61), channel_id=1, source_target_pairs={{0,4},{4,0},{1,5},{5,1},{2,6},{6,2},{3,7},{7,3},{8,12},{12,8},{9,1... | collective-permute-start | bytes 1179656 | tf_op jit(solution)/shard_map/ppermute | solution.py:597

commit v6 on v4

--- a/solution.py
+++ b/solution.py
@@ -17,7 +17,7 @@
 SQUARINGS = 6
 DONE = 1e-4
 STEPS_MAX = 60
-ROWS = 16
+ROWS = 32
 WORK = 1
 WORK2 = 2
 WORK3 = 0.1

time: 51.1 us -> 50.8 us (level)
    ppermute x3, waiting for transfers between devices: 8.98 us -> 8.4 us  [local(): lax.ppermute(packed, 'chip', [(i, i ^ offset) for i in range(chips)])]
  transfers between devices with their start and end apart: 19 -> 19, of which waited for: 8 -> 9; matrix products, arithmetic and copies ran while one was open for 0% -> 0% of each run, Pallas kernels for 16% -> 16%
where the time goes in v6:
time: 50.8 us; the launch traced here: 50.6 us
  waiting for transfers between devices  24.7 us (49%)
  starting transfers between devices  15.6 us (31%)
  Pallas kernels  9.4 us (19%)
  between operations  0.79 us (2%)
    pallas_call x10, Pallas kernels, call(): pl.pallas_call(functools.partial(body, axes), out_shape=out_shape, in_spe...  9.4 us
    ppermute x6, waiting for transfers between devices, moved(): return lax.ppermute(piece, 'chip', [(i, i ^ offset) for i in range(4)])  9.07 us
    ppermute x3, waiting for transfers between devices, local(): lax.ppermute(packed, 'chip', [(i, i ^ offset) for i in range(chips)])  8.4 us
    ppermute x6, starting transfers between devices, moved(): return lax.ppermute(piece, 'chip', [(i, i ^ offset) for i in range(4)])  6.24 us
    ppermute x1, waiting for transfers between devices, local(): arrived = lax.ppermute(message, 'space', route)  6.1 us
    ppermute x3, starting transfers between devices, local(): lax.ppermute(packed, 'chip', [(i, i ^ offset) for i in range(chips)])  3.55 us
    ppermute x1, starting transfers between devices, local(): received = lax.ppermute(message, 'space', route)  2.29 us
    ppermute x1, starting transfers between devices, local(): arrived = lax.ppermute(message, 'space', route)  1.29 us
  transfers between devices with their start and end apart: 19, of which 9 were waited for; matrix products, arithmetic and copies ran while one was open for 0% of the time, Pallas kernels for 16%

profile of v6, /device:TPU:0, one launch (start us, length us, event | category | flops | bytes accessed | tf_op | source)
XLA Modules:
  0.0 50.6 jit_solution(7574250614219699821)
XLA Ops:
  0.6 0.5 %collective-permute-start = (f32[2,3,2,128,128]{4,3,2,1,0:T(8,128)}, f32[2,3,2,128,128]{4,3,2,1,0:T(8,128)S(1)}, u32[]{:S(2)}, u32[]{:S(2)}) collective-permute-start(f32[2,3,2,128,128]{4,3,2,1,0:T(8,128)} %bitcast.7), channel_id=1, source_target_pairs={{0,4},{4,0},{1,5},{5,1},{2,6},{6,2},{3,7},{7,3},{8,12},{12,8},{9,1... | collective-permute-start | bytes 2359304 | tf_op jit(solution)/shard_map/ppermute | solution.py:477
  1.2 3.8 %shard_map.59 = (f32[128,256]{1,0:T(8,128)S(1)}, f32[128,256]{1,0:T(8,128)S(1)}, f32[128,256]{1,0:T(8,128)S(1)}, f32[128,256]{1,0:T(8,128)S(1)}, f32[128,256]{1,0:T(8,128)S(1)}, /*index=5*/f32[8,128]{1,0:T(8,128)S(1)}) custom-call(f32[1,2,128,128]{3,2,1,0:T(8,128)} %onsite_far.1, f32[1,2,128,128]{3,2,1,0:T(8,128)} %hopping_far.1, ...), custom_call_target="tpu_custom_call" | custom-call | flops 1342177280 | bytes 2097152 | tf_op jit(solution)/shard_map/pallas_call | solution.py:508
  5.1 2.3 %collective-permute-start.4 = (f32[128,256]{1,0:T(8,128)S(1)}, f32[128,256]{1,0:T(8,128)S(1)}, u32[]{:S(2)}, u32[]{:S(2)}) collective-permute-start(f32[128,256]{1,0:T(8,128)S(1)} %get-tuple-element.36.arguments_4_), channel_id=1, source_target_pairs={{0,1},{3,2},{4,5},{7,6},{8,9},{11,10},{12,13},{15,14},{16,17},{19,... | collective-permute-start | bytes 393224 | tf_op jit(solution)/shard_map/ppermute | solution.py:538
  7.6 1.9 %collective-permute-start.14 = (f32[3,2,128,128]{3,2,1,0:T(8,128)S(1)}, f32[3,2,128,128]{3,2,1,0:T(8,128)S(1)}, u32[]{:S(2)}, u32[]{:S(2)}) collective-permute-start(f32[3,2,128,128]{3,2,1,0:T(8,128)S(1)} %get-tuple-element.64.refs_4_.refs_5_.refs_0_), channel_id=1, source_target_pairs={{0,8},{8,0},{16,24},{24,16},{1,9},{9,1},{17,25},{25,17},{2,10},{10... | collective-permute-start | bytes 1179656 | tf_op jit(solution)/shard_map/ppermute | solution.py:481
  9.5 1.5 %collective-permute-start.15 = (f32[3,2,128,128]{3,2,1,0:T(8,128)S(1)}, f32[3,2,128,128]{3,2,1,0:T(8,128)S(1)}, u32[]{:S(2)}, u32[]{:S(2)}) collective-permute-start(f32[3,2,128,128]{3,2,1,0:T(8,128)S(1)} %get-tuple-element.65.refs_5_.refs_6_.refs_1_), channel_id=1, source_target_pairs={{0,16},{8,24},{16,0},{24,8},{1,17},{9,25},{17,1},{25,9},{2,18},{10... | collective-permute-start | bytes 1179656 | tf_op jit(solution)/shard_map/ppermute | solution.py:481
  11.0 0.5 %collective-permute-start.3 = (f32[3,2,128,128]{3,2,1,0:T(8,128)S(1)}, f32[3,2,128,128]{3,2,1,0:T(8,128)S(1)}, u32[]{:S(2)}, u32[]{:S(2)}) collective-permute-start(f32[3,2,128,128]{3,2,1,0:T(8,128)S(1)} %get-tuple-element.64.refs_4_.refs_5_.refs_0_), channel_id=1, source_target_pairs={{0,16},{8,24},{16,0},{24,8},{1,17},{9,25},{17,1},{25,9},{2,18},{10... | collective-permute-start | bytes 1179656 | tf_op jit(solution)/shard_map/ppermute | solution.py:481
  11.8 0.7 %collective-permute-start.5 = (f32[128,256]{1,0:T(8,128)S(1)}, f32[128,256]{1,0:T(8,128)S(1)}, u32[]{:S(2)}, u32[]{:S(2)}) collective-permute-start(f32[128,256]{1,0:T(8,128)S(1)} %get-tuple-element.41), channel_id=1, source_target_pairs={{1,2},{2,1},{5,6},{6,5},{9,10},{10,9},{13,14},{14,13},{17,18},{18,... | collective-permute-start | bytes 393224 | tf_op jit(solution)/shard_map/ppermute | solution.py:547
  12.4 7.1 %collective-permute-done.14.refs_6_.refs_7_.refs_2_ = f32[3,2,128,128]{3,2,1,0:T(8,128)S(1)} collective-permute-done((f32[3,2,128,128]{3,2,1,0:T(8,128)S(1)}, f32[3,2,128,128]{3,2,1,0:T(8,128)S(1)}, u32[]{:S(2)}, u32[]{:S(2)}) %collective-permute-start.14) | collective-permute-done | bytes 393248 | tf_op jit(solution)/shard_map/ppermute | solution.py:481
  19.6 1.9 %collective-permute-done.15.refs_9_.refs_10_.refs_5_ = f32[3,2,128,128]{3,2,1,0:T(8,128)S(1)} collective-permute-done((f32[3,2,128,128]{3,2,1,0:T(8,128)S(1)}, f32[3,2,128,128]{3,2,1,0:T(8,128)S(1)}, u32[]{:S(2)}, u32[]{:S(2)}) %collective-permute-start.15) | collective-permute-done | bytes 393248 | tf_op jit(solution)/shard_map/ppermute | solution.py:481
  21.5 1.5 %collective-permute-start.16 = (f32[3,2,128,128]{3,2,1,0:T(8,128)S(1)}, f32[3,2,128,128]{3,2,1,0:T(8,128)S(1)}, u32[]{:S(2)}, u32[]{:S(2)}) collective-permute-start(f32[3,2,128,128]{3,2,1,0:T(8,128)S(1)} %collective-permute-done.14.refs_6_.refs_7_.refs_2_), channel_id=1, source_target_pairs={{0,16},{8,24},{16,0},{24,8},{1,17},{9,25},{17,1},{25,9},{2,18},{10... | collective-permute-start | bytes 1179656 | tf_op jit(solution)/shard_map/ppermute | solution.py:481
  23.1 1.3 %collective-permute-start.6 = (f32[128,256]{1,0:T(8,128)S(1)}, f32[128,256]{1,0:T(8,128)S(1)}, u32[]{:S(2)}, u32[]{:S(2)}) collective-permute-start(f32[128,256]{1,0:T(8,128)S(1)} %get-tuple-element.44), channel_id=1, source_target_pairs={{1,0},{2,3},{5,4},{6,7},{9,8},{10,11},{13,12},{14,15},{17,16},{18,... | collective-permute-start | bytes 393224 | tf_op jit(solution)/shard_map/ppermute | solution.py:555
  24.4 0.6 %shard_map.62 = (f32[128,256]{1,0:T(8,128)S(1)}, f32[128,256]{1,0:T(8,128)S(1)}, f32[4,128,256]{2,1,0:T(8,128)S(1)}) custom-call(f32[128,256]{1,0:T(8,128)S(1)} %collective-permute-done.5.received, f32[128,256]{1,0:T(8,128)S(1)} %get-tuple-element.45.diagonal.arguments_4_, f32[128,256]{1,0:T(8,128)S(1)} %get-tuple-element.46.u_in, ...), custom_call_target="tpu_custom_call" | custom-call | flops 134217728 | bytes 2097152 | tf_op jit(solution)/shard_map/pallas_call | solution.py:508
  24.9 0.6 %collective-permute-start.17 = (f32[3,2,128,128]{3,2,1,0:T(8,128)S(1)}, f32[3,2,128,128]{3,2,1,0:T(8,128)S(1)}, u32[]{:S(2)}, u32[]{:S(2)}) collective-permute-start(f32[3,2,128,128]{3,2,1,0:T(8,128)S(1)} %collective-permute-done.15.refs_9_.refs_10_.refs_5_), channel_id=1, source_target_pairs={{0,8},{8,0},{16,24},{24,16},{1,9},{9,1},{17,25},{25,17},{2,10},{10... | collective-permute-start | bytes 1179656 | tf_op jit(solution)/shard_map/ppermute | solution.py:481
  25.5 6.1 %collective-permute-done.6.arguments_2_ = f32[128,256]{1,0:T(8,128)S(1)} collective-permute-done((f32[128,256]{1,0:T(8,128)S(1)}, f32[128,256]{1,0:T(8,128)S(1)}, u32[]{:S(2)}, u32[]{:S(2)}) %collective-permute-start.6) | collective-permute-done | bytes 131104 | tf_op jit(solution)/shard_map/ppermute | solution.py:555
  31.6 1.2 %shard_map.63 = (f32[3,128,128]{2,1,0:T(8,128)S(1)}, f32[128,256]{1,0:T(8,128)S(1)}, f32[128,256]{1,0:T(8,128)S(1)}, f32[128,256]{1,0:T(8,128)S(1)}) custom-call(f32[3,2,128,128]{3,2,1,0:T(8,128)S(1)} %collective-permute-done.2.arguments_0_.refs_7_.refs_8_.refs_3_, f32[3,2,128,128]{3,2,1,0:T(8,128)S(1)} %collective-permute-done.3.arguments_1_.refs_8_.refs_9_.refs_4_, ...), custom_call_target="tpu_custom_call" | custom-call | flops 134217728 | bytes 2097152 | tf_op jit(solution)/shard_map/pallas_call | solution.py:508
  32.8 2.5 %collective-permute-start.12 = (f32[3,128,128]{2,1,0:T(8,128)S(1)}, f32[3,128,128]{2,1,0:T(8,128)S(1)}, u32[]{:S(2)}, u32[]{:S(2)}) collective-permute-start(f32[3,128,128]{2,1,0:T(8,128)S(1)} %get-tuple-element.57.refs_0_), channel_id=1, source_target_pairs={{0,24},{8,16},{16,8},{24,0},{1,25},{9,17},{17,9},{25,1},{2,26},{10... | collective-permute-start | bytes 589832 | tf_op jit(solution)/shard_map/ppermute | solution.py:582
  35.9 0.5 %collective-permute-start.8 = (f32[3,128,128]{2,1,0:T(8,128)S(1)}, f32[3,128,128]{2,1,0:T(8,128)S(1)}, u32[]{:S(2)}, u32[]{:S(2)}) collective-permute-start(f32[3,128,128]{2,1,0:T(8,128)S(1)} %get-tuple-element.57.refs_0_), channel_id=1, source_target_pairs={{0,8},{8,0},{16,24},{24,16},{1,9},{9,1},{17,25},{25,17},{2,10},{10... | collective-permute-start | bytes 589832 | tf_op jit(solution)/shard_map/ppermute | solution.py:582
  36.4 0.8 %shard_map.64 = f32[3,2,128,128]{3,2,1,0:T(8,128)} custom-call(f32[128,256]{1,0:T(8,128)S(1)} %get-tuple-element.53.diagonal, f32[128,256]{1,0:T(8,128)S(1)} %get-tuple-element.54.upper, f32[128,256]{1,0:T(8,128)S(1)} %get-tuple-element.55.lower), custom_call_target="tpu_custom_call" | custom-call | flops 1342177280 | bytes 2097152 | tf_op jit(solution)/shard_map/pallas_call | solution.py:508
  37.2 4.9 %collective-permute-done.12.refs_3_ = f32[3,128,128]{2,1,0:T(8,128)S(1)} collective-permute-done((f32[3,128,128]{2,1,0:T(8,128)S(1)}, f32[3,128,128]{2,1,0:T(8,128)S(1)}, u32[]{:S(2)}, u32[]{:S(2)}) %collective-permute-start.12) | collective-permute-done | bytes 196640 | tf_op jit(solution)/shard_map/ppermute | solution.py:582
  42.0 3.5 %collective-permute-done.10.refs_2_ = f32[3,128,128]{2,1,0:T(8,128)S(1)} collective-permute-done((f32[3,128,128]{2,1,0:T(8,128)S(1)}, f32[3,128,128]{2,1,0:T(8,128)S(1)}, u32[]{:S(2)}, u32[]{:S(2)}) %collective-permute-start.10) | collective-permute-done | bytes 196640 | tf_op jit(solution)/shard_map/ppermute | solution.py:582
  45.6 0.5 %collective-permute-start.11 = (f32[3,128,128]{2,1,0:T(8,128)S(1)}, f32[3,128,128]{2,1,0:T(8,128)S(1)}, u32[]{:S(2)}, u32[]{:S(2)}) collective-permute-start(f32[3,128,128]{2,1,0:T(8,128)S(1)} %collective-permute-done.10.refs_2_), channel_id=1, source_target_pairs={{0,4},{4,0},{1,5},{5,1},{2,6},{6,2},{3,7},{7,3},{8,12},{12,8},{9,1... | collective-permute-start | bytes 589832 | tf_op jit(solution)/shard_map/ppermute | solution.py:585
  46.2 0.7 %shard_map.65 = (f32[3,2,128,128]{3,2,1,0:T(8,128)S(1)}, f32[3,2,128,128]{3,2,1,0:T(8,128)S(1)}) custom-call(f32[3,128,128]{2,1,0:T(8,128)S(1)} %get-tuple-element.57.refs_0_, f32[3,128,128]{2,1,0:T(8,128)S(1)} %collective-permute-done.8.refs_1_, f32[3,128,128]{2,1,0:T(8,128)S(1)} %collective-permute-done.10.refs_2_, ...), custom_call_target="tpu_custom_call" | custom-call | flops 13421772 | bytes 2097152 | tf_op jit(solution)/shard_map/pallas_call | solution.py:508
  48.3 1.1 %shard_map.67._ = f32[2,3,2,128,128]{4,3,2,1,0:T(8,128)} custom-call(f32[5,3,2,128,128]{4,3,2,1,0:T(8,128)S(1)} %get-tuple-element.62.spectral, f32[3,2,128,128]{3,2,1,0:T(8,128)S(1)} %get-tuple-element.63.before, f32[3,2,128,128]{3,2,1,0:T(8,128)S(1)} %get-tuple-element.64.refs_4_.refs_5_.refs_0_, ...), custom_call_target="tpu_custom_call" | custom-call | flops 1342177280 | bytes 2097152 | tf_op jit(solution)/shard_map/pallas_call | solution.py:508
  49.8 0.8 %shard_map.68 = f32[2,3,2,128,128]{4,3,2,1,0:T(8,128)} custom-call(f32[3,2,128,128]{3,2,1,0:T(8,128)S(1)} %collective-permute-done.18.received, f32[2,3,2,128,128]{4,3,2,1,0:T(8,128)} %shard_map.67._), custom_call_target="tpu_custom_call", output_to_operand_aliasing={{}: (1, {})} | custom-call | flops 1342177280 | bytes 2097152 | tf_op jit(solution)/shard_map/pallas_call | solution.py:508
  (28 shorter events, 3.0 us)
Async XLA Ops:
  0.6 6.8 %copy-start = (f32[1,1,2,3,2,128,128]{6,5,4,3,2,1,0:T(8,128)S(1)}, f32[1,1,2,3,2,128,128]{6,5,4,3,2,1,0:T(8,128)}, u32[]{:S(2)}) copy-start(f32[1,1,2,3,2,128,128]{6,5,4,3,2,1,0:T(8,128)} %param.7) | copy-start | bytes 2359300
  0.6 6.8 %collective-permute-start = (f32[2,3,2,128,128]{4,3,2,1,0:T(8,128)}, f32[2,3,2,128,128]{4,3,2,1,0:T(8,128)S(1)}, u32[]{:S(2)}, u32[]{:S(2)}) collective-permute-start(f32[2,3,2,128,128]{4,3,2,1,0:T(8,128)} %bitcast.7), channel_id=1, source_target_pairs={{0,4},{4,0},{1,5},{5,1},{2,6},{6,2},{3,7},{7,3},{8,12},{12,8},{9,1... | collective-permute-start | bytes 2359304 | tf_op jit(solution)/shard_map/ppermute | solution.py:477
  5.0 2.5 %collective-permute-start.1 = (f32[8,128]{1,0:T(8,128)S(1)}, f32[8,128]{1,0:T(8,128)S(1)}, u32[]{:S(2)}, u32[]{:S(2)}) collective-permute-start(f32[8,128]{1,0:T(8,128)S(1)} %get-tuple-element.33), channel_id=1, source_target_pairs={{0,4},{4,0},{1,5},{5,1},{2,6},{6,2},{3,7},{7,3},{8,12},{12,8},{9,1... | collective-permute-start | bytes 12296 | tf_op jit(solution)/shard_map/ppermute | solution.py:533
  5.1 6.5 %collective-permute-start.4 = (f32[128,256]{1,0:T(8,128)S(1)}, f32[128,256]{1,0:T(8,128)S(1)}, u32[]{:S(2)}, u32[]{:S(2)}) collective-permute-start(f32[128,256]{1,0:T(8,128)S(1)} %get-tuple-element.36.arguments_4_), channel_id=1, source_target_pairs={{0,1},{3,2},{4,5},{7,6},{8,9},{11,10},{12,13},{15,14},{16,17},{19,... | collective-permute-start | bytes 393224 | tf_op jit(solution)/shard_map/ppermute | solution.py:538
  7.6 12.0 %collective-permute-start.14 = (f32[3,2,128,128]{3,2,1,0:T(8,128)S(1)}, f32[3,2,128,128]{3,2,1,0:T(8,128)S(1)}, u32[]{:S(2)}, u32[]{:S(2)}) collective-permute-start(f32[3,2,128,128]{3,2,1,0:T(8,128)S(1)} %get-tuple-element.64.refs_4_.refs_5_.refs_0_), channel_id=1, source_target_pairs={{0,8},{8,0},{16,24},{24,16},{1,9},{9,1},{17,25},{25,17},{2,10},{10... | collective-permute-start | bytes 1179656 | tf_op jit(solution)/shard_map/ppermute | solution.py:481
  9.5 12.0 %collective-permute-start.15 = (f32[3,2,128,128]{3,2,1,0:T(8,128)S(1)}, f32[3,2,128,128]{3,2,1,0:T(8,128)S(1)}, u32[]{:S(2)}, u32[]{:S(2)}) collective-permute-start(f32[3,2,128,128]{3,2,1,0:T(8,128)S(1)} %get-tuple-element.65.refs_5_.refs_6_.refs_1_), channel_id=1, source_target_pairs={{0,16},{8,24},{16,0},{24,8},{1,17},{9,25},{17,1},{25,9},{2,18},{10... | collective-permute-start | bytes 1179656 | tf_op jit(solution)/shard_map/ppermute | solution.py:481
  11.0 20.6 %collective-permute-start.3 = (f32[3,2,128,128]{3,2,1,0:T(8,128)S(1)}, f32[3,2,128,128]{3,2,1,0:T(8,128)S(1)}, u32[]{:S(2)}, u32[]{:S(2)}) collective-permute-start(f32[3,2,128,128]{3,2,1,0:T(8,128)S(1)} %get-tuple-element.64.refs_4_.refs_5_.refs_0_), channel_id=1, source_target_pairs={{0,16},{8,24},{16,0},{24,8},{1,17},{9,25},{17,1},{25,9},{2,18},{10... | collective-permute-start | bytes 1179656 | tf_op jit(solution)/shard_map/ppermute | solution.py:481
  11.5 20.1 %collective-permute-start.2 = (f32[3,2,128,128]{3,2,1,0:T(8,128)S(1)}, f32[3,2,128,128]{3,2,1,0:T(8,128)S(1)}, u32[]{:S(2)}, u32[]{:S(2)}) collective-permute-start(f32[3,2,128,128]{3,2,1,0:T(8,128)S(1)} %get-tuple-element.65.refs_5_.refs_6_.refs_1_), channel_id=1, source_target_pairs={{0,8},{8,0},{16,24},{24,16},{1,9},{9,1},{17,25},{25,17},{2,10},{10... | collective-permute-start | bytes 1179656 | tf_op jit(solution)/shard_map/ppermute | solution.py:481
  11.8 11.3 %collective-permute-start.5 = (f32[128,256]{1,0:T(8,128)S(1)}, f32[128,256]{1,0:T(8,128)S(1)}, u32[]{:S(2)}, u32[]{:S(2)}) collective-permute-start(f32[128,256]{1,0:T(8,128)S(1)} %get-tuple-element.41), channel_id=1, source_target_pairs={{1,2},{2,1},{5,6},{6,5},{9,10},{10,9},{13,14},{14,13},{17,18},{18,... | collective-permute-start | bytes 393224 | tf_op jit(solution)/shard_map/ppermute | solution.py:547
  21.5 24.6 %collective-permute-start.16 = (f32[3,2,128,128]{3,2,1,0:T(8,128)S(1)}, f32[3,2,128,128]{3,2,1,0:T(8,128)S(1)}, u32[]{:S(2)}, u32[]{:S(2)}) collective-permute-start(f32[3,2,128,128]{3,2,1,0:T(8,128)S(1)} %collective-permute-done.14.refs_6_.refs_7_.refs_2_), channel_id=1, source_target_pairs={{0,16},{8,24},{16,0},{24,8},{1,17},{9,25},{17,1},{25,9},{2,18},{10... | collective-permute-start | bytes 1179656 | tf_op jit(solution)/shard_map/ppermute | solution.py:481
  23.1 8.6 %collective-permute-start.6 = (f32[128,256]{1,0:T(8,128)S(1)}, f32[128,256]{1,0:T(8,128)S(1)}, u32[]{:S(2)}, u32[]{:S(2)}) collective-permute-start(f32[128,256]{1,0:T(8,128)S(1)} %get-tuple-element.44), channel_id=1, source_target_pairs={{1,0},{2,3},{5,4},{6,7},{9,8},{10,11},{13,12},{14,15},{17,16},{18,... | collective-permute-start | bytes 393224 | tf_op jit(solution)/shard_map/ppermute | solution.py:555
  24.9 21.2 %collective-permute-start.17 = (f32[3,2,128,128]{3,2,1,0:T(8,128)S(1)}, f32[3,2,128,128]{3,2,1,0:T(8,128)S(1)}, u32[]{:S(2)}, u32[]{:S(2)}) collective-permute-start(f32[3,2,128,128]{3,2,1,0:T(8,128)S(1)} %collective-permute-done.15.refs_9_.refs_10_.refs_5_), channel_id=1, source_target_pairs={{0,8},{8,0},{16,24},{24,16},{1,9},{9,1},{17,25},{25,17},{2,10},{10... | collective-permute-start | bytes 1179656 | tf_op jit(solution)/shard_map/ppermute | solution.py:481
  32.8 9.2 %collective-permute-start.12 = (f32[3,128,128]{2,1,0:T(8,128)S(1)}, f32[3,128,128]{2,1,0:T(8,128)S(1)}, u32[]{:S(2)}, u32[]{:S(2)}) collective-permute-start(f32[3,128,128]{2,1,0:T(8,128)S(1)} %get-tuple-element.57.refs_0_), channel_id=1, source_target_pairs={{0,24},{8,16},{16,8},{24,0},{1,25},{9,17},{17,9},{25,1},{2,26},{10... | collective-permute-start | bytes 589832 | tf_op jit(solution)/shard_map/ppermute | solution.py:582
  35.4 10.2 %collective-permute-start.10 = (f32[3,128,128]{2,1,0:T(8,128)S(1)}, f32[3,128,128]{2,1,0:T(8,128)S(1)}, u32[]{:S(2)}, u32[]{:S(2)}) collective-permute-start(f32[3,128,128]{2,1,0:T(8,128)S(1)} %get-tuple-element.57.refs_0_), channel_id=1, source_target_pairs={{0,16},{8,24},{16,0},{24,8},{1,17},{9,25},{17,1},{25,9},{2,18},{10... | collective-permute-start | bytes 589832 | tf_op jit(solution)/shard_map/ppermute | solution.py:582
  35.9 9.7 %collective-permute-start.8 = (f32[3,128,128]{2,1,0:T(8,128)S(1)}, f32[3,128,128]{2,1,0:T(8,128)S(1)}, u32[]{:S(2)}, u32[]{:S(2)}) collective-permute-start(f32[3,128,128]{2,1,0:T(8,128)S(1)} %get-tuple-element.57.refs_0_), channel_id=1, source_target_pairs={{0,8},{8,0},{16,24},{24,16},{1,9},{9,1},{17,25},{25,17},{2,10},{10... | collective-permute-start | bytes 589832 | tf_op jit(solution)/shard_map/ppermute | solution.py:582
  42.0 4.9 %collective-permute-start.7 = (f32[3,128,128]{2,1,0:T(8,128)S(1)}, f32[3,128,128]{2,1,0:T(8,128)S(1)}, u32[]{:S(2)}, u32[]{:S(2)}) collective-permute-start(f32[3,128,128]{2,1,0:T(8,128)S(1)} %get-tuple-element.57.refs_0_), channel_id=1, source_target_pairs={{0,4},{4,0},{1,5},{5,1},{2,6},{6,2},{3,7},{7,3},{8,12},{12,8},{9,1... | collective-permute-start | bytes 589832 | tf_op jit(solution)/shard_map/ppermute | solution.py:585
  45.6 1.4 %collective-permute-start.13 = (f32[3,128,128]{2,1,0:T(8,128)S(1)}, f32[3,128,128]{2,1,0:T(8,128)S(1)}, u32[]{:S(2)}, u32[]{:S(2)}) collective-permute-start(f32[3,128,128]{2,1,0:T(8,128)S(1)} %collective-permute-done.12.refs_3_), channel_id=1, source_target_pairs={{0,4},{4,0},{1,5},{5,1},{2,6},{6,2},{3,7},{7,3},{8,12},{12,8},{9,1... | collective-permute-start | bytes 589832 | tf_op jit(solution)/shard_map/ppermute | solution.py:585
  45.6 1.7 %collective-permute-start.11 = (f32[3,128,128]{2,1,0:T(8,128)S(1)}, f32[3,128,128]{2,1,0:T(8,128)S(1)}, u32[]{:S(2)}, u32[]{:S(2)}) collective-permute-start(f32[3,128,128]{2,1,0:T(8,128)S(1)} %collective-permute-done.10.refs_2_), channel_id=1, source_target_pairs={{0,4},{4,0},{1,5},{5,1},{2,6},{6,2},{3,7},{7,3},{8,12},{12,8},{9,1... | collective-permute-start | bytes 589832 | tf_op jit(solution)/shard_map/ppermute | solution.py:585
  46.1 1.5 %collective-permute-start.9 = (f32[3,128,128]{2,1,0:T(8,128)S(1)}, f32[3,128,128]{2,1,0:T(8,128)S(1)}, u32[]{:S(2)}, u32[]{:S(2)}) collective-permute-start(f32[3,128,128]{2,1,0:T(8,128)S(1)} %collective-permute-done.8.refs_1_), channel_id=1, source_target_pairs={{0,4},{4,0},{1,5},{5,1},{2,6},{6,2},{3,7},{7,3},{8,12},{12,8},{9,1... | collective-permute-start | bytes 589832 | tf_op jit(solution)/shard_map/ppermute | solution.py:585
  48.0 1.8 %collective-permute-start.18 = (f32[3,2,128,128]{3,2,1,0:T(8,128)S(1)}, f32[3,2,128,128]{3,2,1,0:T(8,128)S(1)}, u32[]{:S(2)}, u32[]{:S(2)}) collective-permute-start(f32[3,2,128,128]{3,2,1,0:T(8,128)S(1)} %get-tuple-element.61), channel_id=1, source_target_pairs={{0,4},{4,0},{1,5},{5,1},{2,6},{6,2},{3,7},{7,3},{8,12},{12,8},{9,1... | collective-permute-start | bytes 1179656 | tf_op jit(solution)/shard_map/ppermute | solution.py:596

commit v7 on v6

--- a/solution.py
+++ b/solution.py
@@ -17,7 +17,7 @@
 SQUARINGS = 6
 DONE = 1e-4
 STEPS_MAX = 60
-ROWS = 32
+ROWS = 64
 WORK = 1
 WORK2 = 2
 WORK3 = 0.1

time: 50.8 us -> 51.1 us (level)
    ppermute x3, waiting for transfers between devices: 8.4 us -> 8.98 us  [local(): lax.ppermute(packed, 'chip', [(i, i ^ offset) for i in range(chips)])]
  transfers between devices with their start and end apart: 19 -> 19, of which waited for: 9 -> 8; matrix products, arithmetic and copies ran while one was open for 0% -> 0% of each run, Pallas kernels for 16% -> 16%
where the time goes in v7:
time: 51.1 us; the launch traced here: 51.2 us
  waiting for transfers between devices  25.1 us (49%)
  starting transfers between devices  15.7 us (31%)
  Pallas kernels  9.49 us (19%)
  between operations  0.79 us (2%)
    pallas_call x10, Pallas kernels, call(): pl.pallas_call(functools.partial(body, axes), out_shape=out_shape, in_spe...  9.49 us
    ppermute x6, waiting for transfers between devices, moved(): return lax.ppermute(piece, 'chip', [(i, i ^ offset) for i in range(4)])  9.16 us
    ppermute x3, waiting for transfers between devices, local(): lax.ppermute(packed, 'chip', [(i, i ^ offset) for i in range(chips)])  8.98 us
    ppermute x6, starting transfers between devices, moved(): return lax.ppermute(piece, 'chip', [(i, i ^ offset) for i in range(4)])  6.32 us
    ppermute x1, waiting for transfers between devices, local(): arrived = lax.ppermute(message, 'space', route)  5.93 us
    ppermute x3, starting transfers between devices, local(): lax.ppermute(packed, 'chip', [(i, i ^ offset) for i in range(chips)])  3.55 us
    ppermute x1, starting transfers between devices, local(): received = lax.ppermute(message, 'space', route)  2.29 us
    ppermute x1, starting transfers between devices, local(): arrived = lax.ppermute(message, 'space', route)  1.29 us
  transfers between devices with their start and end apart: 19, of which 8 were waited for; matrix products, arithmetic and copies ran while one was open for 0% of the time, Pallas kernels for 16%

profile of v7, /device:TPU:0, one launch (start us, length us, event | category | flops | bytes accessed | tf_op | source)
XLA Modules:
  0.0 51.2 jit_solution(5726704083425049822)
XLA Ops:
  0.6 0.5 %collective-permute-start = (f32[2,3,2,128,128]{4,3,2,1,0:T(8,128)}, f32[2,3,2,128,128]{4,3,2,1,0:T(8,128)S(1)}, u32[]{:S(2)}, u32[]{:S(2)}) collective-permute-start(f32[2,3,2,128,128]{4,3,2,1,0:T(8,128)} %bitcast.7), channel_id=1, source_target_pairs={{0,4},{4,0},{1,5},{5,1},{2,6},{6,2},{3,7},{7,3},{8,12},{12,8},{9,1... | collective-permute-start | bytes 2359304 | tf_op jit(solution)/shard_map/ppermute | solution.py:477
  1.2 3.8 %shard_map.59 = (f32[128,256]{1,0:T(8,128)S(1)}, f32[128,256]{1,0:T(8,128)S(1)}, f32[128,256]{1,0:T(8,128)S(1)}, f32[128,256]{1,0:T(8,128)S(1)}, f32[128,256]{1,0:T(8,128)S(1)}, /*index=5*/f32[8,128]{1,0:T(8,128)S(1)}) custom-call(f32[1,2,128,128]{3,2,1,0:T(8,128)} %onsite_far.1, f32[1,2,128,128]{3,2,1,0:T(8,128)} %hopping_far.1, ...), custom_call_target="tpu_custom_call" | custom-call | flops 1342177280 | bytes 2097152 | tf_op jit(solution)/shard_map/pallas_call | solution.py:508
  5.1 2.3 %collective-permute-start.4 = (f32[128,256]{1,0:T(8,128)S(1)}, f32[128,256]{1,0:T(8,128)S(1)}, u32[]{:S(2)}, u32[]{:S(2)}) collective-permute-start(f32[128,256]{1,0:T(8,128)S(1)} %get-tuple-element.36.arguments_4_), channel_id=1, source_target_pairs={{0,1},{3,2},{4,5},{7,6},{8,9},{11,10},{12,13},{15,14},{16,17},{19,... | collective-permute-start | bytes 393224 | tf_op jit(solution)/shard_map/ppermute | solution.py:538
  7.6 2.6 %collective-permute-start.14 = (f32[3,2,128,128]{3,2,1,0:T(8,128)S(1)}, f32[3,2,128,128]{3,2,1,0:T(8,128)S(1)}, u32[]{:S(2)}, u32[]{:S(2)}) collective-permute-start(f32[3,2,128,128]{3,2,1,0:T(8,128)S(1)} %get-tuple-element.64.refs_4_.refs_5_.refs_0_), channel_id=1, source_target_pairs={{0,8},{8,0},{16,24},{24,16},{1,9},{9,1},{17,25},{25,17},{2,10},{10... | collective-permute-start | bytes 1179656 | tf_op jit(solution)/shard_map/ppermute | solution.py:481
  10.1 0.9 %collective-permute-start.15 = (f32[3,2,128,128]{3,2,1,0:T(8,128)S(1)}, f32[3,2,128,128]{3,2,1,0:T(8,128)S(1)}, u32[]{:S(2)}, u32[]{:S(2)}) collective-permute-start(f32[3,2,128,128]{3,2,1,0:T(8,128)S(1)} %get-tuple-element.65.refs_5_.refs_6_.refs_1_), channel_id=1, source_target_pairs={{0,16},{8,24},{16,0},{24,8},{1,17},{9,25},{17,1},{25,9},{2,18},{10... | collective-permute-start | bytes 1179656 | tf_op jit(solution)/shard_map/ppermute | solution.py:481
  11.0 1.1 %collective-permute-start.3 = (f32[3,2,128,128]{3,2,1,0:T(8,128)S(1)}, f32[3,2,128,128]{3,2,1,0:T(8,128)S(1)}, u32[]{:S(2)}, u32[]{:S(2)}) collective-permute-start(f32[3,2,128,128]{3,2,1,0:T(8,128)S(1)} %get-tuple-element.64.refs_4_.refs_5_.refs_0_), channel_id=1, source_target_pairs={{0,16},{8,24},{16,0},{24,8},{1,17},{9,25},{17,1},{25,9},{2,18},{10... | collective-permute-start | bytes 1179656 | tf_op jit(solution)/shard_map/ppermute | solution.py:481
  12.3 0.7 %collective-permute-start.5 = (f32[128,256]{1,0:T(8,128)S(1)}, f32[128,256]{1,0:T(8,128)S(1)}, u32[]{:S(2)}, u32[]{:S(2)}) collective-permute-start(f32[128,256]{1,0:T(8,128)S(1)} %get-tuple-element.41), channel_id=1, source_target_pairs={{1,2},{2,1},{5,6},{6,5},{9,10},{10,9},{13,14},{14,13},{17,18},{18,... | collective-permute-start | bytes 393224 | tf_op jit(solution)/shard_map/ppermute | solution.py:547
  13.0 7.0 %collective-permute-done.14.refs_6_.refs_7_.refs_2_ = f32[3,2,128,128]{3,2,1,0:T(8,128)S(1)} collective-permute-done((f32[3,2,128,128]{3,2,1,0:T(8,128)S(1)}, f32[3,2,128,128]{3,2,1,0:T(8,128)S(1)}, u32[]{:S(2)}, u32[]{:S(2)}) %collective-permute-start.14) | collective-permute-done | bytes 393248 | tf_op jit(solution)/shard_map/ppermute | solution.py:481
  20.0 2.1 %collective-permute-done.15.refs_9_.refs_10_.refs_5_ = f32[3,2,128,128]{3,2,1,0:T(8,128)S(1)} collective-permute-done((f32[3,2,128,128]{3,2,1,0:T(8,128)S(1)}, f32[3,2,128,128]{3,2,1,0:T(8,128)S(1)}, u32[]{:S(2)}, u32[]{:S(2)}) %collective-permute-start.15) | collective-permute-done | bytes 393248 | tf_op jit(solution)/shard_map/ppermute | solution.py:481
  22.1 0.9 %collective-permute-start.16 = (f32[3,2,128,128]{3,2,1,0:T(8,128)S(1)}, f32[3,2,128,128]{3,2,1,0:T(8,128)S(1)}, u32[]{:S(2)}, u32[]{:S(2)}) collective-permute-start(f32[3,2,128,128]{3,2,1,0:T(8,128)S(1)} %collective-permute-done.14.refs_6_.refs_7_.refs_2_), channel_id=1, source_target_pairs={{0,16},{8,24},{16,0},{24,8},{1,17},{9,25},{17,1},{25,9},{2,18},{10... | collective-permute-start | bytes 1179656 | tf_op jit(solution)/shard_map/ppermute | solution.py:481
  23.1 1.3 %collective-permute-start.6 = (f32[128,256]{1,0:T(8,128)S(1)}, f32[128,256]{1,0:T(8,128)S(1)}, u32[]{:S(2)}, u32[]{:S(2)}) collective-permute-start(f32[128,256]{1,0:T(8,128)S(1)} %get-tuple-element.44), channel_id=1, source_target_pairs={{1,0},{2,3},{5,4},{6,7},{9,8},{10,11},{13,12},{14,15},{17,16},{18,... | collective-permute-start | bytes 393224 | tf_op jit(solution)/shard_map/ppermute | solution.py:555
  24.4 0.6 %shard_map.62 = (f32[128,256]{1,0:T(8,128)S(1)}, f32[128,256]{1,0:T(8,128)S(1)}, f32[4,128,256]{2,1,0:T(8,128)S(1)}) custom-call(f32[128,256]{1,0:T(8,128)S(1)} %collective-permute-done.5.received, f32[128,256]{1,0:T(8,128)S(1)} %get-tuple-element.45.diagonal.arguments_4_, f32[128,256]{1,0:T(8,128)S(1)} %get-tuple-element.46.u_in, ...), custom_call_target="tpu_custom_call" | custom-call | flops 134217728 | bytes 2097152 | tf_op jit(solution)/shard_map/pallas_call | solution.py:508
  24.9 0.8 %collective-permute-start.17 = (f32[3,2,128,128]{3,2,1,0:T(8,128)S(1)}, f32[3,2,128,128]{3,2,1,0:T(8,128)S(1)}, u32[]{:S(2)}, u32[]{:S(2)}) collective-permute-start(f32[3,2,128,128]{3,2,1,0:T(8,128)S(1)} %collective-permute-done.15.refs_9_.refs_10_.refs_5_), channel_id=1, source_target_pairs={{0,8},{8,0},{16,24},{24,16},{1,9},{9,1},{17,25},{25,17},{2,10},{10... | collective-permute-start | bytes 1179656 | tf_op jit(solution)/shard_map/ppermute | solution.py:481
  25.7 5.9 %collective-permute-done.6.arguments_2_ = f32[128,256]{1,0:T(8,128)S(1)} collective-permute-done((f32[128,256]{1,0:T(8,128)S(1)}, f32[128,256]{1,0:T(8,128)S(1)}, u32[]{:S(2)}, u32[]{:S(2)}) %collective-permute-start.6) | collective-permute-done | bytes 131104 | tf_op jit(solution)/shard_map/ppermute | solution.py:555
  31.6 1.2 %shard_map.63 = (f32[3,128,128]{2,1,0:T(8,128)S(1)}, f32[128,256]{1,0:T(8,128)S(1)}, f32[128,256]{1,0:T(8,128)S(1)}, f32[128,256]{1,0:T(8,128)S(1)}) custom-call(f32[3,2,128,128]{3,2,1,0:T(8,128)S(1)} %collective-permute-done.2.arguments_0_.refs_7_.refs_8_.refs_3_, f32[3,2,128,128]{3,2,1,0:T(8,128)S(1)} %collective-permute-done.3.arguments_1_.refs_8_.refs_9_.refs_4_, ...), custom_call_target="tpu_custom_call" | custom-call | flops 134217728 | bytes 2097152 | tf_op jit(solution)/shard_map/pallas_call | solution.py:508
  32.8 2.5 %collective-permute-start.12 = (f32[3,128,128]{2,1,0:T(8,128)S(1)}, f32[3,128,128]{2,1,0:T(8,128)S(1)}, u32[]{:S(2)}, u32[]{:S(2)}) collective-permute-start(f32[3,128,128]{2,1,0:T(8,128)S(1)} %get-tuple-element.57.refs_0_), channel_id=1, source_target_pairs={{0,24},{8,16},{16,8},{24,0},{1,25},{9,17},{17,9},{25,1},{2,26},{10... | collective-permute-start | bytes 589832 | tf_op jit(solution)/shard_map/ppermute | solution.py:582
  35.9 0.5 %collective-permute-start.8 = (f32[3,128,128]{2,1,0:T(8,128)S(1)}, f32[3,128,128]{2,1,0:T(8,128)S(1)}, u32[]{:S(2)}, u32[]{:S(2)}) collective-permute-start(f32[3,128,128]{2,1,0:T(8,128)S(1)} %get-tuple-element.57.refs_0_), channel_id=1, source_target_pairs={{0,8},{8,0},{16,24},{24,16},{1,9},{9,1},{17,25},{25,17},{2,10},{10... | collective-permute-start | bytes 589832 | tf_op jit(solution)/shard_map/ppermute | solution.py:582
  36.4 0.8 %shard_map.64 = f32[3,2,128,128]{3,2,1,0:T(8,128)} custom-call(f32[128,256]{1,0:T(8,128)S(1)} %get-tuple-element.53.diagonal, f32[128,256]{1,0:T(8,128)S(1)} %get-tuple-element.54.upper, f32[128,256]{1,0:T(8,128)S(1)} %get-tuple-element.55.lower), custom_call_target="tpu_custom_call" | custom-call | flops 1342177280 | bytes 2097152 | tf_op jit(solution)/shard_map/pallas_call | solution.py:508
  37.2 5.0 %collective-permute-done.12.refs_3_ = f32[3,128,128]{2,1,0:T(8,128)S(1)} collective-permute-done((f32[3,128,128]{2,1,0:T(8,128)S(1)}, f32[3,128,128]{2,1,0:T(8,128)S(1)}, u32[]{:S(2)}, u32[]{:S(2)}) %collective-permute-start.12) | collective-permute-done | bytes 196640 | tf_op jit(solution)/shard_map/ppermute | solution.py:582
  42.2 4.0 %collective-permute-done.10.refs_2_ = f32[3,128,128]{2,1,0:T(8,128)S(1)} collective-permute-done((f32[3,128,128]{2,1,0:T(8,128)S(1)}, f32[3,128,128]{2,1,0:T(8,128)S(1)}, u32[]{:S(2)}, u32[]{:S(2)}) %collective-permute-start.10) | collective-permute-done | bytes 196640 | tf_op jit(solution)/shard_map/ppermute | solution.py:582
  46.2 0.5 collective-permute-start.11
  46.8 0.8 %shard_map.65 = (f32[3,2,128,128]{3,2,1,0:T(8,128)S(1)}, f32[3,2,128,128]{3,2,1,0:T(8,128)S(1)}) custom-call(f32[3,128,128]{2,1,0:T(8,128)S(1)} %get-tuple-element.57.refs_0_, f32[3,128,128]{2,1,0:T(8,128)S(1)} %collective-permute-done.8.refs_1_, f32[3,128,128]{2,1,0:T(8,128)S(1)} %collective-permute-done.10.refs_2_, ...), custom_call_target="tpu_custom_call" | custom-call | flops 13421772 | bytes 2097152 | tf_op jit(solution)/shard_map/pallas_call | solution.py:508
  48.9 1.1 %shard_map.67._ = f32[2,3,2,128,128]{4,3,2,1,0:T(8,128)} custom-call(f32[5,3,2,128,128]{4,3,2,1,0:T(8,128)S(1)} %get-tuple-element.62.spectral, f32[3,2,128,128]{3,2,1,0:T(8,128)S(1)} %get-tuple-element.63.before, f32[3,2,128,128]{3,2,1,0:T(8,128)S(1)} %get-tuple-element.64.refs_4_.refs_5_.refs_0_, ...), custom_call_target="tpu_custom_call" | custom-call | flops 1342177280 | bytes 2097152 | tf_op jit(solution)/shard_map/pallas_call | solution.py:508
  50.4 0.8 %shard_map.68 = f32[2,3,2,128,128]{4,3,2,1,0:T(8,128)} custom-call(f32[3,2,128,128]{3,2,1,0:T(8,128)S(1)} %collective-permute-done.18.received, f32[2,3,2,128,128]{4,3,2,1,0:T(8,128)} %shard_map.67._), custom_call_target="tpu_custom_call", output_to_operand_aliasing={{}: (1, {})} | custom-call | flops 1342177280 | bytes 2097152 | tf_op jit(solution)/shard_map/pallas_call | solution.py:508
  (28 shorter events, 2.8 us)
Async XLA Ops:
  0.6 6.8 %copy-start = (f32[1,1,2,3,2,128,128]{6,5,4,3,2,1,0:T(8,128)S(1)}, f32[1,1,2,3,2,128,128]{6,5,4,3,2,1,0:T(8,128)}, u32[]{:S(2)}) copy-start(f32[1,1,2,3,2,128,128]{6,5,4,3,2,1,0:T(8,128)} %param.7) | copy-start | bytes 2359300
  0.6 6.8 %collective-permute-start = (f32[2,3,2,128,128]{4,3,2,1,0:T(8,128)}, f32[2,3,2,128,128]{4,3,2,1,0:T(8,128)S(1)}, u32[]{:S(2)}, u32[]{:S(2)}) collective-permute-start(f32[2,3,2,128,128]{4,3,2,1,0:T(8,128)} %bitcast.7), channel_id=1, source_target_pairs={{0,4},{4,0},{1,5},{5,1},{2,6},{6,2},{3,7},{7,3},{8,12},{12,8},{9,1... | collective-permute-start | bytes 2359304 | tf_op jit(solution)/shard_map/ppermute | solution.py:477
  5.0 2.5 %collective-permute-start.1 = (f32[8,128]{1,0:T(8,128)S(1)}, f32[8,128]{1,0:T(8,128)S(1)}, u32[]{:S(2)}, u32[]{:S(2)}) collective-permute-start(f32[8,128]{1,0:T(8,128)S(1)} %get-tuple-element.33), channel_id=1, source_target_pairs={{0,4},{4,0},{1,5},{5,1},{2,6},{6,2},{3,7},{7,3},{8,12},{12,8},{9,1... | collective-permute-start | bytes 12296 | tf_op jit(solution)/shard_map/ppermute | solution.py:533
  5.1 7.1 %collective-permute-start.4 = (f32[128,256]{1,0:T(8,128)S(1)}, f32[128,256]{1,0:T(8,128)S(1)}, u32[]{:S(2)}, u32[]{:S(2)}) collective-permute-start(f32[128,256]{1,0:T(8,128)S(1)} %get-tuple-element.36.arguments_4_), channel_id=1, source_target_pairs={{0,1},{3,2},{4,5},{7,6},{8,9},{11,10},{12,13},{15,14},{16,17},{19,... | collective-permute-start | bytes 393224 | tf_op jit(solution)/shard_map/ppermute | solution.py:538
  7.6 12.5 %collective-permute-start.14 = (f32[3,2,128,128]{3,2,1,0:T(8,128)S(1)}, f32[3,2,128,128]{3,2,1,0:T(8,128)S(1)}, u32[]{:S(2)}, u32[]{:S(2)}) collective-permute-start(f32[3,2,128,128]{3,2,1,0:T(8,128)S(1)} %get-tuple-element.64.refs_4_.refs_5_.refs_0_), channel_id=1, source_target_pairs={{0,8},{8,0},{16,24},{24,16},{1,9},{9,1},{17,25},{25,17},{2,10},{10... | collective-permute-start | bytes 1179656 | tf_op jit(solution)/shard_map/ppermute | solution.py:481
  10.1 12.0 %collective-permute-start.15 = (f32[3,2,128,128]{3,2,1,0:T(8,128)S(1)}, f32[3,2,128,128]{3,2,1,0:T(8,128)S(1)}, u32[]{:S(2)}, u32[]{:S(2)}) collective-permute-start(f32[3,2,128,128]{3,2,1,0:T(8,128)S(1)} %get-tuple-element.65.refs_5_.refs_6_.refs_1_), channel_id=1, source_target_pairs={{0,16},{8,24},{16,0},{24,8},{1,17},{9,25},{17,1},{25,9},{2,18},{10... | collective-permute-start | bytes 1179656 | tf_op jit(solution)/shard_map/ppermute | solution.py:481
  11.0 20.6 %collective-permute-start.3 = (f32[3,2,128,128]{3,2,1,0:T(8,128)S(1)}, f32[3,2,128,128]{3,2,1,0:T(8,128)S(1)}, u32[]{:S(2)}, u32[]{:S(2)}) collective-permute-start(f32[3,2,128,128]{3,2,1,0:T(8,128)S(1)} %get-tuple-element.64.refs_4_.refs_5_.refs_0_), channel_id=1, source_target_pairs={{0,16},{8,24},{16,0},{24,8},{1,17},{9,25},{17,1},{25,9},{2,18},{10... | collective-permute-start | bytes 1179656 | tf_op jit(solution)/shard_map/ppermute | solution.py:481
  12.2 19.5 %collective-permute-start.2 = (f32[3,2,128,128]{3,2,1,0:T(8,128)S(1)}, f32[3,2,128,128]{3,2,1,0:T(8,128)S(1)}, u32[]{:S(2)}, u32[]{:S(2)}) collective-permute-start(f32[3,2,128,128]{3,2,1,0:T(8,128)S(1)} %get-tuple-element.65.refs_5_.refs_6_.refs_1_), channel_id=1, source_target_pairs={{0,8},{8,0},{16,24},{24,16},{1,9},{9,1},{17,25},{25,17},{2,10},{10... | collective-permute-start | bytes 1179656 | tf_op jit(solution)/shard_map/ppermute | solution.py:481
  12.3 10.7 %collective-permute-start.5 = (f32[128,256]{1,0:T(8,128)S(1)}, f32[128,256]{1,0:T(8,128)S(1)}, u32[]{:S(2)}, u32[]{:S(2)}) collective-permute-start(f32[128,256]{1,0:T(8,128)S(1)} %get-tuple-element.41), channel_id=1, source_target_pairs={{1,2},{2,1},{5,6},{6,5},{9,10},{10,9},{13,14},{14,13},{17,18},{18,... | collective-permute-start | bytes 393224 | tf_op jit(solution)/shard_map/ppermute | solution.py:547
  22.1 24.5 %collective-permute-start.16 = (f32[3,2,128,128]{3,2,1,0:T(8,128)S(1)}, f32[3,2,128,128]{3,2,1,0:T(8,128)S(1)}, u32[]{:S(2)}, u32[]{:S(2)}) collective-permute-start(f32[3,2,128,128]{3,2,1,0:T(8,128)S(1)} %collective-permute-done.14.refs_6_.refs_7_.refs_2_), channel_id=1, source_target_pairs={{0,16},{8,24},{16,0},{24,8},{1,17},{9,25},{17,1},{25,9},{2,18},{10... | collective-permute-start | bytes 1179656 | tf_op jit(solution)/shard_map/ppermute | solution.py:481
  23.1 8.6 %collective-permute-start.6 = (f32[128,256]{1,0:T(8,128)S(1)}, f32[128,256]{1,0:T(8,128)S(1)}, u32[]{:S(2)}, u32[]{:S(2)}) collective-permute-start(f32[128,256]{1,0:T(8,128)S(1)} %get-tuple-element.44), channel_id=1, source_target_pairs={{1,0},{2,3},{5,4},{6,7},{9,8},{10,11},{13,12},{14,15},{17,16},{18,... | collective-permute-start | bytes 393224 | tf_op jit(solution)/shard_map/ppermute | solution.py:555
  24.9 21.8 %collective-permute-start.17 = (f32[3,2,128,128]{3,2,1,0:T(8,128)S(1)}, f32[3,2,128,128]{3,2,1,0:T(8,128)S(1)}, u32[]{:S(2)}, u32[]{:S(2)}) collective-permute-start(f32[3,2,128,128]{3,2,1,0:T(8,128)S(1)} %collective-permute-done.15.refs_9_.refs_10_.refs_5_), channel_id=1, source_target_pairs={{0,8},{8,0},{16,24},{24,16},{1,9},{9,1},{17,25},{25,17},{2,10},{10... | collective-permute-start | bytes 1179656 | tf_op jit(solution)/shard_map/ppermute | solution.py:481
  32.8 9.4 %collective-permute-start.12 = (f32[3,128,128]{2,1,0:T(8,128)S(1)}, f32[3,128,128]{2,1,0:T(8,128)S(1)}, u32[]{:S(2)}, u32[]{:S(2)}) collective-permute-start(f32[3,128,128]{2,1,0:T(8,128)S(1)} %get-tuple-element.57.refs_0_), channel_id=1, source_target_pairs={{0,24},{8,16},{16,8},{24,0},{1,25},{9,17},{17,9},{25,1},{2,26},{10... | collective-permute-start | bytes 589832 | tf_op jit(solution)/shard_map/ppermute | solution.py:582
  35.4 10.8 %collective-permute-start.10 = (f32[3,128,128]{2,1,0:T(8,128)S(1)}, f32[3,128,128]{2,1,0:T(8,128)S(1)}, u32[]{:S(2)}, u32[]{:S(2)}) collective-permute-start(f32[3,128,128]{2,1,0:T(8,128)S(1)} %get-tuple-element.57.refs_0_), channel_id=1, source_target_pairs={{0,16},{8,24},{16,0},{24,8},{1,17},{9,25},{17,1},{25,9},{2,18},{10... | collective-permute-start | bytes 589832 | tf_op jit(solution)/shard_map/ppermute | solution.py:582
  35.9 10.3 %collective-permute-start.8 = (f32[3,128,128]{2,1,0:T(8,128)S(1)}, f32[3,128,128]{2,1,0:T(8,128)S(1)}, u32[]{:S(2)}, u32[]{:S(2)}) collective-permute-start(f32[3,128,128]{2,1,0:T(8,128)S(1)} %get-tuple-element.57.refs_0_), channel_id=1, source_target_pairs={{0,8},{8,0},{16,24},{24,16},{1,9},{9,1},{17,25},{25,17},{2,10},{10... | collective-permute-start | bytes 589832 | tf_op jit(solution)/shard_map/ppermute | solution.py:582
  42.2 5.4 %collective-permute-start.7 = (f32[3,128,128]{2,1,0:T(8,128)S(1)}, f32[3,128,128]{2,1,0:T(8,128)S(1)}, u32[]{:S(2)}, u32[]{:S(2)}) collective-permute-start(f32[3,128,128]{2,1,0:T(8,128)S(1)} %get-tuple-element.57.refs_0_), channel_id=1, source_target_pairs={{0,4},{4,0},{1,5},{5,1},{2,6},{6,2},{3,7},{7,3},{8,12},{12,8},{9,1... | collective-permute-start | bytes 589832 | tf_op jit(solution)/shard_map/ppermute | solution.py:585
  46.2 1.4 %collective-permute-start.13 = (f32[3,128,128]{2,1,0:T(8,128)S(1)}, f32[3,128,128]{2,1,0:T(8,128)S(1)}, u32[]{:S(2)}, u32[]{:S(2)}) collective-permute-start(f32[3,128,128]{2,1,0:T(8,128)S(1)} %collective-permute-done.12.refs_3_), channel_id=1, source_target_pairs={{0,4},{4,0},{1,5},{5,1},{2,6},{6,2},{3,7},{7,3},{8,12},{12,8},{9,1... | collective-permute-start | bytes 589832 | tf_op jit(solution)/shard_map/ppermute | solution.py:585
  46.2 1.7 %collective-permute-start.11 = (f32[3,128,128]{2,1,0:T(8,128)S(1)}, f32[3,128,128]{2,1,0:T(8,128)S(1)}, u32[]{:S(2)}, u32[]{:S(2)}) collective-permute-start(f32[3,128,128]{2,1,0:T(8,128)S(1)} %collective-permute-done.10.refs_2_), channel_id=1, source_target_pairs={{0,4},{4,0},{1,5},{5,1},{2,6},{6,2},{3,7},{7,3},{8,12},{12,8},{9,1... | collective-permute-start | bytes 589832 | tf_op jit(solution)/shard_map/ppermute | solution.py:585
  46.7 1.5 %collective-permute-start.9 = (f32[3,128,128]{2,1,0:T(8,128)S(1)}, f32[3,128,128]{2,1,0:T(8,128)S(1)}, u32[]{:S(2)}, u32[]{:S(2)}) collective-permute-start(f32[3,128,128]{2,1,0:T(8,128)S(1)} %collective-permute-done.8.refs_1_), channel_id=1, source_target_pairs={{0,4},{4,0},{1,5},{5,1},{2,6},{6,2},{3,7},{7,3},{8,12},{12,8},{9,1... | collective-permute-start | bytes 589832 | tf_op jit(solution)/shard_map/ppermute | solution.py:585
  48.6 1.8 %collective-permute-start.18 = (f32[3,2,128,128]{3,2,1,0:T(8,128)S(1)}, f32[3,2,128,128]{3,2,1,0:T(8,128)S(1)}, u32[]{:S(2)}, u32[]{:S(2)}) collective-permute-start(f32[3,2,128,128]{3,2,1,0:T(8,128)S(1)} %get-tuple-element.61), channel_id=1, source_target_pairs={{0,4},{4,0},{1,5},{5,1},{2,6},{6,2},{3,7},{7,3},{8,12},{12,8},{9,1... | collective-permute-start | bytes 1179656 | tf_op jit(solution)/shard_map/ppermute | solution.py:596
